TPU v7x, 32 devices: a whole 2x2x4 slice. The times are simulated.
32 devices in a mesh: dp: 4 (over y, x), expert: 8 (over z, core).
Axes of the slice: x: 2, y: 2, z: 4, core: 2. Of those that a mesh axis runs over, the one named last changes fastest.
Arguments:
- hidden_in: bfloat16 [8, 1024, 1024], P('expert', 'dp')
- lengths: int32 [8], P('expert'), may hold values from 128 to 1024, as said below
- value_pick: int32 [8, 1024, 4, 2], P('expert', 'dp'), may hold values from 0 to 4, all different within a row
- output_pick: int32 [8, 1024, 4, 2], P('expert', 'dp'), may hold values from 0 to 4, all different within a row
- expert_pick: int32 [8, 1024, 16], P('expert', 'dp'), may hold values from 0 to 47, all different within a row; in each aligned block of 256 rows (0 to 255, 256 to 511, ..., all dimensions but the last counted through in order) at most 128 rows name the same one
- query_weight: bfloat16 [1024, 512], replicated, may hold values from -0.25 to 0.25
- key_weight: bfloat16 [1024, 512], replicated, may hold values from -0.25 to 0.25
- value_weight: bfloat16 [1024, 2560], replicated, may hold values from -0.1875 to 0.1875
- output_weight: bfloat16 [2560, 1024], replicated, may hold values from -2 to 2
- value_router: bfloat16 [1024, 20], replicated, may hold values from -0.125 to 0.125
- output_router: bfloat16 [1024, 20], replicated, may hold values from -0.125 to 0.125
- expert_router: bfloat16 [1024, 48], replicated
- attention_gain: bfloat16 [1024], replicated, may hold values from 0.5 to 1.5
- feedforward_gain: bfloat16 [1024], replicated, may hold values from 0.5 to 1.5
- expert_up: bfloat16 [48, 1024, 128], P('expert'), may hold values from -0.1875 to 0.1875
- expert_down: bfloat16 [48, 128, 1024], P('expert'), may hold values from -0.5 to 0.5
- cotangent: bfloat16 [8, 1024, 1024], P('expert', 'dp'), may hold values from -6 to 6
Outputs:
- block_out: bfloat16 [8, 1024, 1024], P('expert', 'dp')
- grad_input: float32 [8, 1024, 1024], P('expert', 'dp')
- grad_query_weight: float32 [1024, 512], P(('dp', 'expert'))
- grad_key_weight: float32 [1024, 512], P(('dp', 'expert'))
- grad_value_weight: float32 [1024, 2560], P(('dp', 'expert'))
- grad_output_weight: float32 [2560, 1024], P(None, ('dp', 'expert'))
- grad_value_router: float32 [1024, 20], P(('dp', 'expert'))
- grad_output_router: float32 [1024, 20], P(('dp', 'expert'))
- grad_expert_router: float32 [1024, 48], P(('dp', 'expert'))
- grad_attention_gain: float32 [1024], P(('dp', 'expert'))
- grad_feedforward_gain: float32 [1024], P(('dp', 'expert'))
- grad_expert_up: float32 [48, 1024, 128], P('expert', 'dp')
- grad_expert_down: float32 [48, 128, 1024], P('expert', None, 'dp')
- residual_norms: float32 [4], replicated
Inputs may be any that keep to these rules, and one draw needn't show every extreme that they name: `lengths`: in every draw one bucket holds a sequence of 1024 positions and another one of 128. `value_pick`: the experts that a token names for one head are different. `output_pick`: the experts that a token names for one head are different. `expert_pick`: each token names 16 different experts; among the 256 tokens of one device no expert is named more than 128 times, and in every draw some expert exactly 128 times; every expert is named somewhere.
All inputs are finite; a program needn't handle non-finite values.
Results may differ from a plain program's by a relative error of at most 0.018.
Values may be sent and summed in bfloat16 or wider, within the bound.
A program may use at most 192 MiB of HBM per device.

v0:
```python
import jax
import jax.numpy as jnp
from jax import lax
from jax.sharding import PartitionSpec as P

D = 1024
HEADS = 4
HEAD_DIM = 128
VE = 5
TOPK = 16


EPSILON = 1e-05
NEGATIVE = -1000000000.0
PRECISE = lax.Precision.HIGHEST


def low_dot(left_side, right_side):
    return jnp.dot(left_side, right_side, preferred_element_type=jnp.float32)


def exact_dot(left_side, right_side):
    return jnp.dot(left_side, right_side, precision=PRECISE)


def layer_norm(field, scale_gain):
    center = field - jnp.mean(field, axis=-1, keepdims=True)
    spread = jnp.mean(center * center, axis=-1, keepdims=True)
    return center * lax.rsqrt(spread + EPSILON) * scale_gain


def choose(select, count):
    return jnp.sum(
        (select[..., None] == jnp.arange(count, dtype=jnp.int32)).astype(jnp.float32), axis=-2
    )


def attention_probs(query_heads, key_heads, query_pos, length):
    key_pos = jnp.arange(key_heads.shape[0], dtype=jnp.int32)
    raw_scores = jnp.einsum(
        "qhd,khd->hqk", query_heads, key_heads, preferred_element_type=jnp.float32
    )
    allowed = (key_pos[None, :] <= query_pos[:, None]) & (key_pos[None, :] < length)
    scores = jnp.where(allowed[None], raw_scores * HEAD_DIM ** (-0.5), NEGATIVE)
    exp_terms = jnp.exp(scores - jnp.max(scores, axis=-1, keepdims=True))
    return exp_terms / jnp.sum(exp_terms, axis=-1, keepdims=True)


def shards(
    hidden_in,
    lengths,
    value_pick,
    output_pick,
    expert_pick,
    query_weight,
    key_weight,
    value_weight,
    output_weight,
    value_router,
    output_router,
    expert_router,
    attention_gain,
    feedforward_gain,
    expert_up,
    expert_down,
    cotangent,
):
    row_count = hidden_in.shape[1]
    total_experts = expert_router.shape[1]
    local_experts = expert_up.shape[0]
    groups = lax.axis_size("expert")
    capacity = (3 * row_count * TOPK + 2 * total_experts - 1) // (2 * total_experts)
    input_low = hidden_in[0]
    input_full = input_low.astype(jnp.float32)
    length = lengths[0]
    query_pos = lax.axis_index("dp") * row_count + jnp.arange(row_count, dtype=jnp.int32)
    live_mask = (query_pos < length).astype(jnp.float32)[:, None]
    gain_one = attention_gain.astype(jnp.float32)
    gain_two = feedforward_gain.astype(jnp.float32)
    normed_one = layer_norm(input_full, gain_one)
    normed_low = normed_one.astype(jnp.bfloat16)
    queries = low_dot(normed_low, query_weight).astype(jnp.bfloat16)
    key_local = low_dot(normed_low, key_weight).astype(jnp.bfloat16)
    value_sig = jax.nn.sigmoid(low_dot(normed_low, value_router)).reshape(row_count, HEADS, VE)
    value_hot = choose(value_pick[0], VE)
    value_gate = value_sig * value_hot
    value_all = low_dot(input_low, value_weight).reshape(row_count, HEADS, VE, HEAD_DIM)
    value_local = (
        jnp.sum(value_gate[..., None] * value_all, axis=2)
        .astype(jnp.bfloat16)
        .reshape(row_count, HEADS * HEAD_DIM)
    )
    key_all, value_rows = (
        lax.all_gather(key_local, "dp", axis=0, tiled=True),
        lax.all_gather(value_local, "dp", axis=0, tiled=True),
    )
    query_heads = queries.reshape(row_count, HEADS, HEAD_DIM)
    key_heads = key_all.reshape(-1, HEADS, HEAD_DIM)
    value_heads = value_rows.reshape(-1, HEADS, HEAD_DIM)
    soft_probs = attention_probs(query_heads, key_heads, query_pos, length)
    attended = jnp.einsum(
        "hqk,khd->qhd",
        soft_probs.astype(jnp.bfloat16),
        value_heads,
        preferred_element_type=jnp.float32,
    )
    output_sig = jax.nn.sigmoid(low_dot(normed_low, output_router)).reshape(row_count, HEADS, VE)
    output_hot = choose(output_pick[0], VE)
    output_gate = output_sig * output_hot
    mixed = (
        (output_gate[..., None] * attended[:, :, None, :])
        .astype(jnp.bfloat16)
        .reshape(row_count, HEADS * VE * HEAD_DIM)
    )
    attention_out = live_mask * low_dot(mixed, output_weight)
    middle = input_full + attention_out
    normed_two = layer_norm(middle, gain_two)
    normed_two_low = normed_two.astype(jnp.bfloat16)
    router_sig = jax.nn.sigmoid(low_dot(normed_two_low, expert_router))
    flat_pick = expert_pick[0].reshape(-1)
    pick_count = (flat_pick[:, None] == jnp.arange(total_experts, dtype=jnp.int32)).astype(
        jnp.int32
    )
    pick_hot = pick_count.reshape(row_count, TOPK, total_experts).astype(jnp.float32)
    pair_sig = jnp.einsum("tke,te->tk", pick_hot, router_sig, precision=PRECISE)
    expert_gate = pair_sig * live_mask
    running_count = jnp.cumsum(pick_count, axis=0, dtype=jnp.int32)
    slot_rank = jnp.sum((running_count - pick_count) * pick_count, axis=1, dtype=jnp.int32)
    slot_index = flat_pick * capacity + slot_rank
    token_of = jnp.arange(row_count * TOPK, dtype=jnp.int32) // TOPK
    middle_low = middle.astype(jnp.bfloat16)
    dispatch = (
        jnp.zeros((total_experts * capacity, D), jnp.bfloat16)
        .at[slot_index]
        .set(middle_low[token_of])
    )
    outgoing = dispatch.reshape(groups, local_experts, capacity, D)
    received = lax.all_to_all(outgoing, "expert", split_axis=0, concat_axis=0, tiled=True)
    preact = jnp.einsum("sxcd,xdf->sxcf", received, expert_up, preferred_element_type=jnp.float32)
    hidden_rows = jax.nn.silu(preact).astype(jnp.bfloat16)
    result = jnp.einsum(
        "sxcf,xfd->sxcd", hidden_rows, expert_down, preferred_element_type=jnp.float32
    ).astype(jnp.bfloat16)
    result, hidden, received, preact = (result, hidden_rows, received, preact)
    returned = lax.all_to_all(result, "expert", split_axis=0, concat_axis=0, tiled=True)
    picked = (
        returned.reshape(total_experts * capacity, D)[slot_index]
        .reshape(row_count, TOPK, D)
        .astype(jnp.float32)
    )
    feedforward_out = jnp.sum(expert_gate[..., None] * picked, axis=1)
    final_rows = middle + feedforward_out
    total_sums = lax.psum(
        (
            jnp.sum(live_mask * input_full * input_full),
            jnp.sum(attention_out * attention_out),
            jnp.sum(feedforward_out * feedforward_out),
            jnp.sum(live_mask * final_rows * final_rows),
            jnp.sum(live_mask),
        ),
        ("dp", "expert"),
    )
    residual_norms = jnp.sqrt(jnp.stack(total_sums[:4]) / (total_sums[4] * D))
    grad_final = cotangent[0].astype(jnp.float32)
    grad_gate = jnp.sum(picked * grad_final[:, None, :], axis=2) * live_mask
    grad_picked = (
        (expert_gate[..., None] * grad_final[:, None, :])
        .astype(jnp.bfloat16)
        .reshape(row_count * TOPK, D)
    )
    grad_rows = (
        jnp.zeros((total_experts * capacity, D), jnp.bfloat16).at[slot_index].set(grad_picked)
    )
    grad_recv = lax.all_to_all(
        grad_rows.reshape(groups, local_experts, capacity, D),
        "expert",
        split_axis=0,
        concat_axis=0,
        tiled=True,
    )
    grad_hidden = jnp.einsum(
        "sxcd,xfd->sxcf", grad_recv, expert_down, preferred_element_type=jnp.float32
    )
    grad_down = jnp.einsum("sxcf,sxcd->xfd", hidden, grad_recv, preferred_element_type=jnp.float32)
    pre_sig = jax.nn.sigmoid(preact)
    silu_slope = pre_sig * (1.0 + preact * (1.0 - pre_sig))
    grad_pre = (grad_hidden * silu_slope).astype(jnp.bfloat16)
    grad_up = jnp.einsum("sxcd,sxcf->xdf", received, grad_pre, preferred_element_type=jnp.float32)
    grad_sent = jnp.einsum(
        "sxcf,xdf->sxcd", grad_pre, expert_up, preferred_element_type=jnp.float32
    ).astype(jnp.bfloat16)
    grad_back = lax.all_to_all(grad_sent, "expert", split_axis=0, concat_axis=0, tiled=True)
    grad_returned = grad_back.reshape(total_experts * capacity, D)[slot_index].reshape(
        row_count, TOPK, D
    )
    grad_middle = grad_final + jnp.sum(grad_returned.astype(jnp.float32), axis=1)
    grad_pair_logit = grad_gate * pair_sig * (1.0 - pair_sig)
    grad_logit = jnp.einsum("tke,tk->te", pick_hot, grad_pair_logit, precision=PRECISE)
    grad_expert_router = exact_dot(normed_two_low.astype(jnp.float32).T, grad_logit)
    grad_normed_two = exact_dot(grad_logit, expert_router.astype(jnp.float32).T)
    unused_two, norm_two_back = jax.vjp(layer_norm, middle, gain_two)
    grad_middle_norm, grad_gain_two = norm_two_back(grad_normed_two)
    grad_middle = grad_middle + grad_middle_norm
    grad_branch = (live_mask * grad_middle).astype(jnp.bfloat16)
    grad_mixed = jnp.einsum(
        "td,md->tm", grad_branch, output_weight, preferred_element_type=jnp.float32
    ).reshape(row_count, HEADS, VE, HEAD_DIM)
    grad_output_weight = jnp.einsum(
        "tm,td->md", mixed, grad_branch, preferred_element_type=jnp.float32
    )
    grad_attended = jnp.sum(output_gate[..., None] * grad_mixed, axis=2)
    grad_output_logit = (
        jnp.sum(attended[:, :, None, :] * grad_mixed, axis=3)
        * output_hot
        * output_sig
        * (1.0 - output_sig)
    ).reshape(row_count, HEADS * VE)
    grad_attended_low = grad_attended.astype(jnp.bfloat16)
    grad_probs = jnp.einsum(
        "qhd,khd->hqk", grad_attended_low, value_heads, preferred_element_type=jnp.float32
    )
    row_dot = jnp.sum(soft_probs * grad_probs, axis=-1, keepdims=True)
    grad_scores = (soft_probs * (grad_probs - row_dot) * HEAD_DIM ** (-0.5)).astype(jnp.bfloat16)
    grad_query = (
        jnp.einsum("hqk,khd->qhd", grad_scores, key_heads, preferred_element_type=jnp.float32)
        .astype(jnp.bfloat16)
        .reshape(row_count, HEADS * HEAD_DIM)
    )
    grad_key_all = jnp.einsum(
        "hqk,qhd->khd", grad_scores, query_heads, preferred_element_type=jnp.float32
    ).reshape(-1, HEADS * HEAD_DIM)
    grad_value_rows = jnp.einsum(
        "hqk,qhd->khd",
        soft_probs.astype(jnp.bfloat16),
        grad_attended_low,
        preferred_element_type=jnp.float32,
    ).reshape(-1, HEADS * HEAD_DIM)
    grad_key_sum, grad_value_sum = (
        lax.psum_scatter(
            grad_key_all.astype(jnp.bfloat16), "dp", scatter_dimension=0, tiled=True
        ).astype(jnp.float32),
        lax.psum_scatter(
            grad_value_rows.astype(jnp.bfloat16), "dp", scatter_dimension=0, tiled=True
        ).astype(jnp.float32),
    )
    grad_key = grad_key_sum.astype(jnp.bfloat16)
    grad_value_low = (
        grad_value_sum.astype(jnp.bfloat16)
        .astype(jnp.float32)
        .reshape(row_count, HEADS, 1, HEAD_DIM)
    )
    grad_value_each = (
        (value_gate[..., None] * grad_value_low)
        .astype(jnp.bfloat16)
        .reshape(row_count, HEADS * VE * HEAD_DIM)
    )
    grad_value_logit = (
        jnp.sum(value_all * grad_value_low, axis=3) * value_hot * value_sig * (1.0 - value_sig)
    ).reshape(row_count, HEADS * VE)
    grad_value_weight = jnp.einsum(
        "td,tm->dm", input_low, grad_value_each, preferred_element_type=jnp.float32
    )
    grad_query_weight = jnp.einsum(
        "td,tm->dm", normed_low, grad_query, preferred_element_type=jnp.float32
    )
    grad_key_weight = jnp.einsum(
        "td,tm->dm", normed_low, grad_key, preferred_element_type=jnp.float32
    )
    normed_full = normed_low.astype(jnp.float32)
    grad_value_router = exact_dot(normed_full.T, grad_value_logit)
    grad_output_router = exact_dot(normed_full.T, grad_output_logit)
    grad_normed_one = (
        jnp.einsum("tm,dm->td", grad_query, query_weight, preferred_element_type=jnp.float32)
        + jnp.einsum("tm,dm->td", grad_key, key_weight, preferred_element_type=jnp.float32)
        + exact_dot(grad_value_logit, value_router.astype(jnp.float32).T)
        + exact_dot(grad_output_logit, output_router.astype(jnp.float32).T)
    )
    unused_one, norm_one_back = jax.vjp(layer_norm, input_full, gain_one)
    grad_input_norm, grad_gain_one = norm_one_back(grad_normed_one)
    grad_input = (
        grad_middle
        + jnp.einsum("tm,dm->td", grad_value_each, value_weight, preferred_element_type=jnp.float32)
        + grad_input_norm
    )
    dense_grads = (
        lax.psum_scatter(grad_query_weight, ("dp", "expert"), scatter_dimension=0, tiled=True),
        lax.psum_scatter(grad_key_weight, ("dp", "expert"), scatter_dimension=0, tiled=True),
        lax.psum_scatter(grad_value_weight, ("dp", "expert"), scatter_dimension=0, tiled=True),
        lax.psum_scatter(grad_output_weight, ("dp", "expert"), scatter_dimension=1, tiled=True),
        lax.psum_scatter(grad_value_router, ("dp", "expert"), scatter_dimension=0, tiled=True),
        lax.psum_scatter(grad_output_router, ("dp", "expert"), scatter_dimension=0, tiled=True),
        lax.psum_scatter(grad_expert_router, ("dp", "expert"), scatter_dimension=0, tiled=True),
        lax.psum_scatter(grad_gain_one, ("dp", "expert"), scatter_dimension=0, tiled=True),
        lax.psum_scatter(grad_gain_two, ("dp", "expert"), scatter_dimension=0, tiled=True),
    )
    expert_grads = (
        lax.psum_scatter(
            grad_up.astype(jnp.bfloat16), "dp", scatter_dimension=1, tiled=True
        ).astype(jnp.float32),
        lax.psum_scatter(
            grad_down.astype(jnp.bfloat16), "dp", scatter_dimension=2, tiled=True
        ).astype(jnp.float32),
    )
    return (
        final_rows.astype(jnp.bfloat16)[None],
        grad_input[None],
        dense_grads[0],
        dense_grads[1],
        dense_grads[2],
        dense_grads[3],
        dense_grads[4],
        dense_grads[5],
        dense_grads[6],
        dense_grads[7],
        dense_grads[8],
        expert_grads[0],
        expert_grads[1],
        residual_norms,
    )


def solution(mesh):
    placed = (
        P("expert", "dp", None),
        P("expert"),
        P("expert", "dp", None, None),
        P("expert", "dp", None, None),
        P("expert", "dp", None),
        P(),
        P(),
        P(),
        P(),
        P(),
        P(),
        P(),
        P(),
        P(),
        P("expert", None, None),
        P("expert", None, None),
        P("expert", "dp", None),
    )
    return jax.shard_map(
        shards,
        mesh=mesh,
        in_specs=placed,
        out_specs=(
            P("expert", "dp", None),
            P("expert", "dp", None),
            P(("dp", "expert"), None),
            P(("dp", "expert"), None),
            P(("dp", "expert"), None),
            P(None, ("dp", "expert")),
            P(("dp", "expert"), None),
            P(("dp", "expert"), None),
            P(("dp", "expert"), None),
            P(("dp", "expert")),
            P(("dp", "expert")),
            P("expert", "dp", None),
            P("expert", None, "dp"),
            P(),
        ),
        check_vma=False,
    )
```

profile of v0, /device:TPU:0, one launch (start us, length us, event | category | flops | bytes accessed | tf_op | source)
XLA Modules:
  0.0 2561.3 jit_solution(3722553074921668541)
XLA Ops:
  36.0 24.3 reduce-window.6
  84.0 69.3 %scatter_custom_fusion = bf16[6144,1024]{1,0:T(8,128)(2,1)} fusion(s32[4096]{0:T(1024)S(1)} %bitcast.257, bf16[256,1024]{1,0:T(8,128)(2,1)} %get-tuple-element.105, s32[4096]{0:T(1024)S(1)} %broadcast_clamp_fusion.1, bf16[]{:T(256)} %constant.60.clone.1), kind=kCustom, calls=%fused_computation.22 | custom fusion | bytes 12583424 | tf_op jit(solution)/shard_map/scatter | solution.py:135
  153.3 281.2 %all_to_all.20 = bf16[8,6,128,1024]{3,2,1,0:T(8,128)(2,1)} all-to-all(bf16[8,6,128,1024]{3,2,1,0:T(8,128)(2,1)} %bitcast.230), channel_id=1, replica_groups=mesh['dp'=4,'expert'=8] {'expert'}, dimensions={0} | all-to-all | bytes 25165824 | tf_op jit(solution)/shard_map/all_to_all | solution.py:138
  447.3 10.5 copy.138
  457.8 15.6 all-to-all-start.1
  476.5 270.4 %all-to-all-done.1 = bf16[8,6,128,1024]{3,2,1,0:T(8,128)(2,1)} async-done(((bf16[8,6,128,1024]{3,2,1,0:T(8,128)(2,1)}), bf16[8,6,128,1024]{3,2,1,0:T(8,128)(2,1)}, u32[]{:S(2)}, u32[]{:S(2)}) %all-to-all-start.1) | async-done | bytes 12582944 | tf_op jit(solution)/shard_map/all_to_all | solution.py:145
  746.9 27.0 %gather_fusion = bf16[4096,1024]{1,0:T(8,128)(2,1)} fusion(bf16[6144,1024]{1,0:T(8,128)(2,1)} %bitcast.27, s32[4096]{0:T(1024)S(1)} %broadcast_clamp_fusion), kind=kCustom, calls=%fused_computation.1 | custom fusion | bytes 16793600 | tf_op jit(solution)/shard_map/gather | solution.py:147
  784.8 26.7 %scatter_custom_fusion.1 = bf16[6144,1024]{1,0:T(8,128)(2,1)} fusion(s32[4096]{0:T(1024)S(1)} %bitcast.259, bf16[4096,1024]{1,0:T(8,128)(2,1)} %fusion.4, bf16[]{:T(256)} %constant.60.clone.1), kind=kCustom, calls=%fused_computation.25 | custom fusion | bytes 12583424 | tf_op jit(solution)/shard_map/scatter | solution.py:172
  811.5 281.0 %all_to_all.21 = bf16[8,6,128,1024]{3,2,1,0:T(8,128)(2,1)} all-to-all(bf16[8,6,128,1024]{3,2,1,0:T(8,128)(2,1)} %bitcast.229), channel_id=1, replica_groups=mesh['dp'=4,'expert'=8] {'expert'}, dimensions={0} | all-to-all | bytes 25165824 | tf_op jit(solution)/shard_map/all_to_all | solution.py:174
  1108.3 10.5 copy.140
  1142.0 255.9 %all-to-all-done.3 = bf16[8,6,128,1024]{3,2,1,0:T(8,128)(2,1)} async-done(((bf16[8,6,128,1024]{3,2,1,0:T(8,128)(2,1)}), bf16[8,6,128,1024]{3,2,1,0:T(8,128)(2,1)}, u32[]{:S(2)}, u32[]{:S(2)}) %all-to-all-start.3) | async-done | bytes 12582944 | tf_op jit(solution)/shard_map/all_to_all | solution.py:192
  1397.9 27.2 %gather_fusion.1 = bf16[4096,1024]{1,0:T(8,128)(2,1)} fusion(bf16[6144,1024]{1,0:T(8,128)(2,1)} %bitcast.38, s32[4096]{0:T(1024)S(1)} %broadcast_clamp_fusion), kind=kCustom, calls=%fused_computation.2 | custom fusion | bytes 16793600 | tf_op jit(solution)/shard_map/gather | solution.py:193
  1442.6 12.8 fusion.51
  1484.2 11.6 fusion.56
  1514.7 11.5 copy.174
  1532.1 31.9 %reduce-scatter.30.cloned.1.call-done = bf16[6,256,128]{2,1,0:T(8,128)(2,1)} async-done(((bf16[6,1024,128]{2,1,0:T(8,128)(2,1)}), bf16[6,256,128]{2,1,0:T(8,128)(2,1)}) %reduce-scatter.30.cloned.1.call-update) | async-done | bytes 393232 | tf_op jit(solution)/shard_map/reduce_scatter | solution.py:297
  1567.3 132.8 %reduce-scatter.38.cloned.1.call-done = f32[32,20]{1,0:T(8,128)} async-done(((f32[1024,20]{1,0:T(8,128)}), f32[32,20]{1,0:T(8,128)}) %reduce-scatter.38.cloned.1.call-update) | async-done | bytes 2576
  1706.6 37.4 %all-reduce.2 = (f32[1024]{0:T(1024)S(1)}, f32[1024]{0:T(1024)S(1)}, f32[1]{0:T(128)}, f32[1]{0:T(128)}, f32[1]{0:T(128)}, /*index=5*/f32[1]{0:T(128)}, f32[]{:T(128)}) all-reduce(f32[1024]{0:T(1024)S(1)} %get-tuple-element.88, f32[1024]{0:T(1024)S(1)} %get-tuple-element.93, ...), channel_id=11, replica_groups=mesh['dp'=4,'expert'=8] {'dp','expert'}, use_global_device_ids=true, to_apply=%region_35.36.clone | all-reduce | flops 2053 | bytes 16424
  1754.9 78.1 %reduce-scatter.36.cloned.1.call-done = f32[32,20]{1,0:T(8,128)} async-done(((f32[1024,20]{1,0:T(8,128)}), f32[32,20]{1,0:T(8,128)}) %reduce-scatter.36.cloned.1.call-update) | async-done | bytes 2576
  1834.4 131.8 %reduce-scatter.28.cloned.1.call-done = f32[32,48]{1,0:T(8,128)} async-done(((f32[1024,48]{1,0:T(8,128)}), f32[32,48]{1,0:T(8,128)}) %reduce-scatter.28.cloned.1.call-update) | async-done | bytes 6160 | tf_op jit(solution)/shard_map/reduce_scatter | solution.py:292
  1966.3 135.8 %reduce-scatter.22.cloned.1.call-done = f32[32,512]{1,0:T(8,128)} async-done(((f32[1024,512]{1,0:T(8,128)}), f32[32,512]{1,0:T(8,128)}) %reduce-scatter.22.cloned.1.call-update) | async-done | bytes 65552 | tf_op jit(solution)/shard_map/reduce_scatter | solution.py:286
  2102.1 135.7 %reduce-scatter.24.cloned.1.call-done = f32[32,512]{1,0:T(8,128)} async-done(((f32[1024,512]{1,0:T(8,128)}), f32[32,512]{1,0:T(8,128)}) %reduce-scatter.24.cloned.1.call-update) | async-done | bytes 65552 | tf_op jit(solution)/shard_map/reduce_scatter | solution.py:287
  2237.8 157.8 %reduce-scatter.26.cloned.1.call-done = f32[2560,32]{0,1:T(8,128)} async-done(((f32[2560,1024]{0,1:T(8,128)}), f32[2560,32]{0,1:T(8,128)}) %reduce-scatter.26.cloned.1.call-update) | async-done | bytes 327696 | tf_op jit(solution)/shard_map/reduce_scatter | solution.py:289
  2395.6 158.7 %reduce-scatter.34.cloned.1.call-done = f32[32,2560]{1,0:T(8,128)} async-done(((f32[1024,2560]{1,0:T(8,128)}), f32[32,2560]{1,0:T(8,128)}) %reduce-scatter.34.cloned.1.call-update) | async-done | bytes 327696
  (262 shorter events, 209.0 us)
Async XLA Ops:
  7.2 433.8 %copy-start = (bf16[6,128,1024]{2,1,0:T(8,128)(2,1)S(1)}, bf16[6,128,1024]{2,1,0:T(8,128)(2,1)}, u32[]{:S(2)}) copy-start(bf16[6,128,1024]{2,1,0:T(8,128)(2,1)} %param.32) | copy-start | bytes 4718596
  7.2 57.8 %all-gather.5.cloned.1.call-start = ((), (), s32[]{:S(2)}) async-start(), calls=%async_computation.16 | async-start | bytes 1310720 | tf_op jit(solution)/shard_map/all_gather | solution.py:94
  15.9 58.4 %all-gather.3.cloned.1.call-start = ((), (), s32[]{:S(2)}) async-start(), calls=%async_computation.15 | async-start | bytes 1310720 | tf_op jit(solution)/shard_map/all_gather | solution.py:95
  33.2 44.6 %copy-start.27 = (f32[256,4,5]{0,2,1:T(8,128)}, f32[256,4,5]{0,2,1:T(8,128)S(1)}, u32[]{:S(2)}) copy-start(f32[256,4,5]{0,2,1:T(8,128)S(1)} %copy.125) | copy-start | bytes 61444
  153.3 281.2 %copy-start.8 = (bf16[6,1024,128]{2,1,0:T(8,128)(2,1)S(1)}, bf16[6,1024,128]{2,1,0:T(8,128)(2,1)}, u32[]{:S(2)}) copy-start(bf16[6,1024,128]{2,1,0:T(8,128)(2,1)} %param.31) | copy-start | bytes 4718596
  457.8 289.1 %all-to-all-start.1 = ((bf16[8,6,128,1024]{3,2,1,0:T(8,128)(2,1)}), bf16[8,6,128,1024]{3,2,1,0:T(8,128)(2,1)}, u32[]{:S(2)}, u32[]{:S(2)}) async-start(bf16[8,6,128,1024]{3,2,1,0:T(8,128)(2,1)} %copy.138), calls=%async_computation.1 | async-start | bytes 25165824 | tf_op jit(solution)/shard_map/all_to_all | solution.py:145
  1118.7 279.2 %all-to-all-start.3 = ((bf16[8,6,128,1024]{3,2,1,0:T(8,128)(2,1)}), bf16[8,6,128,1024]{3,2,1,0:T(8,128)(2,1)}, u32[]{:S(2)}, u32[]{:S(2)}) async-start(bf16[8,6,128,1024]{3,2,1,0:T(8,128)(2,1)} %copy.140), calls=%async_computation.3 | async-start | bytes 25165824 | tf_op jit(solution)/shard_map/all_to_all | solution.py:192
  1124.2 352.5 %reduce-scatter.18.cloned.1.call-start = ((), (), s32[]{:S(2)}) async-start(), calls=%async_computation.17 | async-start | bytes 1310720 | tf_op jit(solution)/shard_map/reduce_scatter | solution.py:242
  1439.8 58.3 %reduce-scatter.20.cloned.1.call-start = ((), (), s32[]{:S(2)}) async-start(), calls=%async_computation.18 | async-start | bytes 1310720 | tf_op jit(solution)/shard_map/reduce_scatter | solution.py:239
  1455.4 74.7 %reduce-scatter.32.cloned.1.call-start = ((), (), s32[]{:S(2)}) async-start(), calls=%async_computation.24 | async-start | bytes 1966080 | tf_op jit(solution)/shard_map/reduce_scatter | solution.py:300
  1464.6 99.4 %reduce-scatter.30.cloned.1.call-start = ((), (), s32[]{:S(2)}) async-start(), calls=%async_computation.23 | async-start | bytes 1966080 | tf_op jit(solution)/shard_map/reduce_scatter | solution.py:297
  1474.9 225.2 %reduce-scatter.38.cloned.1.call-start = ((), (), s32[]{:S(2)}) async-start(), calls=%async_computation.27 | async-start | bytes 540672
  1476.6 356.4 %reduce-scatter.36.cloned.1.call-start = ((), (), s32[]{:S(2)}) async-start(), calls=%async_computation.26 | async-start | bytes 540672
  1482.5 483.7 %reduce-scatter.28.cloned.1.call-start = ((), (), s32[]{:S(2)}) async-start(), calls=%async_computation.22 | async-start | bytes 540672 | tf_op jit(solution)/shard_map/reduce_scatter | solution.py:292
  1484.2 617.9 %reduce-scatter.22.cloned.1.call-start = ((), (), s32[]{:S(2)}) async-start(), calls=%async_computation.19 | async-start | bytes 2162688 | tf_op jit(solution)/shard_map/reduce_scatter | solution.py:286
  1497.8 740.0 %reduce-scatter.24.cloned.1.call-start = ((), (), s32[]{:S(2)}) async-start(), calls=%async_computation.20 | async-start | bytes 2162688 | tf_op jit(solution)/shard_map/reduce_scatter | solution.py:287
  1500.9 894.7 %reduce-scatter.26.cloned.1.call-start = ((), (), s32[]{:S(2)}) async-start(), calls=%async_computation.21 | async-start | bytes 10813440 | tf_op jit(solution)/shard_map/reduce_scatter | solution.py:289
  1507.9 1046.4 %reduce-scatter.34.cloned.1.call-start = ((), (), s32[]{:S(2)}) async-start(), calls=%async_computation.25 | async-start | bytes 10813440
  1526.2 39.7 %copy-start.11 = (bf16[1024,512]{1,0:T(8,128)(2,1)S(1)}, bf16[1024,512]{1,0:T(8,128)(2,1)}, u32[]{:S(2)}) copy-start(bf16[1024,512]{1,0:T(8,128)(2,1)} %param.22) | copy-start | bytes 3145732
  1526.2 175.3 %copy-start.22 = (bf16[256,512]{0,1:T(8,128)(2,1)S(1)}, bf16[256,512]{0,1:T(8,128)(2,1)}, u32[]{:S(2)}) copy-start(bf16[256,512]{0,1:T(8,128)(2,1)} %reduce-scatter.20.cloned.1.call-done) | copy-start | bytes 786436
  1526.3 177.3 %copy-start.33 = (bf16[1024,20]{0,1:T(8,128)(2,1)S(1)}, bf16[1024,20]{0,1:T(8,128)(2,1)}, u32[]{:S(2)}) copy-start(bf16[1024,20]{0,1:T(8,128)(2,1)} %param.26) | copy-start | bytes 122884
  1565.9 138.4 %copy-start.35 = (bf16[1024,20]{0,1:T(8,128)(2,1)S(1)}, bf16[1024,20]{0,1:T(8,128)(2,1)}, u32[]{:S(2)}) copy-start(bf16[1024,20]{0,1:T(8,128)(2,1)} %param.27) | copy-start | bytes 122884
  1567.3 137.8 %copy-start.50 = (f32[256]{0:T(256)S(1)}, f32[256]{0:T(256)}, u32[]{:S(2)}) copy-start(f32[256]{0:T(256)} %copy-done.49) | copy-start | bytes 3076
  1748.9 805.5 %copy-start.1 = (bf16[6,128,1024]{2,1,0:T(8,128)(2,1)S(1)}, bf16[6,128,1024]{2,1,0:T(8,128)(2,1)}, u32[]{:S(2)}) copy-start(bf16[6,128,1024]{2,1,0:T(8,128)(2,1)} %param.32) | copy-start | bytes 4718596
  (49 other events, 365.1 us)
Sparse Core Ops, SparseCore 0:
  16.0 29.3 all-gather.4
  47.8 26.4 all-gather.2
  1439.9 25.6 reduce-scatter.17
  1468.6 27.7 reduce-scatter.19
  1499.2 30.8 reduce-scatter.31
  1533.0 30.9 reduce-scatter.29
  1566.2 133.8 reduce-scatter.37
  1702.5 130.5 reduce-scatter.35
  1835.8 130.3 reduce-scatter.27
  1969.0 133.0 reduce-scatter.21
  2104.9 132.8 reduce-scatter.23
  2240.6 154.9 reduce-scatter.25
  2398.6 155.6 reduce-scatter.33
where the time goes:
time: 2570 us; the launch traced here: 2560 us
  waiting for transfers between devices  1500 us (58%)
  blocking collectives  600 us (23%)
  local copies, waits for them, and re-layouts  207 us (8%)
  matrix products  143 us (6%)
  other arithmetic  77.2 us (3%)
    unnamed x16, waiting for transfers between devices  370 us
    all_to_all x1, blocking collectives, shards(): lax.all_to_all(outgoing, 'expert', split_axis=0, concat_axis=0, tiled=True)  281 us
    all_to_all x1, blocking collectives, shards(): lax.all_to_all(grad_rows.reshape(groups, local_experts, capacity, D), 'ex...  281 us
    all_to_all x1, waiting for transfers between devices, shards(): lax.all_to_all(result, 'expert', split_axis=0, concat_axis=0, tiled=True)  270 us
    all_to_all x1, waiting for transfers between devices, shards(): lax.all_to_all(grad_sent, 'expert', split_axis=0, concat_axis=0, tiled=True)  256 us
    reduce_scatter x1, waiting for transfers between devices, shards(): lax.psum_scatter(grad_output_weight, ('dp', 'expert'), scatter_dimension=...  158 us
    reduce_scatter x1, waiting for transfers between devices, shards(): lax.psum_scatter(grad_query_weight, ('dp', 'expert'), scatter_dimension=0...  136 us
    reduce_scatter x1, waiting for transfers between devices, shards(): lax.psum_scatter(grad_key_weight, ('dp', 'expert'), scatter_dimension=0,...  136 us
  transfers between devices with their start and end apart: 15, of which 12 were waited for; matrix products, arithmetic and copies ran while one was open for 7% of the time, Pallas kernels for 0%

commit v1 on v0

--- a/solution.py
+++ b/solution.py
@@ -7,20 +7,14 @@
 HEADS = 4
 HEAD_DIM = 128
 VE = 5
-TOPK = 16
 
 
 EPSILON = 1e-05
 NEGATIVE = -1000000000.0
-PRECISE = lax.Precision.HIGHEST
 
 
 def low_dot(left_side, right_side):
     return jnp.dot(left_side, right_side, preferred_element_type=jnp.float32)
-
-
-def exact_dot(left_side, right_side):
-    return jnp.dot(left_side, right_side, precision=PRECISE)
 
 
 def layer_norm(field, scale_gain):
@@ -44,6 +38,44 @@
     scores = jnp.where(allowed[None], raw_scores * HEAD_DIM ** (-0.5), NEGATIVE)
     exp_terms = jnp.exp(scores - jnp.max(scores, axis=-1, keepdims=True))
     return exp_terms / jnp.sum(exp_terms, axis=-1, keepdims=True)
+
+
+def expert_visit(sent, cotangent, expert_up, expert_down):
+    local_experts = expert_up.shape[0]
+    group = lax.axis_index("expert")
+    cot_all = lax.all_gather(cotangent, "expert", axis=0, tiled=True)
+    sent_all = lax.all_gather(sent, "expert", axis=0, tiled=True)
+    rows_all = sent_all[:, :D]
+    total_experts = sent.shape[1] - D
+    gate_all = lax.dynamic_slice_in_dim(
+        sent_all[:, D:], group * local_experts, local_experts, 1
+    ).astype(jnp.float32).T[:, :, None]
+    preact = jnp.einsum("td,xdf->xtf", rows_all, expert_up, preferred_element_type=jnp.float32)
+    pre_sig = jax.nn.sigmoid(preact)
+    hidden = preact * pre_sig
+    back = jnp.einsum("td,xfd->xtf", cot_all, expert_down, preferred_element_type=jnp.float32)
+    gate_grad = jnp.sum(hidden * back, axis=2).T
+    gated = (gate_all * hidden).astype(jnp.bfloat16)
+    grad_pre = (gate_all * back * (pre_sig * (1.0 + preact * (1.0 - pre_sig)))).astype(jnp.bfloat16)
+    partial_out = jnp.einsum("xtf,xfd->td", gated, expert_down, preferred_element_type=jnp.float32)
+    partial_grad = jnp.einsum("xtf,xdf->td", grad_pre, expert_up, preferred_element_type=jnp.float32)
+    wide_grad = lax.dynamic_update_slice_in_dim(
+        jnp.zeros((gate_grad.shape[0], total_experts), jnp.bfloat16),
+        gate_grad.astype(jnp.bfloat16),
+        group * local_experts,
+        1,
+    )
+    returned = lax.psum_scatter(
+        jnp.concatenate(
+            [partial_out.astype(jnp.bfloat16), partial_grad.astype(jnp.bfloat16), wide_grad], axis=1
+        ),
+        "expert",
+        scatter_dimension=0,
+        tiled=True,
+    )
+    grad_down = jnp.einsum("xtf,td->xfd", gated, cot_all, preferred_element_type=jnp.float32)
+    grad_up = jnp.einsum("td,xtf->xdf", rows_all, grad_pre, preferred_element_type=jnp.float32)
+    return returned, grad_up, grad_down
 
 
 def shards(
@@ -67,9 +99,6 @@
 ):
     row_count = hidden_in.shape[1]
     total_experts = expert_router.shape[1]
-    local_experts = expert_up.shape[0]
-    groups = lax.axis_size("expert")
-    capacity = (3 * row_count * TOPK + 2 * total_experts - 1) // (2 * total_experts)
     input_low = hidden_in[0]
     input_full = input_low.astype(jnp.float32)
     length = lengths[0]
@@ -117,38 +146,35 @@
     normed_two = layer_norm(middle, gain_two)
     normed_two_low = normed_two.astype(jnp.bfloat16)
     router_sig = jax.nn.sigmoid(low_dot(normed_two_low, expert_router))
-    flat_pick = expert_pick[0].reshape(-1)
-    pick_count = (flat_pick[:, None] == jnp.arange(total_experts, dtype=jnp.int32)).astype(
-        jnp.int32
-    )
-    pick_hot = pick_count.reshape(row_count, TOPK, total_experts).astype(jnp.float32)
-    pair_sig = jnp.einsum("tke,te->tk", pick_hot, router_sig, precision=PRECISE)
-    expert_gate = pair_sig * live_mask
-    running_count = jnp.cumsum(pick_count, axis=0, dtype=jnp.int32)
-    slot_rank = jnp.sum((running_count - pick_count) * pick_count, axis=1, dtype=jnp.int32)
-    slot_index = flat_pick * capacity + slot_rank
-    token_of = jnp.arange(row_count * TOPK, dtype=jnp.int32) // TOPK
+    hot = jnp.any(
+        expert_pick[0][:, :, None] == jnp.arange(total_experts, dtype=jnp.int32), axis=1
+    ).astype(jnp.float32)
+    picked_hot = hot * live_mask
+    expert_gate = router_sig * picked_hot
     middle_low = middle.astype(jnp.bfloat16)
-    dispatch = (
-        jnp.zeros((total_experts * capacity, D), jnp.bfloat16)
-        .at[slot_index]
-        .set(middle_low[token_of])
-    )
-    outgoing = dispatch.reshape(groups, local_experts, capacity, D)
-    received = lax.all_to_all(outgoing, "expert", split_axis=0, concat_axis=0, tiled=True)
-    preact = jnp.einsum("sxcd,xdf->sxcf", received, expert_up, preferred_element_type=jnp.float32)
-    hidden_rows = jax.nn.silu(preact).astype(jnp.bfloat16)
-    result = jnp.einsum(
-        "sxcf,xfd->sxcd", hidden_rows, expert_down, preferred_element_type=jnp.float32
-    ).astype(jnp.bfloat16)
-    result, hidden, received, preact = (result, hidden_rows, received, preact)
-    returned = lax.all_to_all(result, "expert", split_axis=0, concat_axis=0, tiled=True)
-    picked = (
-        returned.reshape(total_experts * capacity, D)[slot_index]
-        .reshape(row_count, TOPK, D)
-        .astype(jnp.float32)
-    )
-    feedforward_out = jnp.sum(expert_gate[..., None] * picked, axis=1)
+    sent = jnp.concatenate([middle_low, expert_gate.astype(jnp.bfloat16)], axis=1)
+    groups = lax.axis_size("expert")
+    rounds = max(1, groups // 8)
+
+    def visit(grads, item):
+        returned, grad_up, grad_down = expert_visit(*item, expert_up, expert_down)
+        return (grads[0] + grad_up, grads[1] + grad_down), returned
+
+    if rounds == 1:
+        returned, grad_up, grad_down = expert_visit(sent, cotangent[0], expert_up, expert_down)
+    else:
+        zeros = jnp.zeros(expert_up.shape, jnp.float32), jnp.zeros(expert_down.shape, jnp.float32)
+        (grad_up, grad_down), returned = lax.scan(
+            visit,
+            zeros,
+            (
+                sent.reshape(rounds, -1, sent.shape[1]),
+                cotangent[0].reshape(rounds, -1, D),
+            ),
+        )
+        returned = returned.reshape(row_count, -1)
+    returned = returned.astype(jnp.float32)
+    feedforward_out = returned[:, :D]
     final_rows = middle + feedforward_out
     total_sums = lax.psum(
         (
@@ -162,42 +188,12 @@
     )
     residual_norms = jnp.sqrt(jnp.stack(total_sums[:4]) / (total_sums[4] * D))
     grad_final = cotangent[0].astype(jnp.float32)
-    grad_gate = jnp.sum(picked * grad_final[:, None, :], axis=2) * live_mask
-    grad_picked = (
-        (expert_gate[..., None] * grad_final[:, None, :])
-        .astype(jnp.bfloat16)
-        .reshape(row_count * TOPK, D)
-    )
-    grad_rows = (
-        jnp.zeros((total_experts * capacity, D), jnp.bfloat16).at[slot_index].set(grad_picked)
-    )
-    grad_recv = lax.all_to_all(
-        grad_rows.reshape(groups, local_experts, capacity, D),
-        "expert",
-        split_axis=0,
-        concat_axis=0,
-        tiled=True,
-    )
-    grad_hidden = jnp.einsum(
-        "sxcd,xfd->sxcf", grad_recv, expert_down, preferred_element_type=jnp.float32
-    )
-    grad_down = jnp.einsum("sxcf,sxcd->xfd", hidden, grad_recv, preferred_element_type=jnp.float32)
-    pre_sig = jax.nn.sigmoid(preact)
-    silu_slope = pre_sig * (1.0 + preact * (1.0 - pre_sig))
-    grad_pre = (grad_hidden * silu_slope).astype(jnp.bfloat16)
-    grad_up = jnp.einsum("sxcd,sxcf->xdf", received, grad_pre, preferred_element_type=jnp.float32)
-    grad_sent = jnp.einsum(
-        "sxcf,xdf->sxcd", grad_pre, expert_up, preferred_element_type=jnp.float32
+    grad_middle = grad_final + returned[:, D : 2 * D]
+    grad_logit = (
+        returned[:, 2 * D :] * picked_hot * router_sig * (1.0 - router_sig)
     ).astype(jnp.bfloat16)
-    grad_back = lax.all_to_all(grad_sent, "expert", split_axis=0, concat_axis=0, tiled=True)
-    grad_returned = grad_back.reshape(total_experts * capacity, D)[slot_index].reshape(
-        row_count, TOPK, D
-    )
-    grad_middle = grad_final + jnp.sum(grad_returned.astype(jnp.float32), axis=1)
-    grad_pair_logit = grad_gate * pair_sig * (1.0 - pair_sig)
-    grad_logit = jnp.einsum("tke,tk->te", pick_hot, grad_pair_logit, precision=PRECISE)
-    grad_expert_router = exact_dot(normed_two_low.astype(jnp.float32).T, grad_logit)
-    grad_normed_two = exact_dot(grad_logit, expert_router.astype(jnp.float32).T)
+    grad_expert_router = low_dot(normed_two_low.T, grad_logit)
+    grad_normed_two = low_dot(grad_logit, expert_router.T)
     unused_two, norm_two_back = jax.vjp(layer_norm, middle, gain_two)
     grad_middle_norm, grad_gain_two = norm_two_back(grad_normed_two)
     grad_middle = grad_middle + grad_middle_norm
@@ -206,7 +202,7 @@
         "td,md->tm", grad_branch, output_weight, preferred_element_type=jnp.float32
     ).reshape(row_count, HEADS, VE, HEAD_DIM)
     grad_output_weight = jnp.einsum(
-        "tm,td->md", mixed, grad_branch, preferred_element_type=jnp.float32
+        "td,tm->dm", grad_branch, mixed, preferred_element_type=jnp.float32
     )
     grad_attended = jnp.sum(output_gate[..., None] * grad_mixed, axis=2)
     grad_output_logit = (
@@ -266,14 +262,15 @@
     grad_key_weight = jnp.einsum(
         "td,tm->dm", normed_low, grad_key, preferred_element_type=jnp.float32
     )
-    normed_full = normed_low.astype(jnp.float32)
-    grad_value_router = exact_dot(normed_full.T, grad_value_logit)
-    grad_output_router = exact_dot(normed_full.T, grad_output_logit)
+    grad_value_logit = grad_value_logit.astype(jnp.bfloat16)
+    grad_output_logit = grad_output_logit.astype(jnp.bfloat16)
+    grad_value_router = low_dot(normed_low.T, grad_value_logit)
+    grad_output_router = low_dot(normed_low.T, grad_output_logit)
     grad_normed_one = (
         jnp.einsum("tm,dm->td", grad_query, query_weight, preferred_element_type=jnp.float32)
         + jnp.einsum("tm,dm->td", grad_key, key_weight, preferred_element_type=jnp.float32)
-        + exact_dot(grad_value_logit, value_router.astype(jnp.float32).T)
-        + exact_dot(grad_output_logit, output_router.astype(jnp.float32).T)
+        + low_dot(grad_value_logit, value_router.T)
+        + low_dot(grad_output_logit, output_router.T)
     )
     unused_one, norm_one_back = jax.vjp(layer_norm, input_full, gain_one)
     grad_input_norm, grad_gain_one = norm_one_back(grad_normed_one)
@@ -282,17 +279,31 @@
         + jnp.einsum("tm,dm->td", grad_value_each, value_weight, preferred_element_type=jnp.float32)
         + grad_input_norm
     )
-    dense_grads = (
-        lax.psum_scatter(grad_query_weight, ("dp", "expert"), scatter_dimension=0, tiled=True),
-        lax.psum_scatter(grad_key_weight, ("dp", "expert"), scatter_dimension=0, tiled=True),
-        lax.psum_scatter(grad_value_weight, ("dp", "expert"), scatter_dimension=0, tiled=True),
-        lax.psum_scatter(grad_output_weight, ("dp", "expert"), scatter_dimension=1, tiled=True),
-        lax.psum_scatter(grad_value_router, ("dp", "expert"), scatter_dimension=0, tiled=True),
-        lax.psum_scatter(grad_output_router, ("dp", "expert"), scatter_dimension=0, tiled=True),
-        lax.psum_scatter(grad_expert_router, ("dp", "expert"), scatter_dimension=0, tiled=True),
-        lax.psum_scatter(grad_gain_one, ("dp", "expert"), scatter_dimension=0, tiled=True),
-        lax.psum_scatter(grad_gain_two, ("dp", "expert"), scatter_dimension=0, tiled=True),
-    )
+    parts = (
+        grad_query_weight,
+        grad_key_weight,
+        grad_value_weight,
+        grad_output_weight,
+        grad_value_router,
+        grad_output_router,
+        grad_expert_router,
+        grad_gain_one[:, None],
+        grad_gain_two[:, None],
+    )
+    summed = lax.psum_scatter(
+        jnp.concatenate([part.astype(jnp.bfloat16) for part in parts], axis=1),
+        ("dp", "expert"),
+        scatter_dimension=0,
+        tiled=True,
+    ).astype(jnp.float32)
+    dense_grads = []
+    start = 0
+    for part in parts:
+        dense_grads.append(summed[:, start : start + part.shape[1]])
+        start += part.shape[1]
+    dense_grads[3] = dense_grads[3].T
+    dense_grads[7] = dense_grads[7][:, 0]
+    dense_grads[8] = dense_grads[8][:, 0]
     expert_grads = (
         lax.psum_scatter(
             grad_up.astype(jnp.bfloat16), "dp", scatter_dimension=1, tiled=True

time: 2570 us -> 660 us (0.26)
  waiting for transfers between devices: 1500 us -> 316 us
  blocking collectives: 600 us -> 39.9 us
  local copies, waits for them, and re-layouts: 207 us -> 115 us
  other arithmetic: 77.2 us -> 36.3 us
    all_to_all x2 -> x0, blocking collectives: 562 us -> none  [the longest x1 281 us: shards(): lax.all_to_all(outgoing, 'expert', split_axis=0, concat_axis=0, tiled=True)]
    all_to_all x2 -> x0, waiting for transfers between devices: 526 us -> none  [the longest x1 270 us: shards(): lax.all_to_all(result, 'expert', split_axis=0, concat_axis=0, tiled=True)]
    reduce_scatter x4 -> x1, waiting for transfers between devices: 561 us -> 94.8 us  [expert_visit(): lax.psum_scatter(jnp.concatenate([partial_out.astype(jnp.bfloat16), parti...]
    unnamed x16 -> x11, waiting for transfers between devices: 370 us -> 110 us
    scatter x2 -> x0, local copies, waits for them, and re-layouts: 96 us -> none  [the longest x1 69.3 us: shards(): dispatch = jnp.zeros((total_experts * capacity, D), jnp.bfloat16).at[slot...]
    all_gather x0 -> x2, waiting for transfers between devices: none -> 78.4 us  [the longest x1 48.4 us: expert_visit(): sent_all = lax.all_gather(sent, 'expert', axis=0, tiled=True)]
    concatenate x0 -> x1, local copies, waits for them, and re-layouts: none -> 57.9 us  [shards(): jnp.concatenate([part.astype(jnp.bfloat16) for part in parts], axis=1)]
    gather x2 -> x0, local copies, waits for them, and re-layouts: 54.2 us -> none  [the longest x1 27.2 us: shards(): grad_back.reshape(total_experts * capacity, D)[slot_index]]
  transfers between devices with their start and end apart: 15 -> 10, of which waited for: 12 -> 6; matrix products, arithmetic and copies ran while one was open for 7% -> 31% of each run, Pallas kernels for 0% -> 0%
where the time goes in v1:
time: 660 us; the launch traced here: 650 us
  waiting for transfers between devices  316 us (48%)
  matrix products  125 us (19%)
  local copies, waits for them, and re-layouts  115 us (17%)
  blocking collectives  39.9 us (6%)
  other arithmetic  36.3 us (5%)
  between operations  16.9 us (3%)
    unnamed x11, waiting for transfers between devices  110 us
    reduce_scatter x1, waiting for transfers between devices, expert_visit(): lax.psum_scatter(jnp.concatenate([partial_out.astype(jnp.bfloat16), parti...  94.8 us
    concatenate x1, local copies, waits for them, and re-layouts, shards(): jnp.concatenate([part.astype(jnp.bfloat16) for part in parts], axis=1)  57.9 us
    all_gather x1, waiting for transfers between devices, expert_visit(): sent_all = lax.all_gather(sent, 'expert', axis=0, tiled=True)  48.4 us
    unnamed x158, local copies, waits for them, and re-layouts  44.8 us
    psum x1, blocking collectives, shards(): lax.psum((jnp.sum(live_mask * input_full * input_full), jnp.sum(attention...  39.9 us
    all_gather x1, waiting for transfers between devices, expert_visit(): cot_all = lax.all_gather(cotangent, 'expert', axis=0, tiled=True)  30 us
    all_gather x1, waiting for transfers between devices, shards(): lax.all_gather(value_local, 'dp', axis=0, tiled=True)  22.6 us
  transfers between devices with their start and end apart: 10, of which 6 were waited for; matrix products, arithmetic and copies ran while one was open for 31% of the time, Pallas kernels for 0%

profile of v1, /device:TPU:0, one launch (start us, length us, event | category | flops | bytes accessed | tf_op | source)
XLA Modules:
  0.0 650.0 jit_solution(15031494386543797718)
XLA Ops:
  17.9 8.0 %copy.150 = bf16[1024,2560]{0,1:T(8,128)(2,1)} copy(bf16[1024,2560]{1,0:T(8,128)(2,1)} %param.24) | data formatting | bytes 10485760 | tf_op args[7]
  26.0 6.5 %multiply_reduce_fusion.4 = (bf16[256,4,128]{0,2,1:T(8,128)(2,1)}, f32[256,4,5,128]{0,3,2,1:T(8,128)}) fusion(f32[256,4,5]{0,2,1:T(8,128)S(1)} %copy.149, bf16[4,5,128,1024]{3,2,1,0:T(8,128)(2,1)} %bitcast.187, bf16[1,256,1024]{2,1,0:T(8,128)(2,1)S(1)} %copy-done.2), kind=kOutput, calls=%fused_computation.36 | convolution fusion | flops 1343356928 | bytes 8671232 | tf_op jit(solution)/shard_map/dot_general | solution.py:17
  36.6 9.7 %all-gather.8.cloned.1.call-done = bf16[1024,512]{1,0:T(8,128)(2,1)} async-done(((bf16[256,512]{1,0:T(8,128)(2,1)}), bf16[1024,512]{1,0:T(8,128)(2,1)}) %all-gather.8.cloned.1.call-update) | async-done | bytes 1048592 | tf_op jit(solution)/shard_map/all_gather | solution.py:123
  47.9 4.9 fusion.109
  52.7 22.6 %all-gather.6.cloned.1.call-done = bf16[1024,512]{0,1:T(8,128)(2,1)} async-done(((bf16[256,512]{0,1:T(8,128)(2,1)}), bf16[1024,512]{0,1:T(8,128)(2,1)}) %all-gather.6.cloned.1.call-update) | async-done | bytes 1048592 | tf_op jit(solution)/shard_map/all_gather | solution.py:124
  79.1 6.0 fusion.106
  91.3 48.4 %all-gather.10.cloned.1.call-done = bf16[2048,1072]{1,0:T(8,128)(2,1)} async-done(((bf16[256,1072]{1,0:T(8,128)(2,1)}), bf16[2048,1072]{1,0:T(8,128)(2,1)}) %all-gather.10.cloned.1.call-update) | async-done | bytes 4390928 | tf_op jit(solution)/shard_map/all_gather | solution.py:47
  143.5 5.8 fusion.15
  152.0 5.1 bitcast_convert_fusion.1
  157.1 30.0 %all-gather.12.cloned.1.call-done = bf16[1,2048,1024]{2,1,0:T(8,128)(2,1)} async-done(((bf16[1,256,1024]{2,1,0:T(8,128)(2,1)}), bf16[1,2048,1024]{2,1,0:T(8,128)(2,1)}) %all-gather.12.cloned.1.call-update) | async-done | bytes 4194320 | tf_op jit(solution)/shard_map/all_gather | solution.py:46
  187.1 9.8 %fusion.3 = (bf16[6,2048,128]{1,2,0:T(8,128)(2,1)}, bf16[6,2048]{1,0:T(8,128)(2,1)S(1)}) fusion(f32[6,2048,128]{1,2,0:T(8,128)} %bitcast.205, f32[6,2048]{1,0:T(8,128)S(1)} %copy.155, bf16[6,128,1024]{2,1,0:T(8,128)(2,1)S(1)} %copy-done, bf16[1,2048,1024]{2,1,0:T(8,128)(2,1)} %all-gather.12.cloned.1.call-done), kind=kOutput, calls=%fused_computation.8 | convolution fusion | flops 3241660416 | bytes 15278080 | tf_op jit(solution)/shard_map/td,xfd->xtf/dot_general | solution.py:56
  197.2 7.8 %bitcast_convert_fusion = bf16[2048,1024]{1,0:T(8,128)(2,1)} fusion(bf16[6,2048,128]{1,2,0:T(8,128)(2,1)} %get-tuple-element.105, bf16[6,1024,128]{2,1,0:T(8,128)(2,1)} %param.31), kind=kOutput, calls=%fused_computation.3 | convolution fusion | flops 3223322624 | bytes 8912896 | tf_op jit(solution)/shard_map/xtf,xdf->td/dot_general | solution.py:61
  207.1 7.2 %pad_maximum_fusion = bf16[2048,2096]{1,0:T(8,128)(2,1)} fusion(bf16[2048,48]{1,0:T(8,128)(2,1)S(1)} %dynamic_update_slice.3, bf16[2048,1024]{1,0:T(8,128)(2,1)} %bitcast_convert_fusion, bf16[2048,1024]{1,0:T(8,128)(2,1)} %bitcast_convert_fusion.1), kind=kLoop, calls=%fused_computation.2 | loop fusion | flops 25755648 | bytes 17170432 | tf_op jit(solution)/shard_map/concatenate | solution.py:69
  214.6 94.8 %reduce-scatter.9.cloned.1.call-done = bf16[256,2096]{1,0:T(8,128)(2,1)} async-done(((bf16[2048,2096]{1,0:T(8,128)(2,1)}), bf16[256,2096]{1,0:T(8,128)(2,1)}) %reduce-scatter.9.cloned.1.call-update) | async-done | bytes 1073168 | tf_op jit(solution)/shard_map/reduce_scatter | solution.py:68
  321.6 12.8 %fusion.44 = bf16[4,128,1024]{2,1,0:T(8,128)(2,1)} fusion(bf16[256,4,128]{0,2,1:T(8,128)(2,1)S(1)} %bitcast.199, f32[4,256,1024]{2,1,0:T(8,128)} %fusion.112, f32[4,256,1024]{2,1,0:T(8,128)} %get-tuple-element.120, f32[4,256]{1,0:T(4,128)S(1)} %copy-done.71), kind=kOutput, calls=%fused_computation.60 | convolution fusion | flops 276301824 | bytes 9703424 | tf_op jit(solution)/shard_map/hqk,qhd->khd/dot_general | solution.py:225
  334.4 8.7 %fusion.31 = bf16[6,128,1024]{2,1,0:T(8,128)(2,1)} fusion(bf16[1,2048,1024]{2,1,0:T(8,128)(2,1)} %all-gather.12.cloned.1.call-done, f32[6,2048]{1,0:T(8,128)S(1)} %copy-done.41, f32[6,2048,128]{1,2,0:T(8,128)} %bitcast.206), kind=kOutput, calls=%fused_computation.50 | convolution fusion | flops 3231449088 | bytes 12107776 | tf_op jit(solution)/shard_map/xtf,td->xfd/dot_general | solution.py:76
  343.2 7.8 %fusion.41 = bf16[6,1024,128]{1,2,0:T(8,128)(2,1)} fusion(bf16[6,2048,128]{1,2,0:T(8,128)(2,1)} %get-tuple-element.105, bf16[2048,1072]{1,0:T(8,128)(2,1)} %all-gather.10.cloned.1.call-done), kind=kOutput, calls=%fused_computation.59 | convolution fusion | flops 3222011904 | bytes 8912896 | tf_op jit(solution)/shard_map/td,xtf->xdf/dot_general | solution.py:77
  352.4 11.7 %fusion.49 = bf16[4,128,256]{2,1,0:T(8,128)(2,1)S(1)} fusion(bf16[1024,4,128]{0,2,1:T(8,128)(2,1)} %bitcast.191, f32[4,256,1024]{2,1,0:T(8,128)} %fusion.112, f32[4,256,1024]{2,1,0:T(8,128)} %get-tuple-element.120, f32[4,256]{1,0:T(4,128)S(1)} %copy-done.71), kind=kOutput, calls=%fused_computation.73 | convolution fusion | flops 275908608 | bytes 9703424 | tf_op jit(solution)/shard_map/hqk,khd->qhd/dot_general | solution.py:221
  367.3 3.9 convolution_convert_fusion
  391.2 57.9 %concatenate.11 = bf16[1024,6234]{0,1:T(8,128)(2,1)} concatenate(bf16[1024,512]{0,1:T(8,128)(2,1)} %convolution_convert_fusion.4, bf16[1024,512]{0,1:T(8,128)(2,1)} %convolution_convert_fusion.3, bf16[1024,2560]{0,1:T(8,128)(2,1)} %fusion.6, bf16[1024,2560]{0,1:T(8,128)(2,1)} %convolution_convert_fusion, bf16[1024,20]{0,1:T(8,128)(2,1)S(1)} %convolution_convert_fusion.9, ...), dimensions={1} | concatenate | bytes 25534464 | tf_op jit(solution)/shard_map/concatenate | solution.py:294
  449.1 16.4 %copy.192 = bf16[1024,6234]{1,0:T(8,128)(2,1)} copy(bf16[1024,6234]{0,1:T(8,128)(2,1)} %concatenate.11) | data formatting | bytes 25534464
  470.2 39.9 %all-reduce = (f32[1]{0:T(128)}, f32[1]{0:T(128)}, f32[1]{0:T(128)}, f32[1]{0:T(128)}, f32[]{:T(128)}) all-reduce(f32[1]{0:T(128)} %bitcast.48, f32[1]{0:T(128)} %bitcast.47, f32[1]{0:T(128)} %bitcast.46, f32[1]{0:T(128)} %bitcast.45, f32[]{:T(128)} %fusion.100), channel_id=1, replica_groups=mesh['dp'=4,'expert'=8] {'dp','expert'}, use_global_device_ids=true, to_apply=%region_34.35 | all-reduce | flops 5 | bytes 40 | tf_op jit(solution)/shard_map/psum | solution.py:179
  514.0 5.6 fusion.48
  519.6 109.5 %reduce-scatter.19.cloned.1.call-done = bf16[32,6234]{1,0:T(8,128)(2,1)} async-done(((bf16[1024,6234]{1,0:T(8,128)(2,1)}), bf16[32,6234]{1,0:T(8,128)(2,1)}) %reduce-scatter.19.cloned.1.call-update) | async-done | bytes 398992
  (272 shorter events, 92.2 us)
Async XLA Ops:
  7.2 144.8 %copy-start = (bf16[6,128,1024]{2,1,0:T(8,128)(2,1)S(1)}, bf16[6,128,1024]{2,1,0:T(8,128)(2,1)}, u32[]{:S(2)}) copy-start(bf16[6,128,1024]{2,1,0:T(8,128)(2,1)} %param.32) | copy-start | bytes 4718596
  7.2 39.2 %all-gather.8.cloned.1.call-start = ((), (), s32[]{:S(2)}) async-start(), calls=%async_computation.7 | async-start | bytes 1310720 | tf_op jit(solution)/shard_map/all_gather | solution.py:123
  9.2 76.5 %copy-start.44 = (f32[256]{0:T(256)}, f32[256]{0:T(256)S(1)}, u32[]{:S(2)}) copy-start(f32[256]{0:T(256)S(1)} %compare_convert_fusion) | copy-start | bytes 3076
  16.9 58.4 %all-gather.6.cloned.1.call-start = ((), (), s32[]{:S(2)}) async-start(), calls=%async_computation.6 | async-start | bytes 1310720 | tf_op jit(solution)/shard_map/all_gather | solution.py:124
  32.5 107.1 %all-gather.10.cloned.1.call-start = ((), (), s32[]{:S(2)}) async-start(), calls=%async_computation.8 | async-start | bytes 5308416 | tf_op jit(solution)/shard_map/all_gather | solution.py:47
  32.6 52.9 %copy-start.42 = (f32[1024]{0:T(1024)}, f32[1024]{0:T(1024)S(1)}, u32[]{:S(2)}) copy-start(f32[1024]{0:T(1024)S(1)} %convert_element_type.241) | copy-start | bytes 12292
  32.9 52.9 %copy-start.32 = (pred[256,48]{1,0:T(32,128)(4,1)}, pred[256,48]{1,0:T(32,128)(4,1)S(1)}, u32[]{:S(2)}) copy-start(pred[256,48]{1,0:T(32,128)(4,1)S(1)} %copy.154) | copy-start | bytes 36868
  85.5 55.2 %copy-start.61 = (f32[256]{0:T(256)}, f32[256]{0:T(256)S(1)}, u32[]{:S(2)}) copy-start(f32[256]{0:T(256)S(1)} %multiply_reduce_fusion.9) | copy-start | bytes 3076
  85.5 55.2 %copy-start.55 = (f32[256]{0:T(256)}, f32[256]{0:T(256)S(1)}, u32[]{:S(2)}) copy-start(f32[256]{0:T(256)S(1)} %fusion.92) | copy-start | bytes 3076
  87.8 99.3 %all-gather.12.cloned.1.call-start = ((), (), s32[]{:S(2)}) async-start(), calls=%async_computation.14 | async-start | bytes 4718592 | tf_op jit(solution)/shard_map/all_gather | solution.py:46
  88.4 221.0 %reduce-scatter.9.cloned.1.call-start = ((), (), s32[]{:S(2)}) async-start(), calls=%async_computation.9 | async-start | bytes 10027008 | tf_op jit(solution)/shard_map/reduce_scatter | solution.py:68
  214.3 96.7 %copy-start.33 = (pred[256,48]{1,0:T(32,128)(4,1)S(1)}, pred[256,48]{1,0:T(32,128)(4,1)}, u32[]{:S(2)}) copy-start(pred[256,48]{1,0:T(32,128)(4,1)} %copy-done.32) | copy-start | bytes 36868
  214.3 96.7 %copy-start.45 = (f32[256]{0:T(256)S(1)}, f32[256]{0:T(256)}, u32[]{:S(2)}) copy-start(f32[256]{0:T(256)} %copy-done.44) | copy-start | bytes 3076
  214.3 97.0 %copy-start.43 = (f32[1024]{0:T(1024)S(1)}, f32[1024]{0:T(1024)}, u32[]{:S(2)}) copy-start(f32[1024]{0:T(1024)} %copy-done.42) | copy-start | bytes 12292
  214.3 97.0 %copy-start.52 = (f32[256]{0:T(256)S(1)}, f32[256]{0:T(256)}, u32[]{:S(2)}) copy-start(f32[256]{0:T(256)} %copy-done.51) | copy-start | bytes 3076
  214.4 97.0 %copy-start.56 = (f32[256]{0:T(256)S(1)}, f32[256]{0:T(256)}, u32[]{:S(2)}) copy-start(f32[256]{0:T(256)} %copy-done.55) | copy-start | bytes 3076
  214.4 99.3 %copy-start.62 = (f32[256]{0:T(256)S(1)}, f32[256]{0:T(256)}, u32[]{:S(2)}) copy-start(f32[256]{0:T(256)} %copy-done.61) | copy-start | bytes 3076
  214.4 158.9 %reduce-scatter.11.cloned.1.call-start = ((), (), s32[]{:S(2)}) async-start(), calls=%async_computation.10 | async-start | bytes 1310720 | tf_op jit(solution)/shard_map/reduce_scatter | solution.py:238
  318.8 61.3 %reduce-scatter.13.cloned.1.call-start = ((), (), s32[]{:S(2)}) async-start(), calls=%async_computation.11 | async-start | bytes 1310720 | tf_op jit(solution)/shard_map/reduce_scatter | solution.py:235
  334.4 131.9 %reduce-scatter.17.cloned.1.call-start = ((), (), s32[]{:S(2)}) async-start(), calls=%async_computation.13 | async-start | bytes 1966080 | tf_op jit(solution)/shard_map/reduce_scatter | solution.py:311
  343.2 125.0 %reduce-scatter.15.cloned.1.call-start = ((), (), s32[]{:S(2)}) async-start(), calls=%async_computation.12 | async-start | bytes 1966080 | tf_op jit(solution)/shard_map/reduce_scatter | solution.py:308
  351.1 278.0 %reduce-scatter.19.cloned.1.call-start = ((), (), s32[]{:S(2)}) async-start(), calls=%async_computation.15 | async-start | bytes 13246464
  465.6 48.4 %copy-start.50 = (f32[256]{0:T(256)S(1)}, f32[256]{0:T(256)}, u32[]{:S(2)}) copy-start(f32[256]{0:T(256)} %copy-done.48) | copy-start | bytes 3076
  465.6 48.4 %copy-start.60 = (f32[256]{0:T(256)S(1)}, f32[256]{0:T(256)}, u32[]{:S(2)}) copy-start(f32[256]{0:T(256)} %copy-done.58) | copy-start | bytes 3076
  (60 other events, 462.0 us)
Sparse Core Ops, SparseCore 0:
  17.0 29.3 all-gather.7
  48.8 26.4 all-gather.5
  87.9 51.7 all-gather.9
  141.1 45.9 all-gather.11
  214.4 94.9 reduce-scatter.8
  318.9 26.1 reduce-scatter.10
  348.2 27.7 reduce-scatter.12
  379.0 30.9 reduce-scatter.16
  412.9 30.9 reduce-scatter.14
  465.7 163.3 reduce-scatter.18

commit v2 on v1

--- a/solution.py
+++ b/solution.py
@@ -1,6 +1,10 @@
+import functools
+
 import jax
 import jax.numpy as jnp
 from jax import lax
+from jax.experimental import pallas as pl
+from jax.experimental.pallas import tpu as pltpu
 from jax.sharding import PartitionSpec as P
 
 D = 1024
@@ -9,6 +13,9 @@
 VE = 5
 
 
+MESH = pl.DeviceIdType.MESH
+ROWS = 32
+CHUNK = 512
 EPSILON = 1e-05
 NEGATIVE = -1000000000.0
 
@@ -76,6 +83,134 @@
     grad_down = jnp.einsum("xtf,td->xfd", gated, cot_all, preferred_element_type=jnp.float32)
     grad_up = jnp.einsum("td,xtf->xdf", rows_all, grad_pre, preferred_element_type=jnp.float32)
     return returned, grad_up, grad_down
+
+
+def dense_sum_kernel(widths, *refs):
+    n = len(widths)
+    grads, stats = refs[:n], refs[n]
+    outs, stats_out = refs[n + 1 : 2 * n + 1], refs[2 * n + 1]
+    core_in, near_in, far_in, line_in, total_in, send, recv = refs[2 * n + 2 :]
+    dp, ex = lax.axis_index("dp"), lax.axis_index("expert")
+    y, x, z, core = dp // 2, dp % 2, ex // 2, ex % 2
+    sibling = (dp, z * 2 + 1 - core)
+    beside = (y * 2 + 1 - x, ex)
+    behind = ((1 - y) * 2 + x, ex)
+    line = [(dp, ((z + k) % 4) * 2 + core) for k in (1, 2, 3)]
+    barrier = pltpu.get_barrier_semaphore()
+    for place in (sibling, beside, behind, *line):
+        pl.semaphore_signal(barrier, inc=1, device_id=place, device_id_type=MESH)
+    pl.semaphore_wait(barrier, 6)
+
+    pieces = []
+    for which, width in enumerate(widths):
+        for start in range(0, width, CHUNK):
+            pieces.append((which, start, min(CHUNK, width - start)))
+
+    def copy(source, target, slot, place):
+        made = pltpu.make_async_remote_copy(
+            src_ref=source, dst_ref=target, send_sem=send.at[slot], recv_sem=recv.at[slot],
+            device_id=place, device_id_type=MESH)
+        made.start()
+        return made
+
+    def add(target, source):
+        target[...] = (target[...].astype(jnp.float32) + source[...].astype(jnp.float32)).astype(target.dtype)
+
+    count = len(pieces)
+    first, second, third, fourth = {}, {}, {}, {}
+
+    def halve_core(i):
+        which, start, width = pieces[i]
+        columns = pl.ds(start, width)
+        first[i] = copy(grads[which].at[:, :, 1 - core, :, columns], core_in.at[i, :, :, :, pl.ds(0, width)], (i, 0), sibling)
+
+    def halve_near(i):
+        which, start, width = pieces[i]
+        first[i].wait()
+        held = core_in.at[i, :, :, :, pl.ds(0, width)]
+        add(held, grads[which].at[:, :, core, :, pl.ds(start, width)])
+        for half in range(2):
+            if i % 2 == 0:
+                source = core_in.at[i, half * 2 + 1 - x, :, :, pl.ds(0, width)]
+            else:
+                source = core_in.at[i, (1 - y) * 2 + half, :, :, pl.ds(0, width)]
+            second[i, half] = copy(source, near_in.at[i, half, :, :, pl.ds(0, width)], (i, 1 + half), beside if i % 2 == 0 else behind)
+
+    def halve_far(i):
+        which, start, width = pieces[i]
+        for half in range(2):
+            second[i, half].wait()
+            kept = half * 2 + x if i % 2 == 0 else y * 2 + half
+            add(near_in.at[i, half, :, :, pl.ds(0, width)], core_in.at[i, kept, :, :, pl.ds(0, width)])
+        other = 1 - y if i % 2 == 0 else 1 - x
+        third[i] = copy(near_in.at[i, other, :, :, pl.ds(0, width)], far_in.at[i, :, :, pl.ds(0, width)], (i, 3), behind if i % 2 == 0 else beside)
+
+    def spread_line(i):
+        which, start, width = pieces[i]
+        third[i].wait()
+        add(far_in.at[i, :, :, pl.ds(0, width)], near_in.at[i, y if i % 2 == 0 else x, :, :, pl.ds(0, width)])
+        for k in (1, 2, 3):
+            fourth[i, k] = copy(far_in.at[i, (z + k) % 4, :, pl.ds(0, width)], line_in.at[i, k - 1, :, pl.ds(0, width)], (i, 3 + k), line[k - 1])
+
+    def finish(i):
+        which, start, width = pieces[i]
+        columns = pl.ds(0, width)
+        total = far_in[i, z, :, columns].astype(jnp.float32)
+        for k in (1, 2, 3):
+            fourth[i, k].wait()
+            total = total + line_in[i, k - 1, :, columns].astype(jnp.float32)
+        outs[which][:, pl.ds(start, width)] = total
+
+    for i in range(count):
+        halve_core(i)
+    total_in[0] = stats[...]
+    rounds = [[sibling], [beside], [behind], line]
+    place = 1
+    for r, partners in enumerate(rounds):
+        copies = [copy(total_in.at[0], total_in.at[place + j], (count + j, r), p) for j, p in enumerate(partners)]
+        for made in copies:
+            made.wait()
+        summed = total_in[0]
+        for j in range(len(partners)):
+            summed = summed + total_in[place + j]
+        total_in[0] = summed
+        place += len(partners)
+    stats_out[...] = total_in[0]
+
+    lead, lag, tail = 4, 3, 2
+    for step in range(count + lead + lag + tail):
+        if step < count:
+            halve_near(step)
+        if 0 <= step - lead < count:
+            halve_far(step - lead)
+        if 0 <= step - lead - lag < count:
+            spread_line(step - lead - lag)
+        if 0 <= step - lead - lag - tail < count:
+            finish(step - lead - lag - tail)
+
+def dense_sum(grads, stats):
+    widths = [g.shape[1] for g in grads]
+    count = sum(-(-w // CHUNK) for w in widths)
+    vmem = pl.BlockSpec(memory_space=pltpu.VMEM)
+    low = jnp.bfloat16
+    outs = pl.pallas_call(
+        functools.partial(dense_sum_kernel, widths),
+        out_shape=[jax.ShapeDtypeStruct((ROWS, w), jnp.float32) for w in widths] + [jax.ShapeDtypeStruct((8, 128), jnp.float32)],
+        in_specs=[vmem] * (len(widths) + 1),
+        out_specs=[vmem] * (len(widths) + 1),
+        scratch_shapes=[
+            pltpu.VMEM((count, 4, 4, ROWS, CHUNK), low),
+            pltpu.VMEM((count, 2, 4, ROWS, CHUNK), low),
+            pltpu.VMEM((count, 4, ROWS, CHUNK), low),
+            pltpu.VMEM((count, 3, ROWS, CHUNK), low),
+            pltpu.VMEM((7, 8, 128), jnp.float32),
+            pltpu.SemaphoreType.DMA((count + 3, 7)),
+            pltpu.SemaphoreType.DMA((count + 3, 7)),
+        ],
+        compiler_params=pltpu.CompilerParams(collective_id=4, has_side_effects=True, vmem_limit_bytes=56 * 2**20),
+        name="dense_sum",
+    )(*[g.reshape(4, 4, 2, ROWS, g.shape[1]) for g in grads], stats)
+    return outs[:-1], outs[-1]
 
 
 def shards(
@@ -176,17 +311,15 @@
     returned = returned.astype(jnp.float32)
     feedforward_out = returned[:, :D]
     final_rows = middle + feedforward_out
-    total_sums = lax.psum(
-        (
+    sums = jnp.stack(
+        [
             jnp.sum(live_mask * input_full * input_full),
             jnp.sum(attention_out * attention_out),
             jnp.sum(feedforward_out * feedforward_out),
             jnp.sum(live_mask * final_rows * final_rows),
             jnp.sum(live_mask),
-        ),
-        ("dp", "expert"),
-    )
-    residual_norms = jnp.sqrt(jnp.stack(total_sums[:4]) / (total_sums[4] * D))
+        ]
+    )
     grad_final = cotangent[0].astype(jnp.float32)
     grad_middle = grad_final + returned[:, D : 2 * D]
     grad_logit = (
@@ -279,31 +412,51 @@
         + jnp.einsum("tm,dm->td", grad_value_each, value_weight, preferred_element_type=jnp.float32)
         + grad_input_norm
     )
-    parts = (
-        grad_query_weight,
-        grad_key_weight,
-        grad_value_weight,
-        grad_output_weight,
-        grad_value_router,
-        grad_output_router,
-        grad_expert_router,
-        grad_gain_one[:, None],
-        grad_gain_two[:, None],
-    )
-    summed = lax.psum_scatter(
-        jnp.concatenate([part.astype(jnp.bfloat16) for part in parts], axis=1),
-        ("dp", "expert"),
-        scatter_dimension=0,
-        tiled=True,
-    ).astype(jnp.float32)
-    dense_grads = []
-    start = 0
-    for part in parts:
-        dense_grads.append(summed[:, start : start + part.shape[1]])
-        start += part.shape[1]
-    dense_grads[3] = dense_grads[3].T
-    dense_grads[7] = dense_grads[7][:, 0]
-    dense_grads[8] = dense_grads[8][:, 0]
+    small_grads = jnp.concatenate(
+        [
+            grad_value_router,
+            grad_output_router,
+            grad_expert_router,
+            grad_gain_one[:, None],
+            grad_gain_two[:, None],
+        ],
+        axis=1,
+    )
+    small_count = small_grads.shape[1]
+    small_grads = jnp.pad(small_grads, ((0, 0), (0, -small_count % 128)))
+    low_grads = [
+        part.astype(jnp.bfloat16)
+        for part in (
+            grad_query_weight,
+            grad_key_weight,
+            grad_value_weight,
+            grad_output_weight,
+            small_grads,
+        )
+    ]
+    if lax.axis_size("dp") == 4 and lax.axis_size("expert") == 8:
+        dense_grads, sums_tile = dense_sum(low_grads, jnp.pad(sums[None], ((0, 7), (0, 123))))
+        total_sums = sums_tile[0, :5]
+    else:
+        summed = lax.psum_scatter(
+            jnp.concatenate(low_grads, axis=1), ("dp", "expert"), scatter_dimension=0, tiled=True
+        ).astype(jnp.float32)
+        dense_grads = jnp.split(summed, [512, 1024, 3584, 6144], axis=1)
+        total_sums = lax.psum(sums, ("dp", "expert"))
+    residual_norms = jnp.sqrt(total_sums[:4] / (total_sums[4] * D))
+    small = dense_grads[4]
+    router_end = 2 * HEADS * VE + expert_router.shape[1]
+    dense_grads = [
+        dense_grads[0],
+        dense_grads[1],
+        dense_grads[2],
+        dense_grads[3].T,
+        small[:, : HEADS * VE],
+        small[:, HEADS * VE : 2 * HEADS * VE],
+        small[:, 2 * HEADS * VE : router_end],
+        small[:, router_end],
+        small[:, router_end + 1],
+    ]
     expert_grads = (
         lax.psum_scatter(
             grad_up.astype(jnp.bfloat16), "dp", scatter_dimension=1, tiled=True

time: 660 us -> 576 us (0.87)
  Pallas kernels: 0 us -> 90.4 us
  local copies, waits for them, and re-layouts: 115 us -> 42 us
  waiting for transfers between devices: 316 us -> 257 us
  blocking collectives: 39.9 us -> 0 us
    unnamed x11 -> x9, waiting for transfers between devices: 110 us -> 0.65 us
    pallas_call x0 -> x1, Pallas kernels: none -> 90.4 us  [dense_sum(): pl.pallas_call(functools.partial(dense_sum_kernel, widths), out_shape=[ja...]
    concatenate x1, local copies, waits for them, and re-layouts: 57.9 us -> 0.46 us  [shards(): jnp.concatenate([grad_value_router, grad_output_router, grad_expert_route...]
    psum x1 -> x0, blocking collectives: 39.9 us -> none  [shards(): lax.psum((jnp.sum(live_mask * input_full * input_full), jnp.sum(attention...]
    reduce_scatter x1, waiting for transfers between devices: 0.01 us -> 32 us  [shards(): lax.psum_scatter(grad_up.astype(jnp.bfloat16), 'dp', scatter_dimension=1,...]
    unnamed x158 -> x150, local copies, waits for them, and re-layouts: 44.8 us -> 24 us
    reduce_scatter x1, waiting for transfers between devices: 0.01 us -> 19.7 us  [shards(): lax.psum_scatter(grad_down.astype(jnp.bfloat16), 'dp', scatter_dimension=...]
    reduce_scatter x1, waiting for transfers between devices: 94.8 us -> 78.2 us  [expert_visit(): lax.psum_scatter(jnp.concatenate([partial_out.astype(jnp.bfloat16), parti...]
  transfers between devices with their start and end apart: 10 -> 9, of which waited for: 6 -> 8; matrix products, arithmetic and copies ran while one was open for 31% -> 22% of each run, Pallas kernels for 0% -> 0%
where the time goes in v2:
time: 576 us; the launch traced here: 568 us
  waiting for transfers between devices  257 us (45%)
  matrix products  127 us (22%)
  Pallas kernels  90.4 us (16%)
  local copies, waits for them, and re-layouts  42 us (7%)
  other arithmetic  33.4 us (6%)
  between operations  16.8 us (3%)
    pallas_call x1, Pallas kernels, dense_sum(): pl.pallas_call(functools.partial(dense_sum_kernel, widths), out_shape=[ja...  90.4 us
    reduce_scatter x1, waiting for transfers between devices, expert_visit(): lax.psum_scatter(jnp.concatenate([partial_out.astype(jnp.bfloat16), parti...  78.2 us
    all_gather x1, waiting for transfers between devices, expert_visit(): sent_all = lax.all_gather(sent, 'expert', axis=0, tiled=True)  48.1 us
    reduce_scatter x1, waiting for transfers between devices, shards(): lax.psum_scatter(grad_up.astype(jnp.bfloat16), 'dp', scatter_dimension=1,...  32 us
    all_gather x1, waiting for transfers between devices, expert_visit(): cot_all = lax.all_gather(cotangent, 'expert', axis=0, tiled=True)  30 us
    unnamed x150, local copies, waits for them, and re-layouts  24 us
    all_gather x1, waiting for transfers between devices, shards(): lax.all_gather(value_local, 'dp', axis=0, tiled=True)  22.6 us
    reduce_scatter x1, waiting for transfers between devices, shards(): lax.psum_scatter(grad_down.astype(jnp.bfloat16), 'dp', scatter_dimension=...  19.7 us
  transfers between devices with their start and end apart: 9, of which 8 were waited for; matrix products, arithmetic and copies ran while one was open for 22% of the time, Pallas kernels for 0%

profile of v2, /device:TPU:0, one launch (start us, length us, event | category | flops | bytes accessed | tf_op | source)
XLA Modules:
  0.0 568.1 jit_solution(4475424628249638753)
XLA Ops:
  17.9 8.0 %copy.138 = bf16[1024,2560]{0,1:T(8,128)(2,1)} copy(bf16[1024,2560]{1,0:T(8,128)(2,1)} %param.24) | data formatting | bytes 10485760 | tf_op args[7]
  26.0 6.5 %multiply_reduce_fusion.4 = (bf16[256,4,128]{0,2,1:T(8,128)(2,1)}, f32[256,4,5,128]{0,3,2,1:T(8,128)}) fusion(f32[256,4,5]{0,2,1:T(8,128)S(1)} %copy.137, bf16[4,5,128,1024]{3,2,1,0:T(8,128)(2,1)} %bitcast.191, bf16[1,256,1024]{2,1,0:T(8,128)(2,1)S(1)} %copy-done.2), kind=kOutput, calls=%fused_computation.35 | convolution fusion | flops 1343356928 | bytes 8671232 | tf_op jit(solution)/shard_map/dot_general | solution.py:24
  36.6 9.7 %all-gather.8.cloned.1.call-done = bf16[1024,512]{1,0:T(8,128)(2,1)} async-done(((bf16[256,512]{1,0:T(8,128)(2,1)}), bf16[1024,512]{1,0:T(8,128)(2,1)}) %all-gather.8.cloned.1.call-update) | async-done | bytes 1048592 | tf_op jit(solution)/shard_map/all_gather | solution.py:258
  47.9 4.8 fusion.106
  52.7 22.6 %all-gather.6.cloned.1.call-done = bf16[1024,512]{0,1:T(8,128)(2,1)} async-done(((bf16[256,512]{0,1:T(8,128)(2,1)}), bf16[1024,512]{0,1:T(8,128)(2,1)}) %all-gather.6.cloned.1.call-update) | async-done | bytes 1048592 | tf_op jit(solution)/shard_map/all_gather | solution.py:259
  79.1 6.0 %fusion.104 = (bf16[256,1024]{1,0:T(8,128)(2,1)}, f32[256,1024]{1,0:T(8,128)S(1)}, f32[]{:T(128)}) fusion(bf16[1,256,1024]{2,1,0:T(8,128)(2,1)S(1)} %copy-done.3, bf16[256,2560]{0,1:T(8,128)(2,1)S(1)} %bitcast.192, bf16[2560,1024]{1,0:T(8,128)(2,1)} %param.25, f32[256]{0:T(256)S(1)} %compare_convert_fusion), kind=kOutput, calls=%fused_computation.171 | convolution fusion | flops 1343750144 | bytes 8651780 | tf_op jit(solution)/shard_map/dot_general | solution.py:24
  91.5 48.1 %all-gather.10.cloned.1.call-done = bf16[2048,1072]{1,0:T(8,128)(2,1)} async-done(((bf16[256,1072]{1,0:T(8,128)(2,1)}), bf16[2048,1072]{1,0:T(8,128)(2,1)}) %all-gather.10.cloned.1.call-update) | async-done | bytes 4390928 | tf_op jit(solution)/shard_map/all_gather | solution.py:54
  143.5 5.7 %fusion.14 = f32[2048,768]{0,1:S(1)} fusion(bf16[1024,768]{0,1:T(8,128)(2,1)} %bitcast.196, bf16[2048,1072]{1,0:T(8,128)(2,1)} %all-gather.10.cloned.1.call-done), kind=kOutput, calls=%fused_computation.27 | convolution fusion | flops 3221225472 | bytes 12058624
  151.9 5.1 bitcast_convert_fusion.1
  157.1 30.0 %all-gather.12.cloned.1.call-done = bf16[1,2048,1024]{2,1,0:T(8,128)(2,1)} async-done(((bf16[1,256,1024]{2,1,0:T(8,128)(2,1)}), bf16[1,2048,1024]{2,1,0:T(8,128)(2,1)}) %all-gather.12.cloned.1.call-update) | async-done | bytes 4194320 | tf_op jit(solution)/shard_map/all_gather | solution.py:53
  187.1 9.8 %fusion.3 = (bf16[6,2048,128]{1,2,0:T(8,128)(2,1)}, bf16[6,2048]{1,0:T(8,128)(2,1)S(1)}) fusion(f32[6,2048,128]{1,2,0:T(8,128)} %bitcast.216, f32[6,2048]{1,0:T(8,128)S(1)} %copy.143, bf16[6,128,1024]{2,1,0:T(8,128)(2,1)S(1)} %copy-done, bf16[1,2048,1024]{2,1,0:T(8,128)(2,1)} %all-gather.12.cloned.1.call-done), kind=kOutput, calls=%fused_computation.8 | convolution fusion | flops 3241660416 | bytes 15278080 | tf_op jit(solution)/shard_map/td,xfd->xtf/dot_general | solution.py:63
  197.2 7.8 %bitcast_convert_fusion = bf16[2048,1024]{1,0:T(8,128)(2,1)} fusion(bf16[6,2048,128]{1,2,0:T(8,128)(2,1)} %get-tuple-element.114, bf16[6,1024,128]{2,1,0:T(8,128)(2,1)} %param.31), kind=kOutput, calls=%fused_computation.3 | convolution fusion | flops 3223322624 | bytes 8912896 | tf_op jit(solution)/shard_map/xtf,xdf->td/dot_general | solution.py:68
  207.1 7.2 %pad_maximum_fusion = bf16[2048,2096]{1,0:T(8,128)(2,1)} fusion(bf16[2048,48]{1,0:T(8,128)(2,1)S(1)} %dynamic_update_slice.3, bf16[2048,1024]{1,0:T(8,128)(2,1)} %bitcast_convert_fusion, bf16[2048,1024]{1,0:T(8,128)(2,1)} %bitcast_convert_fusion.1), kind=kLoop, calls=%fused_computation.2 | loop fusion | flops 25755648 | bytes 17170432 | tf_op jit(solution)/shard_map/concatenate | solution.py:76
  214.5 8.7 %fusion.30 = bf16[6,128,1024]{2,1,0:T(8,128)(2,1)} fusion(bf16[1,2048,1024]{2,1,0:T(8,128)(2,1)} %all-gather.12.cloned.1.call-done, f32[6,2048]{1,0:T(8,128)S(1)} %copy.143, f32[6,2048,128]{1,2,0:T(8,128)} %bitcast.217), kind=kOutput, calls=%fused_computation.49 | convolution fusion | flops 3231449088 | bytes 12107776 | tf_op jit(solution)/shard_map/xtf,td->xfd/dot_general | solution.py:83
  223.3 7.8 %fusion.40 = bf16[6,1024,128]{1,2,0:T(8,128)(2,1)} fusion(bf16[6,2048,128]{1,2,0:T(8,128)(2,1)} %get-tuple-element.114, bf16[2048,1072]{1,0:T(8,128)(2,1)} %all-gather.10.cloned.1.call-done), kind=kOutput, calls=%fused_computation.58 | convolution fusion | flops 3222011904 | bytes 8912896 | tf_op jit(solution)/shard_map/td,xtf->xdf/dot_general | solution.py:84
  231.2 78.2 %reduce-scatter.6.cloned.1.call-done = bf16[256,2096]{1,0:T(8,128)(2,1)} async-done(((bf16[2048,2096]{1,0:T(8,128)(2,1)}), bf16[256,2096]{1,0:T(8,128)(2,1)}) %reduce-scatter.6.cloned.1.call-update) | async-done | bytes 1073168 | tf_op jit(solution)/shard_map/reduce_scatter | solution.py:75
  321.9 19.7 %reduce-scatter.14.cloned.1.call-done = bf16[6,128,256]{2,1,0:T(8,128)(2,1)} async-done(((bf16[6,128,1024]{2,1,0:T(8,128)(2,1)}), bf16[6,128,256]{2,1,0:T(8,128)(2,1)}) %reduce-scatter.14.cloned.1.call-update) | async-done | bytes 393232 | tf_op jit(solution)/shard_map/reduce_scatter | solution.py:464
  343.5 32.0 %reduce-scatter.12.cloned.1.call-done = bf16[6,256,128]{1,2,0:T(8,128)(2,1)} async-done(((bf16[6,1024,128]{1,2,0:T(8,128)(2,1)}), bf16[6,256,128]{1,2,0:T(8,128)(2,1)}) %reduce-scatter.12.cloned.1.call-update) | async-done | bytes 393232 | tf_op jit(solution)/shard_map/reduce_scatter | solution.py:461
  388.9 11.5 %fusion.48 = bf16[4,128,256]{2,1,0:T(8,128)(2,1)S(1)} fusion(bf16[1024,4,128]{0,2,1:T(8,128)(2,1)S(1)} %bitcast.200, f32[4,256,1024]{2,1,0:T(8,128)} %fusion.109, f32[4,256,1024]{2,1,0:T(8,128)} %get-tuple-element.125, f32[4,256]{1,0:T(4,128)S(1)} %copy-done.67), kind=kOutput, calls=%fused_computation.71 | convolution fusion | flops 275908608 | bytes 9703424 | tf_op jit(solution)/shard_map/hqk,khd->qhd/dot_general | solution.py:354
  400.5 12.7 %fusion.43 = bf16[4,128,1024]{2,1,0:T(8,128)(2,1)} fusion(bf16[256,4,128]{0,2,1:T(8,128)(2,1)S(1)} %bitcast.209, f32[4,256,1024]{2,1,0:T(8,128)} %fusion.109, f32[4,256,1024]{2,1,0:T(8,128)} %get-tuple-element.125, f32[4,256]{1,0:T(4,128)S(1)} %copy-done.67), kind=kOutput, calls=%fused_computation.59 | convolution fusion | flops 276301824 | bytes 9703424 | tf_op jit(solution)/shard_map/hqk,qhd->khd/dot_general | solution.py:358
  417.8 5.3 convolution_convert_fusion
  426.7 16.2 %reduce-scatter.10.cloned.1.call-done = bf16[256,512]{0,1:T(8,128)(2,1)} async-done(((bf16[1024,512]{0,1:T(8,128)(2,1)}), bf16[256,512]{0,1:T(8,128)(2,1)}) %reduce-scatter.10.cloned.1.call-update) | async-done | bytes 262160 | tf_op jit(solution)/shard_map/reduce_scatter | solution.py:368
  454.3 90.4 %dense_sum.1 = (f32[32,512]{1,0:T(8,128)}, f32[32,512]{1,0:T(8,128)}, f32[32,2560]{1,0:T(8,128)}, f32[32,2560]{1,0:T(8,128)}, f32[32,128]{1,0:T(8,128)}, /*index=5*/f32[8,128]{1,0:T(8,128)}) custom-call(bf16[4,4,2,32,512]{4,3,2,1,0:T(8,128)(2,1)} %bitcast.197, bf16[4,4,2,32,512]{4,3,2,1,0:T(8,128)(2,1)} %bitcast.194, bf16[4,4,2,32,2560]{4,3,2,1,0:T(8,128)(2,1)} %bitcast.184, ...), custom_call_target="tpu_custom_call" | custom-call | tf_op jit(solution)/shard_map/dense_sum/pallas_call | solution.py:196
  548.6 5.4 fusion.47
  (261 shorter events, 91.7 us)
Async XLA Ops:
  7.2 144.7 %copy-start = (bf16[6,128,1024]{2,1,0:T(8,128)(2,1)S(1)}, bf16[6,128,1024]{2,1,0:T(8,128)(2,1)}, u32[]{:S(2)}) copy-start(bf16[6,128,1024]{2,1,0:T(8,128)(2,1)} %param.32) | copy-start | bytes 4718596
  7.2 39.2 %all-gather.8.cloned.1.call-start = ((), (), s32[]{:S(2)}) async-start(), calls=%async_computation.6 | async-start | bytes 1310720 | tf_op jit(solution)/shard_map/all_gather | solution.py:258
  9.2 76.5 %copy-start.44 = (f32[256]{0:T(256)}, f32[256]{0:T(256)S(1)}, u32[]{:S(2)}) copy-start(f32[256]{0:T(256)S(1)} %compare_convert_fusion) | copy-start | bytes 3076
  16.9 58.4 %all-gather.6.cloned.1.call-start = ((), (), s32[]{:S(2)}) async-start(), calls=%async_computation.5 | async-start | bytes 1310720 | tf_op jit(solution)/shard_map/all_gather | solution.py:259
  32.5 107.1 %all-gather.10.cloned.1.call-start = ((), (), s32[]{:S(2)}) async-start(), calls=%async_computation.7 | async-start | bytes 5308416 | tf_op jit(solution)/shard_map/all_gather | solution.py:54
  32.6 52.9 %copy-start.43 = (f32[1024]{0:T(1024)}, f32[1024]{0:T(1024)S(1)}, u32[]{:S(2)}) copy-start(f32[1024]{0:T(1024)S(1)} %convert_element_type.206) | copy-start | bytes 12292
  85.5 55.2 %copy-start.58 = (f32[256]{0:T(256)}, f32[256]{0:T(256)S(1)}, u32[]{:S(2)}) copy-start(f32[256]{0:T(256)S(1)} %multiply_reduce_fusion.9) | copy-start | bytes 3076
  85.5 55.2 %copy-start.53 = (f32[256]{0:T(256)}, f32[256]{0:T(256)S(1)}, u32[]{:S(2)}) copy-start(f32[256]{0:T(256)S(1)} %fusion.91) | copy-start | bytes 3076
  87.8 99.3 %all-gather.12.cloned.1.call-start = ((), (), s32[]{:S(2)}) async-start(), calls=%async_computation.13 | async-start | bytes 4718592 | tf_op jit(solution)/shard_map/all_gather | solution.py:53
  88.4 221.0 %reduce-scatter.6.cloned.1.call-start = ((), (), s32[]{:S(2)}) async-start(), calls=%async_computation.8 | async-start | bytes 10027008 | tf_op jit(solution)/shard_map/reduce_scatter | solution.py:75
  214.3 127.2 %reduce-scatter.14.cloned.1.call-start = ((), (), s32[]{:S(2)}) async-start(), calls=%async_computation.12 | async-start | bytes 1966080 | tf_op jit(solution)/shard_map/reduce_scatter | solution.py:464
  223.2 152.3 %reduce-scatter.12.cloned.1.call-start = ((), (), s32[]{:S(2)}) async-start(), calls=%async_computation.11 | async-start | bytes 1966080 | tf_op jit(solution)/shard_map/reduce_scatter | solution.py:461
  231.1 79.9 %copy-start.37 = (pred[256,48]{1,0:T(32,128)(4,1)S(1)}, pred[256,48]{1,0:T(32,128)(4,1)}, u32[]{:S(2)}) copy-start(pred[256,48]{1,0:T(32,128)(4,1)} %copy-done.36) | copy-start | bytes 36868
  231.1 79.9 %copy-start.45 = (f32[256]{0:T(256)S(1)}, f32[256]{0:T(256)}, u32[]{:S(2)}) copy-start(f32[256]{0:T(256)} %copy-done.44) | copy-start | bytes 3076
  231.1 192.0 %reduce-scatter.8.cloned.1.call-start = ((), (), s32[]{:S(2)}) async-start(), calls=%async_computation.9 | async-start | bytes 1310720 | tf_op jit(solution)/shard_map/reduce_scatter | solution.py:371
  316.5 101.3 %copy-start.5 = (f32[256,1024]{1,0:T(8,128)}, f32[256,1024]{1,0:T(8,128)S(1)}, u32[]{:S(2)}) copy-start(f32[256,1024]{1,0:T(8,128)S(1)} %fusion.68) | copy-start | bytes 3145732
  319.3 62.0 %copy-start.59 = (bf16[1024]{0:T(1024)(128)(2,1)S(1)}, bf16[1024]{0:T(1024)(128)(2,1)}, u32[]{:S(2)}) copy-start(bf16[1024]{0:T(1024)(128)(2,1)} %get-tuple-element.105) | copy-start | bytes 6148
  319.3 62.6 %copy-start.33 = (f32[256,4,5]{0,1,2:T(4,128)S(1)}, f32[256,4,5]{0,1,2:T(4,128)}, u32[]{:S(2)}) copy-start(f32[256,4,5]{0,1,2:T(4,128)} %copy-done.32) | copy-start | bytes 61444
  319.3 64.8 %copy-start.13 = (bf16[256,1024]{1,0:T(8,128)(2,1)S(1)}, bf16[256,1024]{1,0:T(8,128)(2,1)}, u32[]{:S(2)}) copy-start(bf16[256,1024]{1,0:T(8,128)(2,1)} %copy-done.12) | copy-start | bytes 1572868
  321.0 122.0 %reduce-scatter.10.cloned.1.call-start = ((), (), s32[]{:S(2)}) async-start(), calls=%async_computation.10 | async-start | bytes 1310720 | tf_op jit(solution)/shard_map/reduce_scatter | solution.py:368
  321.9 67.1 %copy-start.18 = (bf16[1024,512]{0,1:T(8,128)(2,1)S(1)}, bf16[1024,512]{0,1:T(8,128)(2,1)}, u32[]{:S(2)}) copy-start(bf16[1024,512]{0,1:T(8,128)(2,1)} %copy-done.17) | copy-start | bytes 3145732
  454.3 94.2 %copy-start.6 = (f32[256,1024]{1,0:T(8,128)S(1)}, f32[256,1024]{1,0:T(8,128)}, u32[]{:S(2)}) copy-start(f32[256,1024]{1,0:T(8,128)} %copy-done.5) | copy-start | bytes 3145732
  454.3 94.2 %copy-start.8 = (bf16[256,4,5,128]{0,3,2,1:T(8,128)(2,1)S(1)}, bf16[256,4,5,128]{0,3,2,1:T(8,128)(2,1)}, u32[]{:S(2)}) copy-start(bf16[256,4,5,128]{0,3,2,1:T(8,128)(2,1)} %copy-done.7) | copy-start | bytes 3932164
  454.3 94.2 %copy-start.11 = (f32[256,1024]{1,0:T(8,128)S(1)}, f32[256,1024]{1,0:T(8,128)}, u32[]{:S(2)}) copy-start(f32[256,1024]{1,0:T(8,128)} %copy-done.10) | copy-start | bytes 3145732
  (55 other events, 533.7 us)
Sparse Core Ops, SparseCore 0:
  17.0 29.3 all-gather.7
  48.8 26.4 all-gather.5
  87.9 51.7 all-gather.9
  141.1 45.9 all-gather.11
  214.4 94.9 reduce-scatter.5
  312.2 29.2 reduce-scatter.13
  344.5 30.9 reduce-scatter.11
  378.4 27.7 reduce-scatter.7
  415.0 27.8 reduce-scatter.9

commit v3 on v2

--- a/solution.py
+++ b/solution.py
@@ -45,6 +45,2288 @@
     scores = jnp.where(allowed[None], raw_scores * HEAD_DIM ** (-0.5), NEGATIVE)
     exp_terms = jnp.exp(scores - jnp.max(scores, axis=-1, keepdims=True))
     return exp_terms / jnp.sum(exp_terms, axis=-1, keepdims=True)
+
+
+def dot_last(left_side, right_side):
+    return lax.dot_general(
+        left_side, right_side, (((1,), (1,)), ((), ())), preferred_element_type=jnp.float32
+    )
+
+def dot_first(left_side, right_side):
+    return lax.dot_general(
+        left_side, right_side, (((0,), (0,)), ((), ())), preferred_element_type=jnp.float32
+    )
+
+
+def visit_kernel(
+    sent, cot, up, down, back_out, up_out, down_out,
+    rows, cot_other, up_wide, chosen, cots, gated, grad_pre, gated_turned, pre_turned, partial, paired_in, chain_in, up_low, down_low, up_in, down_in,
+    row_send, row_recv, cot_send, cot_recv, pair_send, pair_recv, chain_send, chain_recv, grad_send, grad_recv,
+):
+    experts = up.shape[0]
+    wide = down.shape[0]
+    hidden = wide // experts
+    dp, ex = lax.axis_index("dp"), lax.axis_index("expert")
+    y, x, z, core = dp // 2, dp % 2, ex // 2, ex % 2
+    half = z // 2
+    inner = z + half * (3 - 2 * z)
+    onward = 1 - 2 * half
+    sibling = (dp, z * 2 + 1 - core)
+    beside, behind = (y * 2 + 1 - x, ex), ((1 - y) * 2 + x, ex)
+
+    def at_z(place):
+        return (dp, place * 2 + core)
+
+    barrier = pltpu.get_barrier_semaphore()
+    for place in (sibling, beside, behind):
+        pl.semaphore_signal(barrier, inc=1, device_id=place, device_id_type=MESH)
+
+    @pl.when(z < 3)
+    def _():
+        pl.semaphore_signal(barrier, inc=1, device_id=at_z(z + 1), device_id_type=MESH)
+
+    @pl.when(z > 0)
+    def _():
+        pl.semaphore_signal(barrier, inc=1, device_id=at_z(z - 1), device_id_type=MESH)
+
+    pl.semaphore_wait(barrier, 4 + inner)
+
+    def remote(source, target, send, recv, place):
+        return pltpu.make_async_remote_copy(
+            src_ref=source, dst_ref=target, send_sem=send, recv_sem=recv, device_id=place, device_id_type=MESH
+        )
+
+    def row_copy(way, at, source=None):
+        place = (sibling, at_z(z + 1), at_z(z - 1))[way]
+        block = rows.at[at]
+        target = block if way else rows.at[4 + at]
+        return remote(block if source is None else source, target, row_send.at[way, at], row_recv.at[0 if way else 1, at], place)
+
+    def cot_copy(at):
+        return remote(cot.at[at], cot_other.at[at], cot_send.at[at], cot_recv.at[at], sibling)
+
+    own = row_copy(0, z, sent), row_copy(1, z, sent), row_copy(2, z, sent)
+
+    @pl.when(z < 3)
+    def _():
+        own[1].start()
+
+    @pl.when(z > 0)
+    def _():
+        own[2].start()
+
+    own[0].start()
+    cot_copy(z).start()
+    for k in (1, 2, 3):
+        cot_copy((z + k) % 4).start()
+    rows[z] = sent[...]
+    for e in range(experts):
+        up_wide[:, e * hidden : (e + 1) * hidden] = up[e]
+    chosen[...] = (
+        lax.broadcasted_iota(jnp.int32, (128, wide), 0)
+        == 2 * HEADS * VE + ex * experts + lax.broadcasted_iota(jnp.int32, (128, wide), 1) // hidden
+    ).astype(jnp.float32).astype(jnp.bfloat16)
+
+    def order(p):
+        later = (p + 2) // 3
+        step = p - inner // (p + 1 - later)
+        return later * (step + half * (3 - 2 * step)) + (1 - later) * z
+
+    def pair_copy(at):
+        return remote(partial.at[1, at], paired_in.at[at], pair_send.at[at], pair_recv.at[at], sibling)
+
+    spans = (pl.ds(0, D), pl.ds(D, D + 128))
+
+    def chain_copy(dest, slot, to, stage, part):
+        span = spans[part]
+        return remote(
+            partial.at[0, dest, :, span], chain_in.at[slot, :, span],
+            chain_send.at[stage, part], chain_recv.at[slot, part], at_z(to),
+        )
+
+    def add(target, source):
+        def some(i, carry):
+            part = pl.ds(pl.multiple_of(i * 32, 32), 32)
+            target[part, :] = (
+                target[part, :].astype(jnp.float32) + source[part, :].astype(jnp.float32)
+            ).astype(target.dtype)
+            return carry
+
+        lax.fori_loop(0, target.shape[0] // 32, some, 0)
+
+    def visit(q, carry):
+        p, other = q // 2, q % 2
+        at = order(p)
+        block = other * 4 + at
+
+        @pl.when((other == 0) & (p > 0))
+        def _():
+            row_copy(1, at).wait_recv()
+            row_copy(0, at).start()
+
+            @pl.when((at < z) & (z < 3))
+            def _():
+                row_copy(1, at).start()
+
+            @pl.when((at > z) & (z > 0))
+            def _():
+                row_copy(2, at).start()
+
+        @pl.when(other == 1)
+        def _():
+            row_copy(0, at).wait_recv()
+            cot_copy(at).wait_recv()
+            cots[...] = cot_other[at]
+
+        @pl.when(other == 0)
+        def _():
+            cots[...] = cot[at]
+
+        count = rows.shape[1]
+        places = pl.ds(pl.multiple_of(block * count, count), count)
+
+        def columns(n, gate_grad):
+            span = pl.ds(pl.multiple_of(n * 256, 256), 256)
+            pre = jnp.dot(rows[block, :, :D], up_wide[:, span], preferred_element_type=jnp.float32)
+            back = dot_last(cots[...], down[span, :])
+            mark = chosen[:, span]
+            gate = jnp.dot(rows[block, :, D:], mark, preferred_element_type=jnp.float32)
+            sig = jax.nn.sigmoid(pre)
+            act = pre * sig
+            act_low = (gate * act).astype(jnp.bfloat16)
+            pre_low = (gate * back * (sig * (1.0 + pre * (1.0 - sig)))).astype(jnp.bfloat16)
+            gated[:, span] = act_low
+            grad_pre[:, span] = pre_low
+            gated_turned[span, places] = act_low.T
+            pre_turned[span, places] = pre_low.T
+            return gate_grad + dot_last((act * back).astype(jnp.bfloat16), mark)
+
+        partial[other, at, :, 2 * D :] = lax.fori_loop(
+            0, wide // 256, columns, jnp.zeros((count, 128), jnp.float32)
+        ).astype(jnp.bfloat16)
+
+        def outward(n, carry):
+            span = pl.ds(pl.multiple_of(n * 256, 256), 256)
+            partial[other, at, :, span] = jnp.dot(
+                gated[...], down[:, span], preferred_element_type=jnp.float32
+            ).astype(jnp.bfloat16)
+            partial[other, at, :, pl.ds(pl.multiple_of(D + n * 256, 256), 256)] = dot_last(
+                grad_pre[...], up_wide[span, :]
+            ).astype(jnp.bfloat16)
+            return carry
+
+        lax.fori_loop(0, D // 256, outward, 0)
+
+        @pl.when(other == 1)
+        def _():
+            pair_copy(at).start()
+            pair_copy(at).wait_recv()
+            add(partial.at[0, at], paired_in.at[at])
+
+        @pl.when((inner == 0) & (q == 3))
+        def _():
+            chain_copy(*nearest, 0).start()
+
+        @pl.when((inner == 0) & (q == 5))
+        def _():
+            chain_copy(*next_one, 0).start()
+
+        return carry
+
+    nearest = (z + onward, z + onward, z + onward, 0)
+    farthest = (3 * (1 - half), 3 * (1 - half), z + onward, 1)
+    backward = (3 * half, 3 * half, z - onward, 2)
+    next_one = (2 - half, 2 - half + inner * (2 + half), z + onward, 3)
+    lax.fori_loop(0, 8, visit, 0)
+
+    def relay(dest, slot, to, stage, part):
+        chain_copy(dest, dest, to, stage, part).wait_recv()
+        add(partial.at[0, dest, :, spans[part]], chain_in.at[dest, :, spans[part]])
+        chain_copy(dest, slot, to, stage, part).start()
+
+    @pl.when(inner == 0)
+    def _():
+        chain_copy(*farthest, 0).start()
+        chain_copy(*farthest, 1).start()
+        chain_copy(*next_one, 1).start()
+        chain_copy(*nearest, 1).start()
+
+    @pl.when(inner == 1)
+    def _():
+        relay(*next_one, 0)
+
+    tokens_all = rows.reshape(rows.shape[0] * rows.shape[1], rows.shape[2])
+    cots_own = cot.reshape(cot.shape[0] * cot.shape[1], D)
+    cots_other = cot_other.reshape(cot.shape[0] * cot.shape[1], D)
+    place = cots_own.shape[0]
+    quarter = D // 4
+
+
+    def up_copy(j):
+        return remote(up_low.at[j], up_in.at[j], grad_send.at[0, j], grad_recv.at[0, j], behind if j == 2 else beside)
+
+    def down_copy(j):
+        return remote(down_low.at[j], down_in.at[j], grad_send.at[1, j], grad_recv.at[1, j], beside if j == 1 else behind)
+
+    def weight_grads(j, carry):
+        across, aside = 1 - j % 2, 1 - j // 2
+        at = (y + across * (1 - 2 * y)) * 2 + x + aside * (1 - 2 * x)
+        span = pl.ds(pl.multiple_of(at * quarter, quarter), quarter)
+        up_low[j] = jnp.dot(
+            pre_turned[...], tokens_all[:, span], preferred_element_type=jnp.float32
+        ).astype(jnp.bfloat16)
+        down_low[j] = (
+            jnp.dot(gated_turned[:, :place], cots_own[:, span], preferred_element_type=jnp.float32)
+            + jnp.dot(gated_turned[:, place:], cots_other[:, span], preferred_element_type=jnp.float32)
+        ).astype(jnp.bfloat16)
+
+        @pl.when(j == 0)
+        def _():
+            up_copy(0).start()
+            down_copy(0).start()
+
+        @pl.when(j == 1)
+        def _():
+            up_copy(1).start()
+
+        @pl.when(j == 2)
+        def _():
+            down_copy(2).start()
+
+        return carry
+
+    lax.fori_loop(0, 4, weight_grads, 0)
+    up_copy(0).wait()
+    add(up_low.at[2], up_in.at[0])
+    up_copy(2).start()
+    down_copy(0).wait()
+    add(down_low.at[1], down_in.at[0])
+    down_copy(1).start()
+
+    @pl.when(inner == 1)
+    def _():
+        for way, part in ((farthest, 0), (backward, 0), (farthest, 1), (backward, 1), (next_one, 1)):
+            relay(*way, part)
+
+    up_sum = up_low[3].astype(jnp.float32)
+    down_sum = down_low[3].astype(jnp.float32)
+    for j in (1, 2):
+        up_copy(j).wait()
+        up_sum += up_in[j].astype(jnp.float32)
+        down_copy(j).wait()
+        down_sum += down_in[j].astype(jnp.float32)
+    for e in range(experts):
+        up_out[e] = up_sum[e * hidden : (e + 1) * hidden, :].T
+        down_out[e] = down_sum[e * hidden : (e + 1) * hidden, :]
+
+    for part in range(2):
+        span = spans[part]
+        chain_copy(z, z, z, 0, part).wait_recv()
+        back_out[:, span] = partial[0, z, :, span].astype(jnp.float32) + chain_in[z, :, span].astype(jnp.float32)
+
+        @pl.when(inner == 1)
+        def _():
+            chain_copy(z, 4, z, 0, part).wait_recv()
+            back_out[:, span] = back_out[:, span] + chain_in[4, :, span].astype(jnp.float32)
+
+    for at in range(4):
+        row_copy(0, at).wait_send()
+        cot_copy(at).wait_send()
+        pair_copy(at).wait_send()
+
+        @pl.when((at <= z) & (z < 3))
+        def _():
+            row_copy(1, at).wait_send()
+
+        @pl.when((at >= z) & (z > 0))
+        def _():
+            row_copy(2, at).wait_send()
+
+    for part in range(2):
+
+        @pl.when(inner == 0)
+        def _():
+            chain_copy(z, 0, z, 0, part).wait_send()
+
+        @pl.when(inner == 1)
+        def _():
+            chain_copy(z, 0, z, 2, part).wait_send()
+
+        chain_copy(z, 0, z, 1, part).wait_send()
+        chain_copy(z, 0, z, 3, part).wait_send()
+
+def expert_kernel_visit(sent, cot_line, up, down):
+    tokens = sent.shape[0]
+    experts, _, hidden = up.shape
+    wide = experts * hidden
+    low = jnp.bfloat16
+    vmem = pl.BlockSpec(memory_space=pltpu.VMEM)
+    dma = pltpu.SemaphoreType.DMA
+    f32 = jnp.float32
+    return pl.pallas_call(
+        visit_kernel,
+        out_shape=[
+            jax.ShapeDtypeStruct((tokens, 2 * D + 128), f32),
+            jax.ShapeDtypeStruct((experts, D // 4, hidden), f32),
+            jax.ShapeDtypeStruct((experts, hidden, D // 4), f32),
+        ],
+        in_specs=[vmem] * 4,
+        out_specs=[vmem] * 3,
+        scratch_shapes=[
+            pltpu.VMEM((8, tokens, D + 128), low),
+            pltpu.VMEM((4, tokens, D), low),
+            pltpu.VMEM((D, wide), low),
+            pltpu.VMEM((128, wide), low),
+            pltpu.VMEM((tokens, D), low),
+            pltpu.VMEM((tokens, wide), low),
+            pltpu.VMEM((tokens, wide), low),
+            pltpu.VMEM((wide, 8 * tokens), low),
+            pltpu.VMEM((wide, 8 * tokens), low),
+            pltpu.VMEM((2, 4, tokens, 2 * D + 128), low),
+            pltpu.VMEM((4, tokens, 2 * D + 128), low),
+            pltpu.VMEM((5, tokens, 2 * D + 128), low),
+            pltpu.VMEM((4, wide, D // 4), low),
+            pltpu.VMEM((4, wide, D // 4), low),
+            pltpu.VMEM((3, wide, D // 4), low),
+            pltpu.VMEM((3, wide, D // 4), low),
+            dma((3, 4)), dma((2, 4)), dma((4,)), dma((4,)), dma((4,)), dma((4,)), dma((4, 2)), dma((5, 2)), dma((2, 3)), dma((2, 3)),
+        ],
+        compiler_params=pltpu.CompilerParams(collective_id=2, has_side_effects=True, vmem_limit_bytes=58 * 2**20),
+        name="expert_visit",
+    )(sent, cot_line, up, down.reshape(wide, D))
+
+
+def attend_kernel(
+    expert_total, lengths, hidden, cot, value_pick, output_pick, expert_pick, routers, gains,
+    key_weight_at, value_weight_at, query_weight_at, output_weight_at,
+    middle, sent, normed_one, normed_two, queries, key_value, probs, value_all, attended,
+    gates, slopes, cot_line,
+    key_weight, value_weight, query_weight, output_weight, mixed, hot_turned, hot,
+    fetch, pair_send, pair_recv, cot_send, cot_recv, own_sem,
+):
+    dp, ex = lax.axis_index("dp"), lax.axis_index("expert")
+    z, core = ex // 2, ex % 2
+    half = z // 2
+    inner = z + half * (3 - 2 * z)
+    count = hidden.shape[0]
+    width = HEADS * HEAD_DIM
+    low = jnp.bfloat16
+    length = lengths[0]
+    spread = HEADS * VE
+    total = expert_total
+    weights = [
+        pltpu.make_async_copy(source, target, fetch.at[i])
+        for i, (source, target) in enumerate(
+            (
+                (key_weight_at, key_weight),
+                (value_weight_at, value_weight),
+                (query_weight_at, query_weight),
+                (output_weight_at, output_weight),
+            )
+        )
+    ]
+    for made in weights:
+        made.start()
+
+    def at_z(place):
+        return (dp, place * 2 + core)
+
+    barrier = pltpu.get_barrier_semaphore()
+    for k in (1, 2, 3):
+        pl.semaphore_signal(barrier, inc=1, device_id=((dp + k) % 4, ex), device_id_type=MESH)
+
+    @pl.when(z < 3)
+    def _():
+        pl.semaphore_signal(barrier, inc=1, device_id=at_z(z + 1), device_id_type=MESH)
+
+    @pl.when(z > 0)
+    def _():
+        pl.semaphore_signal(barrier, inc=1, device_id=at_z(z - 1), device_id_type=MESH)
+
+    pl.semaphore_wait(barrier, 4 + inner)
+
+    def cot_copy(way, at, source=None):
+        block = cot_line.at[at]
+        return pltpu.make_async_remote_copy(
+            src_ref=block if source is None else source, dst_ref=block,
+            send_sem=cot_send.at[way, at], recv_sem=cot_recv.at[at],
+            device_id=at_z(z + 1 - 2 * way), device_id_type=MESH,
+        )
+
+    def pass_on(distance):
+        @pl.when(z >= distance)
+        def _():
+            cot_copy(0, z - distance).wait_recv()
+
+        @pl.when((z >= distance) & (z < 3))
+        def _():
+            cot_copy(0, z - distance).start()
+
+        @pl.when(z + distance <= 3)
+        def _():
+            cot_copy(1, z + distance).wait_recv()
+
+        @pl.when((z + distance <= 3) & (z > 0))
+        def _():
+            cot_copy(1, z + distance).start()
+
+    @pl.when(z < 3)
+    def _():
+        cot_copy(0, z, cot).start()
+
+    @pl.when(z > 0)
+    def _():
+        cot_copy(1, z, cot).start()
+
+    keep = pltpu.make_async_copy(cot, cot_line.at[z], own_sem)
+    keep.start()
+
+    def norm(field, gain):
+        center = field - jnp.mean(field, axis=-1, keepdims=True)
+        spread = jnp.mean(center * center, axis=-1, keepdims=True)
+        return (center * lax.rsqrt(spread + EPSILON) * gain).astype(low)
+
+    parts = (pl.ds(0, width), pl.ds(width, width))
+
+    def pair_copy(step, part, block):
+        return pltpu.make_async_remote_copy(
+            src_ref=key_value.at[block, :, parts[part]], dst_ref=key_value.at[block, :, parts[part]],
+            send_sem=pair_send.at[step, part], recv_sem=pair_recv.at[block, part],
+            device_id=((dp + step) % 4, ex), device_id_type=MESH,
+        )
+
+    def send_part(part):
+        for step in (1, 2, 3):
+
+            @pl.when(dp + step < 4)
+            def _():
+                pair_copy(step, part, dp).start()
+
+    normed_one[...] = norm(hidden[...].astype(jnp.float32), gains[0:1, :])
+    weights[0].wait()
+    key_value[dp, :, parts[0]] = jnp.dot(
+        normed_one[...], key_weight[...], preferred_element_type=jnp.float32
+    ).astype(low)
+    send_part(0)
+
+    hot_turned[...] = jnp.zeros(hot_turned.shape, jnp.float32)
+
+    def mark(picks, base, size):
+        place = lax.broadcasted_iota(jnp.int32, (size, count), 0)
+        found = jnp.zeros((size, count), jnp.float32)
+        for pick in picks:
+            found = jnp.where(place == pick, 1.0, found)
+        hot_turned[base : base + size, :] = found
+
+    mark([value_pick[h, i : i + 1, :] + h * VE for h in range(HEADS) for i in range(value_pick.shape[1])], 0, spread)
+    mark(
+        [output_pick[h, i : i + 1, :] + h * VE for h in range(HEADS) for i in range(output_pick.shape[1])],
+        spread,
+        spread,
+    )
+    mark([expert_pick[i : i + 1, :] for i in range(expert_pick.shape[0])], 2 * spread, total)
+    hot[...] = hot_turned[...].T
+    sig = jax.nn.sigmoid(dot_last(normed_one[...], routers[...]))
+    gates[...] = sig * hot[...]
+    slopes[...] = gates[...] * (1.0 - sig)
+    weights[1].wait()
+
+    def values(n, carry):
+        span = pl.ds(pl.multiple_of(n * 256, 256), 256)
+        value_all[:, span] = jnp.dot(
+            hidden[...], value_weight[:, span], preferred_element_type=jnp.float32
+        ).astype(low)
+        return carry
+
+    lax.fori_loop(0, HEADS * VE * HEAD_DIM // 256, values, 0)
+    for h in range(HEADS):
+        row = jnp.zeros((count, HEAD_DIM), jnp.float32)
+        for e in range(h * VE, (h + 1) * VE):
+            row += gates[:, e : e + 1] * value_all[:, e * HEAD_DIM : (e + 1) * HEAD_DIM].astype(jnp.float32)
+        key_value[dp, :, width + h * HEAD_DIM : width + (h + 1) * HEAD_DIM] = row.astype(low)
+    send_part(1)
+
+    weights[2].wait()
+    queries[...] = jnp.dot(normed_one[...], query_weight[...], preferred_element_type=jnp.float32).astype(low)
+    for block in range(4):
+
+        @pl.when(block > dp)
+        def _():
+            key_value[block] = jnp.zeros((count, 2 * width), low)
+
+    pass_on(1)
+
+    def wait_part(part):
+        for block in range(3):
+
+            @pl.when(block < dp)
+            def _():
+                pair_copy(1, part, block).wait_recv()
+
+    wait_part(0)
+    pair_all = key_value.reshape(4 * count, 2 * width)
+    query_pos = dp * count + lax.broadcasted_iota(jnp.int32, (count, 4 * count), 0)
+    key_pos = lax.broadcasted_iota(jnp.int32, (count, 4 * count), 1)
+    allowed = (key_pos <= query_pos) & (key_pos < length)
+
+    def score(h, carry):
+        span = pl.ds(pl.multiple_of(h * HEAD_DIM, HEAD_DIM), HEAD_DIM)
+        raw = dot_last(queries[:, span], pair_all[:, span])
+        scores = jnp.where(allowed, raw * HEAD_DIM ** (-0.5), NEGATIVE)
+        terms = jnp.exp(scores - jnp.max(scores, axis=-1, keepdims=True))
+        probs[h] = (terms * (1.0 / jnp.sum(terms, axis=-1, keepdims=True))).astype(low)
+        return carry
+
+    lax.fori_loop(0, HEADS, score, 0)
+    wait_part(1)
+    pass_on(2)
+
+    def collect(h, carry):
+        span = pl.ds(pl.multiple_of(h * HEAD_DIM, HEAD_DIM), HEAD_DIM)
+        value_span = pl.ds(pl.multiple_of(width + h * HEAD_DIM, HEAD_DIM), HEAD_DIM)
+        attended[:, span] = jnp.dot(probs[h], pair_all[:, value_span], preferred_element_type=jnp.float32)
+        return carry
+
+    lax.fori_loop(0, HEADS, collect, 0)
+    for h in range(HEADS):
+        row = attended[:, h * HEAD_DIM : (h + 1) * HEAD_DIM]
+        for e in range(h * VE, (h + 1) * VE):
+            mixed[:, e * HEAD_DIM : (e + 1) * HEAD_DIM] = (gates[:, spread + e : spread + e + 1] * row).astype(low)
+
+    place = dp * count + lax.broadcasted_iota(jnp.int32, (count, 1), 0)
+    live = jnp.where(place < length, 1.0, 0.0)
+    weights[3].wait()
+
+    def outward(n, carry):
+        span = pl.ds(pl.multiple_of(n * 256, 256), 256)
+        branch = jnp.dot(mixed[...], output_weight[:, span], preferred_element_type=jnp.float32)
+        middle[:, span] = hidden[:, span].astype(jnp.float32) + live * branch
+        return carry
+
+    lax.fori_loop(0, D // 256, outward, 0)
+    sent[:, :D] = middle[...].astype(low)
+    normed_two[...] = norm(middle[...], gains[1:2, :])
+    sig = jax.nn.sigmoid(dot_last(normed_two[...], routers[...]))
+    gate = sig * hot[...] * live
+    sent[:, D:] = gate.astype(low)
+    lane = lax.broadcasted_iota(jnp.int32, (count, 128), 1)
+    slopes[...] = jnp.where(lane < 2 * spread, slopes[...], gate * (1.0 - sig))
+
+    pass_on(3)
+    keep.wait()
+    for part in range(2):
+        for step in (1, 2, 3):
+
+            @pl.when(dp + step < 4)
+            def _():
+                pair_copy(step, part, dp).wait_send()
+
+    for at in range(4):
+
+        @pl.when((at <= z) & (z < 3))
+        def _():
+            cot_copy(0, at).wait_send()
+
+        @pl.when((at >= z) & (z > 0))
+        def _():
+            cot_copy(1, at).wait_send()
+
+
+def attend(total, lengths, *operands):
+    count = operands[0].shape[0]
+    low, full = jnp.bfloat16, jnp.float32
+    vmem = pl.BlockSpec(memory_space=pltpu.VMEM)
+    anywhere = pl.BlockSpec(memory_space=pl.ANY)
+    dma = pltpu.SemaphoreType.DMA
+    width, wide = HEADS * HEAD_DIM, HEADS * VE * HEAD_DIM
+    shapes = [
+        ((count, D), full),
+        ((count, D + 128), low),
+        ((count, D), low),
+        ((count, D), low),
+        ((count, width), low),
+        ((4, count, 2 * width), low),
+        ((HEADS, count, 4 * count), low),
+        ((count, wide), low),
+        ((count, width), full),
+        ((count, 128), full),
+        ((count, 128), full),
+        ((4, count, D), low),
+    ]
+    return pl.pallas_call(
+        functools.partial(attend_kernel, total),
+        out_shape=[jax.ShapeDtypeStruct(*shape) for shape in shapes],
+        in_specs=[pl.BlockSpec(memory_space=pltpu.SMEM)] + [vmem] * (len(operands) - 4) + [anywhere] * 4,
+        out_specs=[vmem] * len(shapes),
+        scratch_shapes=[pltpu.VMEM(a.shape, a.dtype) for a in operands[-4:]]
+        + [
+            pltpu.VMEM((count, wide), low),
+            pltpu.VMEM((128, count), full),
+            pltpu.VMEM((count, 128), full),
+            dma((4,)),
+            dma((4, 2)),
+            dma((4, 2)),
+            dma((2, 4)),
+            dma((4,)),
+            dma,
+        ],
+        compiler_params=pltpu.CompilerParams(
+            collective_id=1, has_side_effects=True, vmem_limit_bytes=58 * 2**20
+        ),
+        name="attend",
+    )(lengths, *operands)
+
+
+def backward_kernel(
+    total_experts, lengths, gates, slopes, routers, gains,
+    returned_at, middle_at, cot_at, hidden_at, normed_one_at, queries_at, key_value_at, probs_at, value_all_at,
+    attended_at, normed_two_at, query_weight_at, key_weight_at, value_weight_at, output_weight_at,
+    block_out, grad_in, out_query, out_key, out_value, out_output, out_small, sums_out,
+    returned, middle, cot, hidden, normed_one, queries, key_value, probs, value_all,
+    attended, normed_two, query_weight, key_weight, value_part, output_part,
+    branch, branch_turned, one_turned, hidden_turned, grad_att, grad_query, leave, arrive, grad_key, grad_value,
+    grad_each, grad_middle, grad_one, logit_one, logit_two, small_turned, mixed,
+    grads, grads_small, core_in, plane_in, last_in, sums_in,
+    fetch, part_fetch, leave_send, leave_recv, send, recv,
+):
+    dp, ex = lax.axis_index("dp"), lax.axis_index("expert")
+    y, x, z, core = dp // 2, dp % 2, ex // 2, ex % 2
+    count = hidden.shape[0]
+    width = HEADS * HEAD_DIM
+    low, full = jnp.bfloat16, jnp.float32
+    length = lengths[0]
+    sibling = (dp, z * 2 + 1 - core)
+    beside = (y * 2 + 1 - x, ex)
+    behind = ((1 - y) * 2 + x, ex)
+    across = ((1 - y) * 2 + 1 - x, ex)
+    line = [(dp, ((z + k) % 4) * 2 + core) for k in (1, 2, 3)]
+    barrier = pltpu.get_barrier_semaphore()
+    for place in (sibling, beside, behind, across, *line):
+        pl.semaphore_signal(barrier, inc=1, device_id=place, device_id_type=MESH)
+
+    held = dict(
+        returned=(returned_at, returned),
+        middle=(middle_at, middle),
+        cot=(cot_at, cot),
+        hidden=(hidden_at, hidden),
+        attended=(attended_at, attended),
+        key_value=(key_value_at, key_value),
+        probs=(probs_at, probs),
+        queries=(queries_at, queries),
+        normed_one=(normed_one_at, normed_one),
+        query_weight=(query_weight_at, query_weight),
+        value_all=(value_all_at, value_all),
+        key_weight=(key_weight_at, key_weight),
+        normed_two=(normed_two_at, normed_two),
+    )
+    got = {
+        name: pltpu.make_async_copy(source, target, fetch.at[i])
+        for i, (name, (source, target)) in enumerate(held.items())
+    }
+
+    def output_copy(n):
+        return pltpu.make_async_copy(
+            output_weight_at.at[pl.ds(n * 512, 512)], output_part.at[n % 2], part_fetch.at[0, n % 2]
+        )
+
+    def value_copy(n):
+        return pltpu.make_async_copy(
+            value_weight_at.at[:, pl.ds(n * 512, 512)], value_part.at[n % 2], part_fetch.at[1, n % 2]
+        )
+
+    first_held = ("returned", "middle", "cot", "hidden")
+    for name in first_held:
+        got[name].start()
+    for n in range(2):
+        output_copy(n).start()
+    for name in held:
+        if name not in first_held:
+            got[name].start()
+    for n in range(2):
+        value_copy(n).start()
+
+    pieces = (
+        [(out_output, 512 * n, 512, n) for n in range(5)]
+        + [(out_query, 0, 512, 5), (out_key, 0, 512, 6)]
+        + [(out_value, 512 * n, 512, n) for n in range(5)]
+        + [(out_small, 0, 128, None)]
+    )
+    along_line = (0, 1, 2, 3)
+    in_plane = [i for i in range(len(pieces)) if i not in along_line]
+    x_first = {i: n % 2 == 0 for n, i in enumerate(in_plane)}
+
+    def remote(source, target, slot, place):
+        return pltpu.make_async_remote_copy(
+            src_ref=source, dst_ref=target, send_sem=send.at[slot], recv_sem=recv.at[slot],
+            device_id=place, device_id_type=MESH,
+        )
+
+    def add(target, source):
+        target[...] = (target[...].astype(full) + source[...].astype(full)).astype(target.dtype)
+
+    def own(i):
+        slot = pieces[i][3]
+        return grads_small if slot is None else grads.at[slot]
+
+    def columns(i):
+        return pl.ds(0, pieces[i][2])
+
+    started = {}
+
+    def begin(key, source, target, slot, place):
+        started[key] = remote(source, target, slot, place)
+        started[key].start()
+
+    def halve_core(i):
+        begin((i, 0), own(i).at[:, :, 1 - core], core_in.at[i, :, :, :, columns(i)], (i, 0), sibling)
+
+    def halve_near(i):
+        span = columns(i)
+        started[i, 0].wait()
+        add(core_in.at[i, :, :, :, span], own(i).at[:, :, core])
+        if i in along_line:
+            for k in (1, 2, 3):
+                begin(
+                    (i, k), core_in.at[i, :, (z + k) % 4, :, span],
+                    plane_in.at[i, pl.ds(4 * k - 4, 4), :, span], (i, k), line[k - 1],
+                )
+            return
+        for part in range(2):
+            if x_first[i]:
+                source = core_in.at[i, part * 2 + 1 - x, :, :, span]
+            else:
+                source = core_in.at[i, (1 - y) * 2 + part, :, :, span]
+            target = plane_in.at[i, pl.ds(part * 4, 4), :, span]
+            begin((i, 1 + part), source, target, (i, 1 + part), beside if x_first[i] else behind)
+
+    def halve_far(i):
+        span = columns(i)
+        if i in along_line:
+            held = core_in.at[i, :, z, :, span]
+            for k in (1, 2, 3):
+                started[i, k].wait()
+                add(held, plane_in.at[i, pl.ds(4 * k - 4, 4), :, span])
+            for part in range(2):
+                begin(
+                    (i, 4 + part), core_in.at[i, part * 2 + 1 - x, z, :, span],
+                    last_in.at[i, part, :, span], (i, 4 + part), beside,
+                )
+            return
+        for part in range(2):
+            started[i, 1 + part].wait()
+            kept = part * 2 + x if x_first[i] else y * 2 + part
+            add(plane_in.at[i, pl.ds(part * 4, 4), :, span], core_in.at[i, kept, :, :, span])
+        other = 1 - y if x_first[i] else 1 - x
+        begin(
+            (i, 3), plane_in.at[i, pl.ds(other * 4, 4), :, span], plane_in.at[i, pl.ds(8, 4), :, span],
+            (i, 3), behind if x_first[i] else beside,
+        )
+
+    def spread(i):
+        span = columns(i)
+        if i in along_line:
+            for part in range(2):
+                started[i, 4 + part].wait()
+                add(last_in.at[i, part, :, span], core_in.at[i, part * 2 + x, z, :, span])
+            begin((i, 6), last_in.at[i, 1 - y, :, span], last_in.at[i, 2, :, span], (i, 6), behind)
+            return
+        started[i, 3].wait()
+        add(plane_in.at[i, pl.ds(8, 4), :, span], plane_in.at[i, pl.ds((y if x_first[i] else x) * 4, 4), :, span])
+        for k in (1, 2, 3):
+            begin(
+                (i, 3 + k), plane_in.at[i, 8 + (z + k) % 4, :, span],
+                last_in.at[i, k - 1, :, span], (i, 3 + k), line[k - 1],
+            )
+
+    def finish(i):
+        out, start, size, _ = pieces[i]
+        span = columns(i)
+        if i in along_line:
+            started[i, 6].wait()
+            total = last_in[i, y, :, span].astype(full) + last_in[i, 2, :, span].astype(full)
+        else:
+            total = plane_in[i, 8 + z, :, span].astype(full)
+            for k in (1, 2, 3):
+                started[i, 3 + k].wait()
+                total = total + last_in[i, k - 1, :, span].astype(full)
+        out[:, pl.ds(start, size)] = total
+
+    rows_each = 64
+    lane = lax.broadcasted_iota(jnp.int32, (1, 128), 1)
+    for name in first_held:
+        got[name].wait()
+    logit_two[...] = (returned[:, 2 * D :] * slopes[...]).astype(low)
+
+    def live_rows(start):
+        place = dp * count + start + lax.broadcasted_iota(jnp.int32, (rows_each, 1), 0)
+        return jnp.where(place < length, 1.0, 0.0)
+
+    def norm_back(field, grad, gain):
+        center = field - jnp.mean(field, axis=-1, keepdims=True)
+        scale = lax.rsqrt(jnp.mean(center * center, axis=-1, keepdims=True) + EPSILON)
+        unit = center * scale
+        part = grad * gain
+        back = scale * (
+            part
+            - jnp.mean(part, axis=-1, keepdims=True)
+            - unit * jnp.mean(part * unit, axis=-1, keepdims=True)
+        )
+        return back, jnp.sum(grad * unit, axis=0, keepdims=True)
+
+    def square(field, live, at):
+        total = jnp.sum(jnp.sum(field * field, axis=1, keepdims=True) * live, axis=0, keepdims=True)
+        return jnp.where(lane == at, total, 0.0)
+
+    def first_rows(n, carry):
+        gain_sum, sums = carry
+        start = pl.multiple_of(n * rows_each, rows_each)
+        rows = pl.ds(start, rows_each)
+        live = live_rows(start)
+        field = middle[rows, :]
+        forward = returned[rows, :D]
+        final = field + forward
+        block_out[rows, :] = final.astype(low)
+        source = hidden[rows, :].astype(full)
+        one = jnp.ones((rows_each, 1), full)
+        sums += square(source, live, 0) + square(field - source, one, 1)
+        sums += square(forward, one, 2) + square(final, live, 3)
+        sums += jnp.where(lane == 4, jnp.sum(live, axis=0, keepdims=True), 0.0)
+        grad = jnp.dot(logit_two[rows, :], routers[...], preferred_element_type=full)
+        back, gain_part = norm_back(field, grad, gains[1:2, :])
+        total = cot[rows, :].astype(full) + returned[rows, D : 2 * D] + back
+        grad_middle[rows, :] = total
+        branch[rows, :] = (live * total).astype(low)
+        return gain_sum + gain_part, sums
+
+    gain_two_sum, sums = lax.fori_loop(
+        0, count // rows_each, first_rows, (jnp.zeros((1, D), full), jnp.zeros((1, 128), full))
+    )
+    sums_in[0] = jnp.broadcast_to(sums, (8, 128))
+    pl.semaphore_wait(barrier, 7)
+
+    def weight_grad(i, turned, right, size):
+        flat = own(i)
+        flat = flat.reshape(D, size)
+
+        def some(n, carry):
+            rows = pl.ds(pl.multiple_of(n * 256, 256), 256)
+            flat[rows, :] = jnp.dot(turned[rows, :], right, preferred_element_type=full).astype(low)
+            return carry
+
+        lax.fori_loop(0, D // 256, some, 0)
+        halve_core(i)
+
+    branch_turned[...] = branch[...].T
+    got["attended"].wait()
+
+    def head_of(c):
+        return slice((c // VE) * HEAD_DIM, (c // VE + 1) * HEAD_DIM)
+
+    spread_count = HEADS * VE
+    for n in range(5):
+        for j in range(4):
+            c = 4 * n + j
+            gate = gates[:, spread_count + c : spread_count + c + 1]
+            mixed[:, j * HEAD_DIM : (j + 1) * HEAD_DIM] = (gate * attended[:, head_of(c)]).astype(low)
+        weight_grad(n, branch_turned, mixed[...], 512)
+    logit_one[...] = jnp.zeros(logit_one.shape, full)
+    grad_att[...] = jnp.zeros(grad_att.shape, full)
+    for n in range(5):
+        output_copy(n).wait()
+        for j in range(4):
+            c = 4 * n + j
+            grad_mixed = dot_last(branch[...], output_part[n % 2, j * HEAD_DIM : (j + 1) * HEAD_DIM, :])
+            col = spread_count + c
+            grad_att[:, head_of(c)] += gates[:, col : col + 1] * grad_mixed
+            dots = jnp.sum(attended[:, head_of(c)] * grad_mixed, axis=1, keepdims=True)
+            logit_one[:, col : col + 1] = dots * slopes[:, col : col + 1]
+        if n + 2 < 5:
+            output_copy(n + 2).start()
+        halve_near(n)
+
+    pair_all = key_value.reshape(4 * count, 2 * width)
+    for name in ("key_value", "probs", "queries"):
+        got[name].wait()
+
+    def leave_copy(k, h):
+        rows = pl.ds(h * 2 * HEAD_DIM, 2 * HEAD_DIM)
+        return pltpu.make_async_remote_copy(
+            src_ref=leave.at[(dp + 4 - k) % 4, rows], dst_ref=arrive.at[k - 1, rows],
+            send_sem=leave_send.at[k - 1, h], recv_sem=leave_recv.at[k - 1, h],
+            device_id=((dp + 4 - k) % 4, ex), device_id_type=MESH,
+        )
+
+    def head(h, carry):
+        start = pl.multiple_of(h * HEAD_DIM, HEAD_DIM)
+        span = pl.ds(start, HEAD_DIM)
+        grad = grad_att[:, span].astype(low)
+        prob = probs[h].astype(full)
+        grad_prob = dot_last(grad, pair_all[:, pl.ds(width + start, HEAD_DIM)])
+        dots = jnp.sum(prob * grad_prob, axis=-1, keepdims=True)
+        grad_score = (prob * (grad_prob - dots) * HEAD_DIM ** (-0.5)).astype(low)
+        grad_query[:, span] = jnp.dot(grad_score, pair_all[:, span], preferred_element_type=full).astype(low)
+        key_part = dot_first(queries[:, span], grad_score).astype(low)
+        value_part_all = dot_first(grad, probs[h]).astype(low)
+        key_rows = pl.ds(pl.multiple_of(2 * h * HEAD_DIM, 2 * HEAD_DIM), HEAD_DIM)
+        value_rows = pl.ds(pl.multiple_of((2 * h + 1) * HEAD_DIM, HEAD_DIM), HEAD_DIM)
+        for j in range(4):
+            leave[j, key_rows, :] = key_part[:, j * count : (j + 1) * count]
+            leave[j, value_rows, :] = value_part_all[:, j * count : (j + 1) * count]
+        for k in (1, 2, 3):
+
+            @pl.when(dp >= k)
+            def _():
+                leave_copy(k, h).start()
+
+        return carry
+
+    lax.fori_loop(0, HEADS, head, 0)
+
+    for name in ("normed_one", "query_weight"):
+        got[name].wait()
+    one_turned[...] = normed_one[...].T
+    weight_grad(5, one_turned, grad_query[...], 512)
+    hidden_turned[...] = hidden[...].T
+    grad_one[...] = dot_last(grad_query[...], query_weight[...])
+    halve_near(5)
+
+    for h in range(HEADS):
+        rows = pl.ds(h * 2 * HEAD_DIM, 2 * HEAD_DIM)
+        total = leave[dp, rows, :].astype(full)
+        for k in (1, 2, 3):
+
+            @pl.when(dp + k < 4)
+            def _():
+                leave_copy(k, h).wait_recv()
+
+            @pl.when(dp + k >= 4)
+            def _():
+                arrive[k - 1, rows, :] = jnp.zeros((2 * HEAD_DIM, count), low)
+
+            total += arrive[k - 1, rows, :].astype(full)
+        turned = total.T
+        grad_key[:, h * HEAD_DIM : (h + 1) * HEAD_DIM] = turned[:, :HEAD_DIM].astype(low)
+        grad_value[:, h * HEAD_DIM : (h + 1) * HEAD_DIM] = turned[:, HEAD_DIM:].astype(low)
+
+    got["value_all"].wait()
+    for n in range(5):
+        for j in range(4):
+            c = 4 * n + j
+            grad = grad_value[:, head_of(c)].astype(full)
+            here = slice(c * HEAD_DIM, (c + 1) * HEAD_DIM)
+            grad_each[:, here] = (gates[:, c : c + 1] * grad).astype(low)
+            dots = jnp.sum(value_all[:, here].astype(full) * grad, axis=1, keepdims=True)
+            logit_one[:, c : c + 1] = dots * slopes[:, c : c + 1]
+        weight_grad(7 + n, hidden_turned, grad_each[:, n * 512 : (n + 1) * 512], 512)
+        if n:
+            halve_near(6 + n)
+    weight_grad(6, one_turned, grad_key[...], 512)
+    halve_near(11)
+    got["key_weight"].wait()
+    grad_one[...] += dot_last(grad_key[...], key_weight[...])
+    halve_near(6)
+    grad_one[...] += jnp.dot(logit_one[...].astype(low), routers[...], preferred_element_type=full)
+    halve_far(5)
+
+    def first_norm(n, gain_sum):
+        rows = pl.ds(pl.multiple_of(n * rows_each, rows_each), rows_each)
+        back, gain_part = norm_back(hidden[rows, :].astype(full), grad_one[rows, :], gains[0:1, :])
+        grad_in[rows, :] = grad_middle[rows, :] + back
+        return gain_sum + gain_part
+
+    gain_one_sum = lax.fori_loop(0, count // rows_each, first_norm, jnp.zeros((1, D), full))
+    halve_far(7)
+    spread(5)
+    got["normed_two"].wait()
+    small_turned[...] = dot_first(logit_one[...].astype(low), normed_one[...]) + dot_first(
+        logit_two[...], normed_two[...]
+    )
+    small_rows = 2 * spread_count + total_experts
+    small_turned[small_rows : small_rows + 1, :] = gain_one_sum
+    small_turned[small_rows + 1 : small_rows + 2, :] = gain_two_sum
+    grads_small.reshape(D, 128)[...] = small_turned[...].T.astype(low)
+    halve_core(12)
+
+    rounds = [[sibling], [beside], [behind], line]
+    offset = [1, 2, 3, 4]
+
+    def sum_start(r):
+        for j, place in enumerate(rounds[r]):
+            begin(("sum", r, j), sums_in.at[0], sums_in.at[offset[r] + j], (len(pieces) + j, r), place)
+
+    def sum_end(r):
+        for j in range(len(rounds[r])):
+            started["sum", r, j].wait()
+        total = sums_in[0]
+        for j in range(len(rounds[r])):
+            total = total + sums_in[offset[r] + j]
+        sums_in[0] = total
+
+    sum_start(0)
+    for n in range(5):
+        value_copy(n).wait()
+        part = dot_last(grad_each[:, n * 512 : (n + 1) * 512], value_part[n % 2])
+        grad_in[...] += part
+        if n + 2 < 5:
+            value_copy(n + 2).start()
+        if n == 0:
+            halve_near(12)
+            sum_end(0)
+            sum_start(1)
+        if n == 1:
+            halve_far(8)
+            spread(7)
+        if n == 2:
+            finish(5)
+            halve_far(9)
+            spread(8)
+            sum_end(1)
+            sum_start(2)
+        if n == 3:
+            halve_far(0)
+            finish(7)
+        if n == 4:
+            sum_end(2)
+            sum_start(3)
+            halve_far(10)
+            spread(9)
+
+    for action, i in (
+        (halve_far, 1), (spread, 0), (finish, 8), (halve_far, 4), (halve_far, 11), (spread, 10), (finish, 0), (finish, 9),
+        (sum_end, 3),
+        (halve_far, 2), (spread, 1), (spread, 4), (halve_far, 6), (spread, 11), (finish, 10), (finish, 1),
+        (halve_far, 12), (spread, 2), (spread, 6), (finish, 4), (finish, 11), (halve_far, 3), (spread, 12), (finish, 2),
+        (finish, 6), (spread, 3), (finish, 12), (finish, 3),
+    ):
+        action(i)
+    sums_out[...] = sums_in[0]
+    for h in range(HEADS):
+        for k in (1, 2, 3):
+
+            @pl.when(dp >= k)
+            def _():
+                leave_copy(k, h).wait_send()
+
+
+def backward(total_experts, lengths, gates, slopes, routers, gains, *arrays):
+    low, full = jnp.bfloat16, jnp.float32
+    count = gates.shape[0]
+    width, wide = HEADS * HEAD_DIM, HEADS * VE * HEAD_DIM
+    vmem = pl.BlockSpec(memory_space=pltpu.VMEM)
+    anywhere = pl.BlockSpec(memory_space=pl.ANY)
+    dma = pltpu.SemaphoreType.DMA
+    whole = [pltpu.VMEM(a.shape, a.dtype) for a in arrays[:13]]
+    n = 13
+    return pl.pallas_call(
+        functools.partial(backward_kernel, total_experts),
+        out_shape=[
+            jax.ShapeDtypeStruct((count, D), low),
+            jax.ShapeDtypeStruct((count, D), full),
+            jax.ShapeDtypeStruct((ROWS, width), full),
+            jax.ShapeDtypeStruct((ROWS, width), full),
+            jax.ShapeDtypeStruct((ROWS, wide), full),
+            jax.ShapeDtypeStruct((ROWS, wide), full),
+            jax.ShapeDtypeStruct((ROWS, 128), full),
+            jax.ShapeDtypeStruct((8, 128), full),
+        ],
+        in_specs=[pl.BlockSpec(memory_space=pltpu.SMEM)] + [vmem] * 4 + [anywhere] * len(arrays),
+        out_specs=[vmem] * 8,
+        scratch_shapes=whole
+        + [
+            pltpu.VMEM((2, D, 512), low),
+            pltpu.VMEM((2, 512, D), low),
+            pltpu.VMEM((count, D), low),
+            pltpu.VMEM((D, count), low),
+            pltpu.VMEM((D, count), low),
+            pltpu.VMEM((D, count), low),
+            pltpu.VMEM((count, width), full),
+            pltpu.VMEM((count, width), low),
+            pltpu.VMEM((4, 2 * width, count), low),
+            pltpu.VMEM((3, 2 * width, count), low),
+            pltpu.VMEM((count, width), low),
+            pltpu.VMEM((count, width), low),
+            pltpu.VMEM((count, wide), low),
+            pltpu.VMEM((count, D), full),
+            pltpu.VMEM((count, D), full),
+            pltpu.VMEM((count, 128), full),
+            pltpu.VMEM((count, 128), low),
+            pltpu.VMEM((128, D), full),
+            pltpu.VMEM((count, 512), low),
+            pltpu.VMEM((7, 4, 4, 2, ROWS, 512), low),
+            pltpu.VMEM((4, 4, 2, ROWS, 128), low),
+            pltpu.VMEM((n, 4, 4, ROWS, 512), low),
+            pltpu.VMEM((n, 12, ROWS, 512), low),
+            pltpu.VMEM((n, 3, ROWS, 512), low),
+            pltpu.VMEM((7, 8, 128), full),
+            dma((13,)),
+            dma((2, 2)),
+            dma((3, HEADS)),
+            dma((3, HEADS)),
+            dma((n + 3, 7)),
+            dma((n + 3, 7)),
+        ],
+        compiler_params=pltpu.CompilerParams(
+            collective_id=3, has_side_effects=True, vmem_limit_bytes=62 * 2**20
+        ),
+        name="backward",
+    )(lengths, gates, slopes, routers, gains, *arrays)
+
+
+def expert_visit(sent, cotangent, expert_up, expert_down):
+    local_experts = expert_up.shape[0]
+    group = lax.axis_index("expert")
+    cot_all = lax.all_gather(cotangent, "expert", axis=0, tiled=True)
+    sent_all = lax.all_gather(sent, "expert", axis=0, tiled=True)
+    rows_all = sent_all[:, :D]
+    total_experts = sent.shape[1] - D
+    gate_all = lax.dynamic_slice_in_dim(
+        sent_all[:, D:], group * local_experts, local_experts, 1
+    ).astype(jnp.float32).T[:, :, None]
+    preact = jnp.einsum("td,xdf->xtf", rows_all, expert_up, preferred_element_type=jnp.float32)
+    pre_sig = jax.nn.sigmoid(preact)
+    hidden = preact * pre_sig
+    back = jnp.einsum("td,xfd->xtf", cot_all, expert_down, preferred_element_type=jnp.float32)
+    gate_grad = jnp.sum(hidden * back, axis=2).T
+    gated = (gate_all * hidden).astype(jnp.bfloat16)
+    grad_pre = (gate_all * back * (pre_sig * (1.0 + preact * (1.0 - pre_sig)))).astype(jnp.bfloat16)
+    partial_out = jnp.einsum("xtf,xfd->td", gated, expert_down, preferred_element_type=jnp.float32)
+    partial_grad = jnp.einsum("xtf,xdf->td", grad_pre, expert_up, preferred_element_type=jnp.float32)
+    wide_grad = lax.dynamic_update_slice_in_dim(
+        jnp.zeros((gate_grad.shape[0], total_experts), jnp.bfloat16),
+        gate_grad.astype(jnp.bfloat16),
+        group * local_experts,
+        1,
+    )
+    returned = lax.psum_scatter(
+        jnp.concatenate(
+            [partial_out.astype(jnp.bfloat16), partial_grad.astype(jnp.bfloat16), wide_grad], axis=1
+        ),
+        "expert",
+        scatter_dimension=0,
+        tiled=True,
+    )
+    grad_down = jnp.einsum("xtf,td->xfd", gated, cot_all, preferred_element_type=jnp.float32)
+    grad_up = jnp.einsum("td,xtf->xdf", rows_all, grad_pre, preferred_element_type=jnp.float32)
+    return returned, grad_up, grad_down
+
+
+def dot_last(left_side, right_side):
+    return lax.dot_general(
+        left_side, right_side, (((1,), (1,)), ((), ())), preferred_element_type=jnp.float32
+    )
+
+def visit_kernel(
+    sent, cot, up, down, back_out, up_out, down_out,
+    rows, cot_other, up_wide, chosen, cots, gated, grad_pre, gated_turned, pre_turned, partial, paired_in, chain_in, up_low, down_low, up_in, down_in,
+    row_send, row_recv, cot_send, cot_recv, pair_send, pair_recv, chain_send, chain_recv, grad_send, grad_recv,
+):
+    experts = up.shape[0]
+    wide = down.shape[0]
+    hidden = wide // experts
+    dp, ex = lax.axis_index("dp"), lax.axis_index("expert")
+    y, x, z, core = dp // 2, dp % 2, ex // 2, ex % 2
+    half = z // 2
+    inner = z + half * (3 - 2 * z)
+    onward = 1 - 2 * half
+    sibling = (dp, z * 2 + 1 - core)
+    beside, behind = (y * 2 + 1 - x, ex), ((1 - y) * 2 + x, ex)
+
+    def at_z(place):
+        return (dp, place * 2 + core)
+
+    barrier = pltpu.get_barrier_semaphore()
+    for place in (sibling, beside, behind):
+        pl.semaphore_signal(barrier, inc=1, device_id=place, device_id_type=MESH)
+
+    @pl.when(z < 3)
+    def _():
+        pl.semaphore_signal(barrier, inc=1, device_id=at_z(z + 1), device_id_type=MESH)
+
+    @pl.when(z > 0)
+    def _():
+        pl.semaphore_signal(barrier, inc=1, device_id=at_z(z - 1), device_id_type=MESH)
+
+    pl.semaphore_wait(barrier, 4 + inner)
+
+    def remote(source, target, send, recv, place):
+        return pltpu.make_async_remote_copy(
+            src_ref=source, dst_ref=target, send_sem=send, recv_sem=recv, device_id=place, device_id_type=MESH
+        )
+
+    def row_copy(way, at, source=None):
+        place = (sibling, at_z(z + 1), at_z(z - 1))[way]
+        block = rows.at[at]
+        target = block if way else rows.at[4 + at]
+        return remote(block if source is None else source, target, row_send.at[way, at], row_recv.at[0 if way else 1, at], place)
+
+    def cot_copy(at):
+        return remote(cot.at[at], cot_other.at[at], cot_send.at[at], cot_recv.at[at], sibling)
+
+    own = row_copy(0, z, sent), row_copy(1, z, sent), row_copy(2, z, sent)
+
+    @pl.when(z < 3)
+    def _():
+        own[1].start()
+
+    @pl.when(z > 0)
+    def _():
+        own[2].start()
+
+    own[0].start()
+    cot_copy(z).start()
+    for k in (1, 2, 3):
+        cot_copy((z + k) % 4).start()
+    rows[z] = sent[...]
+    for e in range(experts):
+        up_wide[:, e * hidden : (e + 1) * hidden] = up[e]
+    chosen[...] = (
+        lax.broadcasted_iota(jnp.int32, (128, wide), 0)
+        == 2 * HEADS * VE + ex * experts + lax.broadcasted_iota(jnp.int32, (128, wide), 1) // hidden
+    ).astype(jnp.float32).astype(jnp.bfloat16)
+
+    def order(p):
+        later = (p + 2) // 3
+        step = p - inner // (p + 1 - later)
+        return later * (step + half * (3 - 2 * step)) + (1 - later) * z
+
+    def pair_copy(at):
+        return remote(partial.at[1, at], paired_in.at[at], pair_send.at[at], pair_recv.at[at], sibling)
+
+    spans = (pl.ds(0, D), pl.ds(D, D + 128))
+
+    def chain_copy(dest, slot, to, stage, part):
+        span = spans[part]
+        return remote(
+            partial.at[0, dest, :, span], chain_in.at[slot, :, span],
+            chain_send.at[stage, part], chain_recv.at[slot, part], at_z(to),
+        )
+
+    def add(target, source):
+        def some(i, carry):
+            part = pl.ds(pl.multiple_of(i * 32, 32), 32)
+            target[part, :] = (
+                target[part, :].astype(jnp.float32) + source[part, :].astype(jnp.float32)
+            ).astype(target.dtype)
+            return carry
+
+        lax.fori_loop(0, target.shape[0] // 32, some, 0)
+
+    def visit(q, carry):
+        p, other = q // 2, q % 2
+        at = order(p)
+        block = other * 4 + at
+
+        @pl.when((other == 0) & (p > 0))
+        def _():
+            row_copy(1, at).wait_recv()
+            row_copy(0, at).start()
+
+            @pl.when((at < z) & (z < 3))
+            def _():
+                row_copy(1, at).start()
+
+            @pl.when((at > z) & (z > 0))
+            def _():
+                row_copy(2, at).start()
+
+        @pl.when(other == 1)
+        def _():
+            row_copy(0, at).wait_recv()
+            cot_copy(at).wait_recv()
+            cots[...] = cot_other[at]
+
+        @pl.when(other == 0)
+        def _():
+            cots[...] = cot[at]
+
+        count = rows.shape[1]
+        places = pl.ds(pl.multiple_of(block * count, count), count)
+
+        def columns(n, gate_grad):
+            span = pl.ds(pl.multiple_of(n * 256, 256), 256)
+            pre = jnp.dot(rows[block, :, :D], up_wide[:, span], preferred_element_type=jnp.float32)
+            back = dot_last(cots[...], down[span, :])
+            mark = chosen[:, span]
+            gate = jnp.dot(rows[block, :, D:], mark, preferred_element_type=jnp.float32)
+            sig = jax.nn.sigmoid(pre)
+            act = pre * sig
+            act_low = (gate * act).astype(jnp.bfloat16)
+            pre_low = (gate * back * (sig * (1.0 + pre * (1.0 - sig)))).astype(jnp.bfloat16)
+            gated[:, span] = act_low
+            grad_pre[:, span] = pre_low
+            gated_turned[span, places] = act_low.T
+            pre_turned[span, places] = pre_low.T
+            return gate_grad + dot_last((act * back).astype(jnp.bfloat16), mark)
+
+        partial[other, at, :, 2 * D :] = lax.fori_loop(
+            0, wide // 256, columns, jnp.zeros((count, 128), jnp.float32)
+        ).astype(jnp.bfloat16)
+
+        def outward(n, carry):
+            span = pl.ds(pl.multiple_of(n * 256, 256), 256)
+            partial[other, at, :, span] = jnp.dot(
+                gated[...], down[:, span], preferred_element_type=jnp.float32
+            ).astype(jnp.bfloat16)
+            partial[other, at, :, pl.ds(pl.multiple_of(D + n * 256, 256), 256)] = dot_last(
+                grad_pre[...], up_wide[span, :]
+            ).astype(jnp.bfloat16)
+            return carry
+
+        lax.fori_loop(0, D // 256, outward, 0)
+
+        @pl.when(other == 1)
+        def _():
+            pair_copy(at).start()
+            pair_copy(at).wait_recv()
+            add(partial.at[0, at], paired_in.at[at])
+
+        @pl.when((inner == 0) & (q == 3))
+        def _():
+            chain_copy(*nearest, 0).start()
+
+        @pl.when((inner == 0) & (q == 5))
+        def _():
+            chain_copy(*next_one, 0).start()
+
+        return carry
+
+    nearest = (z + onward, z + onward, z + onward, 0)
+    farthest = (3 * (1 - half), 3 * (1 - half), z + onward, 1)
+    backward = (3 * half, 3 * half, z - onward, 2)
+    next_one = (2 - half, 2 - half + inner * (2 + half), z + onward, 3)
+    lax.fori_loop(0, 8, visit, 0)
+
+    def relay(dest, slot, to, stage, part):
+        chain_copy(dest, dest, to, stage, part).wait_recv()
+        add(partial.at[0, dest, :, spans[part]], chain_in.at[dest, :, spans[part]])
+        chain_copy(dest, slot, to, stage, part).start()
+
+    @pl.when(inner == 0)
+    def _():
+        chain_copy(*farthest, 0).start()
+        chain_copy(*farthest, 1).start()
+        chain_copy(*next_one, 1).start()
+        chain_copy(*nearest, 1).start()
+
+    @pl.when(inner == 1)
+    def _():
+        relay(*next_one, 0)
+
+    tokens_all = rows.reshape(rows.shape[0] * rows.shape[1], rows.shape[2])
+    cots_own = cot.reshape(cot.shape[0] * cot.shape[1], D)
+    cots_other = cot_other.reshape(cot.shape[0] * cot.shape[1], D)
+    place = cots_own.shape[0]
+    quarter = D // 4
+
+
+    def up_copy(j):
+        return remote(up_low.at[j], up_in.at[j], grad_send.at[0, j], grad_recv.at[0, j], behind if j == 2 else beside)
+
+    def down_copy(j):
+        return remote(down_low.at[j], down_in.at[j], grad_send.at[1, j], grad_recv.at[1, j], beside if j == 1 else behind)
+
+    def weight_grads(j, carry):
+        across, aside = 1 - j % 2, 1 - j // 2
+        at = (y + across * (1 - 2 * y)) * 2 + x + aside * (1 - 2 * x)
+        span = pl.ds(pl.multiple_of(at * quarter, quarter), quarter)
+        up_low[j] = jnp.dot(
+            pre_turned[...], tokens_all[:, span], preferred_element_type=jnp.float32
+        ).astype(jnp.bfloat16)
+        down_low[j] = (
+            jnp.dot(gated_turned[:, :place], cots_own[:, span], preferred_element_type=jnp.float32)
+            + jnp.dot(gated_turned[:, place:], cots_other[:, span], preferred_element_type=jnp.float32)
+        ).astype(jnp.bfloat16)
+
+        @pl.when(j == 0)
+        def _():
+            up_copy(0).start()
+            down_copy(0).start()
+
+        @pl.when(j == 1)
+        def _():
+            up_copy(1).start()
+
+        @pl.when(j == 2)
+        def _():
+            down_copy(2).start()
+
+        return carry
+
+    lax.fori_loop(0, 4, weight_grads, 0)
+    up_copy(0).wait()
+    add(up_low.at[2], up_in.at[0])
+    up_copy(2).start()
+    down_copy(0).wait()
+    add(down_low.at[1], down_in.at[0])
+    down_copy(1).start()
+
+    @pl.when(inner == 1)
+    def _():
+        for way, part in ((farthest, 0), (backward, 0), (farthest, 1), (backward, 1), (next_one, 1)):
+            relay(*way, part)
+
+    up_sum = up_low[3].astype(jnp.float32)
+    down_sum = down_low[3].astype(jnp.float32)
+    for j in (1, 2):
+        up_copy(j).wait()
+        up_sum += up_in[j].astype(jnp.float32)
+        down_copy(j).wait()
+        down_sum += down_in[j].astype(jnp.float32)
+    for e in range(experts):
+        up_out[e] = up_sum[e * hidden : (e + 1) * hidden, :].T
+        down_out[e] = down_sum[e * hidden : (e + 1) * hidden, :]
+
+    for part in range(2):
+        span = spans[part]
+        chain_copy(z, z, z, 0, part).wait_recv()
+        back_out[:, span] = partial[0, z, :, span].astype(jnp.float32) + chain_in[z, :, span].astype(jnp.float32)
+
+        @pl.when(inner == 1)
+        def _():
+            chain_copy(z, 4, z, 0, part).wait_recv()
+            back_out[:, span] = back_out[:, span] + chain_in[4, :, span].astype(jnp.float32)
+
+    for at in range(4):
+        row_copy(0, at).wait_send()
+        cot_copy(at).wait_send()
+        pair_copy(at).wait_send()
+
+        @pl.when((at <= z) & (z < 3))
+        def _():
+            row_copy(1, at).wait_send()
+
+        @pl.when((at >= z) & (z > 0))
+        def _():
+            row_copy(2, at).wait_send()
+
+    for part in range(2):
+
+        @pl.when(inner == 0)
+        def _():
+            chain_copy(z, 0, z, 0, part).wait_send()
+
+        @pl.when(inner == 1)
+        def _():
+            chain_copy(z, 0, z, 2, part).wait_send()
+
+        chain_copy(z, 0, z, 1, part).wait_send()
+        chain_copy(z, 0, z, 3, part).wait_send()
+
+def expert_kernel_visit(sent, cot_line, up, down):
+    tokens = sent.shape[0]
+    experts, _, hidden = up.shape
+    wide = experts * hidden
+    low = jnp.bfloat16
+    vmem = pl.BlockSpec(memory_space=pltpu.VMEM)
+    dma = pltpu.SemaphoreType.DMA
+    f32 = jnp.float32
+    return pl.pallas_call(
+        visit_kernel,
+        out_shape=[
+            jax.ShapeDtypeStruct((tokens, 2 * D + 128), f32),
+            jax.ShapeDtypeStruct((experts, D // 4, hidden), f32),
+            jax.ShapeDtypeStruct((experts, hidden, D // 4), f32),
+        ],
+        in_specs=[vmem] * 4,
+        out_specs=[vmem] * 3,
+        scratch_shapes=[
+            pltpu.VMEM((8, tokens, D + 128), low),
+            pltpu.VMEM((4, tokens, D), low),
+            pltpu.VMEM((D, wide), low),
+            pltpu.VMEM((128, wide), low),
+            pltpu.VMEM((tokens, D), low),
+            pltpu.VMEM((tokens, wide), low),
+            pltpu.VMEM((tokens, wide), low),
+            pltpu.VMEM((wide, 8 * tokens), low),
+            pltpu.VMEM((wide, 8 * tokens), low),
+            pltpu.VMEM((2, 4, tokens, 2 * D + 128), low),
+            pltpu.VMEM((4, tokens, 2 * D + 128), low),
+            pltpu.VMEM((5, tokens, 2 * D + 128), low),
+            pltpu.VMEM((4, wide, D // 4), low),
+            pltpu.VMEM((4, wide, D // 4), low),
+            pltpu.VMEM((3, wide, D // 4), low),
+            pltpu.VMEM((3, wide, D // 4), low),
+            dma((3, 4)), dma((2, 4)), dma((4,)), dma((4,)), dma((4,)), dma((4,)), dma((4, 2)), dma((5, 2)), dma((2, 3)), dma((2, 3)),
+        ],
+        compiler_params=pltpu.CompilerParams(collective_id=2, has_side_effects=True, vmem_limit_bytes=58 * 2**20),
+        name="expert_visit",
+    )(sent, cot_line, up, down.reshape(wide, D))
+
+
+def attend_kernel(
+    expert_total, lengths, hidden, cot, value_pick, output_pick, expert_pick, routers, gains,
+    key_weight_at, value_weight_at, query_weight_at, output_weight_at,
+    middle, sent, normed_one, normed_two, queries, key_value, probs, value_all, attended,
+    gates, slopes, cot_line,
+    key_weight, value_weight, query_weight, output_weight, mixed, hot_turned, hot,
+    fetch, pair_send, pair_recv, cot_send, cot_recv, own_sem,
+):
+    dp, ex = lax.axis_index("dp"), lax.axis_index("expert")
+    z, core = ex // 2, ex % 2
+    half = z // 2
+    inner = z + half * (3 - 2 * z)
+    count = hidden.shape[0]
+    width = HEADS * HEAD_DIM
+    low = jnp.bfloat16
+    length = lengths[0]
+    spread = HEADS * VE
+    total = expert_total
+    weights = [
+        pltpu.make_async_copy(source, target, fetch.at[i])
+        for i, (source, target) in enumerate(
+            (
+                (key_weight_at, key_weight),
+                (value_weight_at, value_weight),
+                (query_weight_at, query_weight),
+                (output_weight_at, output_weight),
+            )
+        )
+    ]
+    for made in weights:
+        made.start()
+
+    def at_z(place):
+        return (dp, place * 2 + core)
+
+    barrier = pltpu.get_barrier_semaphore()
+    for k in (1, 2, 3):
+        pl.semaphore_signal(barrier, inc=1, device_id=((dp + k) % 4, ex), device_id_type=MESH)
+
+    @pl.when(z < 3)
+    def _():
+        pl.semaphore_signal(barrier, inc=1, device_id=at_z(z + 1), device_id_type=MESH)
+
+    @pl.when(z > 0)
+    def _():
+        pl.semaphore_signal(barrier, inc=1, device_id=at_z(z - 1), device_id_type=MESH)
+
+    pl.semaphore_wait(barrier, 4 + inner)
+
+    def cot_copy(way, at, source=None):
+        block = cot_line.at[at]
+        return pltpu.make_async_remote_copy(
+            src_ref=block if source is None else source, dst_ref=block,
+            send_sem=cot_send.at[way, at], recv_sem=cot_recv.at[at],
+            device_id=at_z(z + 1 - 2 * way), device_id_type=MESH,
+        )
+
+    def pass_on(distance):
+        @pl.when(z >= distance)
+        def _():
+            cot_copy(0, z - distance).wait_recv()
+
+        @pl.when((z >= distance) & (z < 3))
+        def _():
+            cot_copy(0, z - distance).start()
+
+        @pl.when(z + distance <= 3)
+        def _():
+            cot_copy(1, z + distance).wait_recv()
+
+        @pl.when((z + distance <= 3) & (z > 0))
+        def _():
+            cot_copy(1, z + distance).start()
+
+    @pl.when(z < 3)
+    def _():
+        cot_copy(0, z, cot).start()
+
+    @pl.when(z > 0)
+    def _():
+        cot_copy(1, z, cot).start()
+
+    keep = pltpu.make_async_copy(cot, cot_line.at[z], own_sem)
+    keep.start()
+
+    def norm(field, gain):
+        center = field - jnp.mean(field, axis=-1, keepdims=True)
+        spread = jnp.mean(center * center, axis=-1, keepdims=True)
+        return (center * lax.rsqrt(spread + EPSILON) * gain).astype(low)
+
+    parts = (pl.ds(0, width), pl.ds(width, width))
+
+    def pair_copy(step, part, block):
+        return pltpu.make_async_remote_copy(
+            src_ref=key_value.at[block, :, parts[part]], dst_ref=key_value.at[block, :, parts[part]],
+            send_sem=pair_send.at[step, part], recv_sem=pair_recv.at[block, part],
+            device_id=((dp + step) % 4, ex), device_id_type=MESH,
+        )
+
+    def send_part(part):
+        for step in (1, 2, 3):
+
+            @pl.when(dp + step < 4)
+            def _():
+                pair_copy(step, part, dp).start()
+
+    normed_one[...] = norm(hidden[...].astype(jnp.float32), gains[0:1, :])
+    weights[0].wait()
+    key_value[dp, :, parts[0]] = jnp.dot(
+        normed_one[...], key_weight[...], preferred_element_type=jnp.float32
+    ).astype(low)
+    send_part(0)
+
+    hot_turned[...] = jnp.zeros(hot_turned.shape, jnp.float32)
+
+    def mark(picks, base, size):
+        place = lax.broadcasted_iota(jnp.int32, (size, count), 0)
+        found = jnp.zeros((size, count), jnp.float32)
+        for pick in picks:
+            found = jnp.where(place == pick, 1.0, found)
+        hot_turned[base : base + size, :] = found
+
+    mark([value_pick[h, i : i + 1, :] + h * VE for h in range(HEADS) for i in range(value_pick.shape[1])], 0, spread)
+    mark(
+        [output_pick[h, i : i + 1, :] + h * VE for h in range(HEADS) for i in range(output_pick.shape[1])],
+        spread,
+        spread,
+    )
+    mark([expert_pick[i : i + 1, :] for i in range(expert_pick.shape[0])], 2 * spread, total)
+    hot[...] = hot_turned[...].T
+    sig = jax.nn.sigmoid(dot_last(normed_one[...], routers[...]))
+    gates[...] = sig * hot[...]
+    slopes[...] = gates[...] * (1.0 - sig)
+    weights[1].wait()
+
+    def values(n, carry):
+        span = pl.ds(pl.multiple_of(n * 256, 256), 256)
+        value_all[:, span] = jnp.dot(
+            hidden[...], value_weight[:, span], preferred_element_type=jnp.float32
+        ).astype(low)
+        return carry
+
+    lax.fori_loop(0, HEADS * VE * HEAD_DIM // 256, values, 0)
+    for h in range(HEADS):
+        row = jnp.zeros((count, HEAD_DIM), jnp.float32)
+        for e in range(h * VE, (h + 1) * VE):
+            row += gates[:, e : e + 1] * value_all[:, e * HEAD_DIM : (e + 1) * HEAD_DIM].astype(jnp.float32)
+        key_value[dp, :, width + h * HEAD_DIM : width + (h + 1) * HEAD_DIM] = row.astype(low)
+    send_part(1)
+
+    weights[2].wait()
+    queries[...] = jnp.dot(normed_one[...], query_weight[...], preferred_element_type=jnp.float32).astype(low)
+    for block in range(4):
+
+        @pl.when(block > dp)
+        def _():
+            key_value[block] = jnp.zeros((count, 2 * width), low)
+
+    pass_on(1)
+
+    def wait_part(part):
+        for block in range(3):
+
+            @pl.when(block < dp)
+            def _():
+                pair_copy(1, part, block).wait_recv()
+
+    wait_part(0)
+    pair_all = key_value.reshape(4 * count, 2 * width)
+    query_pos = dp * count + lax.broadcasted_iota(jnp.int32, (count, 4 * count), 0)
+    key_pos = lax.broadcasted_iota(jnp.int32, (count, 4 * count), 1)
+    allowed = (key_pos <= query_pos) & (key_pos < length)
+
+    def score(h, carry):
+        span = pl.ds(pl.multiple_of(h * HEAD_DIM, HEAD_DIM), HEAD_DIM)
+        raw = dot_last(queries[:, span], pair_all[:, span])
+        scores = jnp.where(allowed, raw * HEAD_DIM ** (-0.5), NEGATIVE)
+        terms = jnp.exp(scores - jnp.max(scores, axis=-1, keepdims=True))
+        probs[h] = (terms * (1.0 / jnp.sum(terms, axis=-1, keepdims=True))).astype(low)
+        return carry
+
+    lax.fori_loop(0, HEADS, score, 0)
+    wait_part(1)
+    pass_on(2)
+
+    def collect(h, carry):
+        span = pl.ds(pl.multiple_of(h * HEAD_DIM, HEAD_DIM), HEAD_DIM)
+        value_span = pl.ds(pl.multiple_of(width + h * HEAD_DIM, HEAD_DIM), HEAD_DIM)
+        attended[:, span] = jnp.dot(probs[h], pair_all[:, value_span], preferred_element_type=jnp.float32)
+        return carry
+
+    lax.fori_loop(0, HEADS, collect, 0)
+    for h in range(HEADS):
+        row = attended[:, h * HEAD_DIM : (h + 1) * HEAD_DIM]
+        for e in range(h * VE, (h + 1) * VE):
+            mixed[:, e * HEAD_DIM : (e + 1) * HEAD_DIM] = (gates[:, spread + e : spread + e + 1] * row).astype(low)
+
+    place = dp * count + lax.broadcasted_iota(jnp.int32, (count, 1), 0)
+    live = jnp.where(place < length, 1.0, 0.0)
+    weights[3].wait()
+
+    def outward(n, carry):
+        span = pl.ds(pl.multiple_of(n * 256, 256), 256)
+        branch = jnp.dot(mixed[...], output_weight[:, span], preferred_element_type=jnp.float32)
+        middle[:, span] = hidden[:, span].astype(jnp.float32) + live * branch
+        return carry
+
+    lax.fori_loop(0, D // 256, outward, 0)
+    sent[:, :D] = middle[...].astype(low)
+    normed_two[...] = norm(middle[...], gains[1:2, :])
+    sig = jax.nn.sigmoid(dot_last(normed_two[...], routers[...]))
+    gate = sig * hot[...] * live
+    sent[:, D:] = gate.astype(low)
+    lane = lax.broadcasted_iota(jnp.int32, (count, 128), 1)
+    slopes[...] = jnp.where(lane < 2 * spread, slopes[...], gate * (1.0 - sig))
+
+    pass_on(3)
+    keep.wait()
+    for part in range(2):
+        for step in (1, 2, 3):
+
+            @pl.when(dp + step < 4)
+            def _():
+                pair_copy(step, part, dp).wait_send()
+
+    for at in range(4):
+
+        @pl.when((at <= z) & (z < 3))
+        def _():
+            cot_copy(0, at).wait_send()
+
+        @pl.when((at >= z) & (z > 0))
+        def _():
+            cot_copy(1, at).wait_send()
+
+
+def attend(total, lengths, *operands):
+    count = operands[0].shape[0]
+    low, full = jnp.bfloat16, jnp.float32
+    vmem = pl.BlockSpec(memory_space=pltpu.VMEM)
+    anywhere = pl.BlockSpec(memory_space=pl.ANY)
+    dma = pltpu.SemaphoreType.DMA
+    width, wide = HEADS * HEAD_DIM, HEADS * VE * HEAD_DIM
+    shapes = [
+        ((count, D), full),
+        ((count, D + 128), low),
+        ((count, D), low),
+        ((count, D), low),
+        ((count, width), low),
+        ((4, count, 2 * width), low),
+        ((HEADS, count, 4 * count), low),
+        ((count, wide), low),
+        ((count, width), full),
+        ((count, 128), full),
+        ((count, 128), full),
+        ((4, count, D), low),
+    ]
+    return pl.pallas_call(
+        functools.partial(attend_kernel, total),
+        out_shape=[jax.ShapeDtypeStruct(*shape) for shape in shapes],
+        in_specs=[pl.BlockSpec(memory_space=pltpu.SMEM)] + [vmem] * (len(operands) - 4) + [anywhere] * 4,
+        out_specs=[vmem] * len(shapes),
+        scratch_shapes=[pltpu.VMEM(a.shape, a.dtype) for a in operands[-4:]]
+        + [
+            pltpu.VMEM((count, wide), low),
+            pltpu.VMEM((128, count), full),
+            pltpu.VMEM((count, 128), full),
+            dma((4,)),
+            dma((4, 2)),
+            dma((4, 2)),
+            dma((2, 4)),
+            dma((4,)),
+            dma,
+        ],
+        compiler_params=pltpu.CompilerParams(
+            collective_id=1, has_side_effects=True, vmem_limit_bytes=58 * 2**20
+        ),
+        name="attend",
+    )(lengths, *operands)
+
+
+def backward_kernel(
+    total_experts, lengths, gates, slopes, routers, gains,
+    returned_at, middle_at, cot_at, hidden_at, normed_one_at, queries_at, key_value_at, probs_at, value_all_at,
+    attended_at, normed_two_at, query_weight_at, key_weight_at, value_weight_at, output_weight_at,
+    block_out, grad_in, out_query, out_key, out_value, out_output, out_small, sums_out,
+    returned, middle, cot, hidden, normed_one, queries, key_value, probs, value_all,
+    attended, normed_two, query_weight, key_weight, value_part, output_part,
+    branch, branch_turned, one_turned, hidden_turned, grad_att, grad_query, leave, arrive, grad_key, grad_value,
+    grad_each, grad_middle, grad_one, logit_one, logit_two, small_turned, mixed,
+    grads, grads_small, core_in, plane_in, last_in, sums_in,
+    fetch, part_fetch, leave_send, leave_recv, send, recv,
+):
+    dp, ex = lax.axis_index("dp"), lax.axis_index("expert")
+    y, x, z, core = dp // 2, dp % 2, ex // 2, ex % 2
+    count = hidden.shape[0]
+    width = HEADS * HEAD_DIM
+    low, full = jnp.bfloat16, jnp.float32
+    length = lengths[0]
+    sibling = (dp, z * 2 + 1 - core)
+    beside = (y * 2 + 1 - x, ex)
+    behind = ((1 - y) * 2 + x, ex)
+    across = ((1 - y) * 2 + 1 - x, ex)
+    line = [(dp, ((z + k) % 4) * 2 + core) for k in (1, 2, 3)]
+    barrier = pltpu.get_barrier_semaphore()
+    for place in (sibling, beside, behind, across, *line):
+        pl.semaphore_signal(barrier, inc=1, device_id=place, device_id_type=MESH)
+
+    held = dict(
+        returned=(returned_at, returned),
+        middle=(middle_at, middle),
+        cot=(cot_at, cot),
+        hidden=(hidden_at, hidden),
+        attended=(attended_at, attended),
+        key_value=(key_value_at, key_value),
+        probs=(probs_at, probs),
+        queries=(queries_at, queries),
+        normed_one=(normed_one_at, normed_one),
+        query_weight=(query_weight_at, query_weight),
+        value_all=(value_all_at, value_all),
+        key_weight=(key_weight_at, key_weight),
+        normed_two=(normed_two_at, normed_two),
+    )
+    got = {
+        name: pltpu.make_async_copy(source, target, fetch.at[i])
+        for i, (name, (source, target)) in enumerate(held.items())
+    }
+
+    def output_copy(n):
+        return pltpu.make_async_copy(
+            output_weight_at.at[pl.ds(n * 512, 512)], output_part.at[n % 2], part_fetch.at[0, n % 2]
+        )
+
+    def value_copy(n):
+        return pltpu.make_async_copy(
+            value_weight_at.at[:, pl.ds(n * 512, 512)], value_part.at[n % 2], part_fetch.at[1, n % 2]
+        )
+
+    first_held = ("returned", "middle", "cot", "hidden")
+    for name in first_held:
+        got[name].start()
+    for n in range(2):
+        output_copy(n).start()
+    for name in held:
+        if name not in first_held:
+            got[name].start()
+    for n in range(2):
+        value_copy(n).start()
+
+    pieces = (
+        [(out_output, 512 * n, 512, n) for n in range(5)]
+        + [(out_query, 0, 512, 5), (out_key, 0, 512, 6)]
+        + [(out_value, 512 * n, 512, n) for n in range(5)]
+        + [(out_small, 0, 128, None)]
+    )
+    along_line = (0, 1, 2, 3)
+    in_plane = [i for i in range(len(pieces)) if i not in along_line]
+    x_first = {i: n % 2 == 0 for n, i in enumerate(in_plane)}
+
+    def remote(source, target, slot, place):
+        return pltpu.make_async_remote_copy(
+            src_ref=source, dst_ref=target, send_sem=send.at[slot], recv_sem=recv.at[slot],
+            device_id=place, device_id_type=MESH,
+        )
+
+    def add(target, source):
+        target[...] = (target[...].astype(full) + source[...].astype(full)).astype(target.dtype)
+
+    def own(i):
+        slot = pieces[i][3]
+        return grads_small if slot is None else grads.at[slot]
+
+    def columns(i):
+        return pl.ds(0, pieces[i][2])
+
+    started = {}
+
+    def begin(key, source, target, slot, place):
+        started[key] = remote(source, target, slot, place)
+        started[key].start()
+
+    def halve_core(i):
+        begin((i, 0), own(i).at[:, :, 1 - core], core_in.at[i, :, :, :, columns(i)], (i, 0), sibling)
+
+    def halve_near(i):
+        span = columns(i)
+        started[i, 0].wait()
+        add(core_in.at[i, :, :, :, span], own(i).at[:, :, core])
+        if i in along_line:
+            for k in (1, 2, 3):
+                begin(
+                    (i, k), core_in.at[i, :, (z + k) % 4, :, span],
+                    plane_in.at[i, pl.ds(4 * k - 4, 4), :, span], (i, k), line[k - 1],
+                )
+            return
+        for part in range(2):
+            if x_first[i]:
+                source = core_in.at[i, part * 2 + 1 - x, :, :, span]
+            else:
+                source = core_in.at[i, (1 - y) * 2 + part, :, :, span]
+            target = plane_in.at[i, pl.ds(part * 4, 4), :, span]
+            begin((i, 1 + part), source, target, (i, 1 + part), beside if x_first[i] else behind)
+
+    def halve_far(i):
+        span = columns(i)
+        if i in along_line:
+            held = core_in.at[i, :, z, :, span]
+            for k in (1, 2, 3):
+                started[i, k].wait()
+                add(held, plane_in.at[i, pl.ds(4 * k - 4, 4), :, span])
+            for part in range(2):
+                begin(
+                    (i, 4 + part), core_in.at[i, part * 2 + 1 - x, z, :, span],
+                    last_in.at[i, part, :, span], (i, 4 + part), beside,
+                )
+            return
+        for part in range(2):
+            started[i, 1 + part].wait()
+            kept = part * 2 + x if x_first[i] else y * 2 + part
+            add(plane_in.at[i, pl.ds(part * 4, 4), :, span], core_in.at[i, kept, :, :, span])
+        other = 1 - y if x_first[i] else 1 - x
+        begin(
+            (i, 3), plane_in.at[i, pl.ds(other * 4, 4), :, span], plane_in.at[i, pl.ds(8, 4), :, span],
+            (i, 3), behind if x_first[i] else beside,
+        )
+
+    def spread(i):
+        span = columns(i)
+        if i in along_line:
+            for part in range(2):
+                started[i, 4 + part].wait()
+                add(last_in.at[i, part, :, span], core_in.at[i, part * 2 + x, z, :, span])
+            begin((i, 6), last_in.at[i, 1 - y, :, span], last_in.at[i, 2, :, span], (i, 6), behind)
+            return
+        started[i, 3].wait()
+        add(plane_in.at[i, pl.ds(8, 4), :, span], plane_in.at[i, pl.ds((y if x_first[i] else x) * 4, 4), :, span])
+        for k in (1, 2, 3):
+            begin(
+                (i, 3 + k), plane_in.at[i, 8 + (z + k) % 4, :, span],
+                last_in.at[i, k - 1, :, span], (i, 3 + k), line[k - 1],
+            )
+
+    def finish(i):
+        out, start, size, _ = pieces[i]
+        span = columns(i)
+        if i in along_line:
+            started[i, 6].wait()
+            total = last_in[i, y, :, span].astype(full) + last_in[i, 2, :, span].astype(full)
+        else:
+            total = plane_in[i, 8 + z, :, span].astype(full)
+            for k in (1, 2, 3):
+                started[i, 3 + k].wait()
+                total = total + last_in[i, k - 1, :, span].astype(full)
+        out[:, pl.ds(start, size)] = total
+
+    rows_each = 64
+    lane = lax.broadcasted_iota(jnp.int32, (1, 128), 1)
+    for name in first_held:
+        got[name].wait()
+    logit_two[...] = (returned[:, 2 * D :] * slopes[...]).astype(low)
+
+    def live_rows(start):
+        place = dp * count + start + lax.broadcasted_iota(jnp.int32, (rows_each, 1), 0)
+        return jnp.where(place < length, 1.0, 0.0)
+
+    def norm_back(field, grad, gain):
+        center = field - jnp.mean(field, axis=-1, keepdims=True)
+        scale = lax.rsqrt(jnp.mean(center * center, axis=-1, keepdims=True) + EPSILON)
+        unit = center * scale
+        part = grad * gain
+        back = scale * (
+            part
+            - jnp.mean(part, axis=-1, keepdims=True)
+            - unit * jnp.mean(part * unit, axis=-1, keepdims=True)
+        )
+        return back, jnp.sum(grad * unit, axis=0, keepdims=True)
+
+    def square(field, live, at):
+        total = jnp.sum(jnp.sum(field * field, axis=1, keepdims=True) * live, axis=0, keepdims=True)
+        return jnp.where(lane == at, total, 0.0)
+
+    def first_rows(n, carry):
+        gain_sum, sums = carry
+        start = pl.multiple_of(n * rows_each, rows_each)
+        rows = pl.ds(start, rows_each)
+        live = live_rows(start)
+        field = middle[rows, :]
+        forward = returned[rows, :D]
+        final = field + forward
+        block_out[rows, :] = final.astype(low)
+        source = hidden[rows, :].astype(full)
+        one = jnp.ones((rows_each, 1), full)
+        sums += square(source, live, 0) + square(field - source, one, 1)
+        sums += square(forward, one, 2) + square(final, live, 3)
+        sums += jnp.where(lane == 4, jnp.sum(live, axis=0, keepdims=True), 0.0)
+        grad = jnp.dot(logit_two[rows, :], routers[...], preferred_element_type=full)
+        back, gain_part = norm_back(field, grad, gains[1:2, :])
+        total = cot[rows, :].astype(full) + returned[rows, D : 2 * D] + back
+        grad_middle[rows, :] = total
+        branch[rows, :] = (live * total).astype(low)
+        return gain_sum + gain_part, sums
+
+    gain_two_sum, sums = lax.fori_loop(
+        0, count // rows_each, first_rows, (jnp.zeros((1, D), full), jnp.zeros((1, 128), full))
+    )
+    sums_in[0] = jnp.broadcast_to(sums, (8, 128))
+    pl.semaphore_wait(barrier, 7)
+
+    def weight_grad(i, turned, right, size):
+        flat = own(i)
+        flat = flat.reshape(D, size)
+
+        def some(n, carry):
+            rows = pl.ds(pl.multiple_of(n * 256, 256), 256)
+            flat[rows, :] = jnp.dot(turned[rows, :], right, preferred_element_type=full).astype(low)
+            return carry
+
+        lax.fori_loop(0, D // 256, some, 0)
+        halve_core(i)
+
+    branch_turned[...] = branch[...].T
+    got["attended"].wait()
+
+    def head_of(c):
+        return slice((c // VE) * HEAD_DIM, (c // VE + 1) * HEAD_DIM)
+
+    spread_count = HEADS * VE
+    for n in range(5):
+        for j in range(4):
+            c = 4 * n + j
+            gate = gates[:, spread_count + c : spread_count + c + 1]
+            mixed[:, j * HEAD_DIM : (j + 1) * HEAD_DIM] = (gate * attended[:, head_of(c)]).astype(low)
+        weight_grad(n, branch_turned, mixed[...], 512)
+    logit_one[...] = jnp.zeros(logit_one.shape, full)
+    grad_att[...] = jnp.zeros(grad_att.shape, full)
+    for n in range(5):
+        output_copy(n).wait()
+        for j in range(4):
+            c = 4 * n + j
+            grad_mixed = dot_last(branch[...], output_part[n % 2, j * HEAD_DIM : (j + 1) * HEAD_DIM, :])
+            col = spread_count + c
+            grad_att[:, head_of(c)] += gates[:, col : col + 1] * grad_mixed
+            dots = jnp.sum(attended[:, head_of(c)] * grad_mixed, axis=1, keepdims=True)
+            logit_one[:, col : col + 1] = dots * slopes[:, col : col + 1]
+        if n + 2 < 5:
+            output_copy(n + 2).start()
+        halve_near(n)
+
+    pair_all = key_value.reshape(4 * count, 2 * width)
+    for name in ("key_value", "probs", "queries"):
+        got[name].wait()
+
+    def leave_copy(k, h):
+        rows = pl.ds(h * 2 * HEAD_DIM, 2 * HEAD_DIM)
+        return pltpu.make_async_remote_copy(
+            src_ref=leave.at[(dp + 4 - k) % 4, rows], dst_ref=arrive.at[k - 1, rows],
+            send_sem=leave_send.at[k - 1, h], recv_sem=leave_recv.at[k - 1, h],
+            device_id=((dp + 4 - k) % 4, ex), device_id_type=MESH,
+        )
+
+    def head(h, carry):
+        start = pl.multiple_of(h * HEAD_DIM, HEAD_DIM)
+        span = pl.ds(start, HEAD_DIM)
+        grad = grad_att[:, span].astype(low)
+        prob = probs[h].astype(full)
+        grad_prob = dot_last(grad, pair_all[:, pl.ds(width + start, HEAD_DIM)])
+        dots = jnp.sum(prob * grad_prob, axis=-1, keepdims=True)
+        grad_score = (prob * (grad_prob - dots) * HEAD_DIM ** (-0.5)).astype(low)
+        grad_query[:, span] = jnp.dot(grad_score, pair_all[:, span], preferred_element_type=full).astype(low)
+        key_part = dot_first(queries[:, span], grad_score).astype(low)
+        value_part_all = dot_first(grad, probs[h]).astype(low)
+        key_rows = pl.ds(pl.multiple_of(2 * h * HEAD_DIM, 2 * HEAD_DIM), HEAD_DIM)
+        value_rows = pl.ds(pl.multiple_of((2 * h + 1) * HEAD_DIM, HEAD_DIM), HEAD_DIM)
+        for j in range(4):
+            leave[j, key_rows, :] = key_part[:, j * count : (j + 1) * count]
+            leave[j, value_rows, :] = value_part_all[:, j * count : (j + 1) * count]
+        for k in (1, 2, 3):
+
+            @pl.when(dp >= k)
+            def _():
+                leave_copy(k, h).start()
+
+        return carry
+
+    lax.fori_loop(0, HEADS, head, 0)
+
+    for name in ("normed_one", "query_weight"):
+        got[name].wait()
+    one_turned[...] = normed_one[...].T
+    weight_grad(5, one_turned, grad_query[...], 512)
+    hidden_turned[...] = hidden[...].T
+    grad_one[...] = dot_last(grad_query[...], query_weight[...])
+    halve_near(5)
+
+    for h in range(HEADS):
+        rows = pl.ds(h * 2 * HEAD_DIM, 2 * HEAD_DIM)
+        total = leave[dp, rows, :].astype(full)
+        for k in (1, 2, 3):
+
+            @pl.when(dp + k < 4)
+            def _():
+                leave_copy(k, h).wait_recv()
+
+            @pl.when(dp + k >= 4)
+            def _():
+                arrive[k - 1, rows, :] = jnp.zeros((2 * HEAD_DIM, count), low)
+
+            total += arrive[k - 1, rows, :].astype(full)
+        turned = total.T
+        grad_key[:, h * HEAD_DIM : (h + 1) * HEAD_DIM] = turned[:, :HEAD_DIM].astype(low)
+        grad_value[:, h * HEAD_DIM : (h + 1) * HEAD_DIM] = turned[:, HEAD_DIM:].astype(low)
+
+    got["value_all"].wait()
+    for n in range(5):
+        for j in range(4):
+            c = 4 * n + j
+            grad = grad_value[:, head_of(c)].astype(full)
+            here = slice(c * HEAD_DIM, (c + 1) * HEAD_DIM)
+            grad_each[:, here] = (gates[:, c : c + 1] * grad).astype(low)
+            dots = jnp.sum(value_all[:, here].astype(full) * grad, axis=1, keepdims=True)
+            logit_one[:, c : c + 1] = dots * slopes[:, c : c + 1]
+        weight_grad(7 + n, hidden_turned, grad_each[:, n * 512 : (n + 1) * 512], 512)
+        if n:
+            halve_near(6 + n)
+    weight_grad(6, one_turned, grad_key[...], 512)
+    halve_near(11)
+    got["key_weight"].wait()
+    grad_one[...] += dot_last(grad_key[...], key_weight[...])
+    halve_near(6)
+    grad_one[...] += jnp.dot(logit_one[...].astype(low), routers[...], preferred_element_type=full)
+    halve_far(5)
+
+    def first_norm(n, gain_sum):
+        rows = pl.ds(pl.multiple_of(n * rows_each, rows_each), rows_each)
+        back, gain_part = norm_back(hidden[rows, :].astype(full), grad_one[rows, :], gains[0:1, :])
+        grad_in[rows, :] = grad_middle[rows, :] + back
+        return gain_sum + gain_part
+
+    gain_one_sum = lax.fori_loop(0, count // rows_each, first_norm, jnp.zeros((1, D), full))
+    halve_far(7)
+    spread(5)
+    got["normed_two"].wait()
+    small_turned[...] = dot_first(logit_one[...].astype(low), normed_one[...]) + dot_first(
+        logit_two[...], normed_two[...]
+    )
+    small_rows = 2 * spread_count + total_experts
+    small_turned[small_rows : small_rows + 1, :] = gain_one_sum
+    small_turned[small_rows + 1 : small_rows + 2, :] = gain_two_sum
+    grads_small.reshape(D, 128)[...] = small_turned[...].T.astype(low)
+    halve_core(12)
+
+    rounds = [[sibling], [beside], [behind], line]
+    offset = [1, 2, 3, 4]
+
+    def sum_start(r):
+        for j, place in enumerate(rounds[r]):
+            begin(("sum", r, j), sums_in.at[0], sums_in.at[offset[r] + j], (len(pieces) + j, r), place)
+
+    def sum_end(r):
+        for j in range(len(rounds[r])):
+            started["sum", r, j].wait()
+        total = sums_in[0]
+        for j in range(len(rounds[r])):
+            total = total + sums_in[offset[r] + j]
+        sums_in[0] = total
+
+    sum_start(0)
+    for n in range(5):
+        value_copy(n).wait()
+        part = dot_last(grad_each[:, n * 512 : (n + 1) * 512], value_part[n % 2])
+        grad_in[...] += part
+        if n + 2 < 5:
+            value_copy(n + 2).start()
+        if n == 0:
+            halve_near(12)
+            sum_end(0)
+            sum_start(1)
+        if n == 1:
+            halve_far(8)
+            spread(7)
+        if n == 2:
+            finish(5)
+            halve_far(9)
+            spread(8)
+            sum_end(1)
+            sum_start(2)
+        if n == 3:
+            halve_far(0)
+            finish(7)
+        if n == 4:
+            sum_end(2)
+            sum_start(3)
+            halve_far(10)
+            spread(9)
+
+    for action, i in (
+        (halve_far, 1), (spread, 0), (finish, 8), (halve_far, 4), (halve_far, 11), (spread, 10), (finish, 0), (finish, 9),
+        (sum_end, 3),
+        (halve_far, 2), (spread, 1), (spread, 4), (halve_far, 6), (spread, 11), (finish, 10), (finish, 1),
+        (halve_far, 12), (spread, 2), (spread, 6), (finish, 4), (finish, 11), (halve_far, 3), (spread, 12), (finish, 2),
+        (finish, 6), (spread, 3), (finish, 12), (finish, 3),
+    ):
+        action(i)
+    sums_out[...] = sums_in[0]
+    for h in range(HEADS):
+        for k in (1, 2, 3):
+
+            @pl.when(dp >= k)
+            def _():
+                leave_copy(k, h).wait_send()
+
+
+def backward(total_experts, lengths, gates, slopes, routers, gains, *arrays):
+    low, full = jnp.bfloat16, jnp.float32
+    count = gates.shape[0]
+    width, wide = HEADS * HEAD_DIM, HEADS * VE * HEAD_DIM
+    vmem = pl.BlockSpec(memory_space=pltpu.VMEM)
+    anywhere = pl.BlockSpec(memory_space=pl.ANY)
+    dma = pltpu.SemaphoreType.DMA
+    whole = [pltpu.VMEM(a.shape, a.dtype) for a in arrays[:13]]
+    n = 13
+    return pl.pallas_call(
+        functools.partial(backward_kernel, total_experts),
+        out_shape=[
+            jax.ShapeDtypeStruct((count, D), low),
+            jax.ShapeDtypeStruct((count, D), full),
+            jax.ShapeDtypeStruct((ROWS, width), full),
+            jax.ShapeDtypeStruct((ROWS, width), full),
+            jax.ShapeDtypeStruct((ROWS, wide), full),
+            jax.ShapeDtypeStruct((ROWS, wide), full),
+            jax.ShapeDtypeStruct((ROWS, 128), full),
+            jax.ShapeDtypeStruct((8, 128), full),
+        ],
+        in_specs=[pl.BlockSpec(memory_space=pltpu.SMEM)] + [vmem] * 4 + [anywhere] * len(arrays),
+        out_specs=[vmem] * 8,
+        scratch_shapes=whole
+        + [
+            pltpu.VMEM((2, D, 512), low),
+            pltpu.VMEM((2, 512, D), low),
+            pltpu.VMEM((count, D), low),
+            pltpu.VMEM((D, count), low),
+            pltpu.VMEM((D, count), low),
+            pltpu.VMEM((D, count), low),
+            pltpu.VMEM((count, width), full),
+            pltpu.VMEM((count, width), low),
+            pltpu.VMEM((4, 2 * width, count), low),
+            pltpu.VMEM((3, 2 * width, count), low),
+            pltpu.VMEM((count, width), low),
+            pltpu.VMEM((count, width), low),
+            pltpu.VMEM((count, wide), low),
+            pltpu.VMEM((count, D), full),
+            pltpu.VMEM((count, D), full),
+            pltpu.VMEM((count, 128), full),
+            pltpu.VMEM((count, 128), low),
+            pltpu.VMEM((128, D), full),
+            pltpu.VMEM((count, 512), low),
+            pltpu.VMEM((7, 4, 4, 2, ROWS, 512), low),
+            pltpu.VMEM((4, 4, 2, ROWS, 128), low),
+            pltpu.VMEM((n, 4, 4, ROWS, 512), low),
+            pltpu.VMEM((n, 12, ROWS, 512), low),
+            pltpu.VMEM((n, 3, ROWS, 512), low),
+            pltpu.VMEM((7, 8, 128), full),
+            dma((13,)),
+            dma((2, 2)),
+            dma((3, HEADS)),
+            dma((3, HEADS)),
+            dma((n + 3, 7)),
+            dma((n + 3, 7)),
+        ],
+        compiler_params=pltpu.CompilerParams(
+            collective_id=3, has_side_effects=True, vmem_limit_bytes=62 * 2**20
+        ),
+        name="backward",
+    )(lengths, gates, slopes, routers, gains, *arrays)
 
 
 def expert_visit(sent, cotangent, expert_up, expert_down):
@@ -295,20 +2577,22 @@
         returned, grad_up, grad_down = expert_visit(*item, expert_up, expert_down)
         return (grads[0] + grad_up, grads[1] + grad_down), returned
 
-    if rounds == 1:
-        returned, grad_up, grad_down = expert_visit(sent, cotangent[0], expert_up, expert_down)
-    else:
-        zeros = jnp.zeros(expert_up.shape, jnp.float32), jnp.zeros(expert_down.shape, jnp.float32)
-        (grad_up, grad_down), returned = lax.scan(
-            visit,
-            zeros,
-            (
-                sent.reshape(rounds, -1, sent.shape[1]),
-                cotangent[0].reshape(rounds, -1, D),
-            ),
-        )
-        returned = returned.reshape(row_count, -1)
-    returned = returned.astype(jnp.float32)
+    zeros = jnp.zeros(expert_up.shape, jnp.float32), jnp.zeros(expert_down.shape, jnp.float32)
+    (up_grad, down_grad), returned = lax.scan(
+        visit,
+        zeros,
+        (
+            sent.reshape(rounds, -1, sent.shape[1]),
+            cotangent[0].reshape(rounds, -1, D),
+        ),
+    )
+    returned = returned.reshape(row_count, -1).astype(jnp.float32)
+    up_grad = lax.psum_scatter(
+        up_grad.astype(jnp.bfloat16), "dp", scatter_dimension=1, tiled=True
+    ).astype(jnp.float32)
+    down_grad = lax.psum_scatter(
+        down_grad.astype(jnp.bfloat16), "dp", scatter_dimension=2, tiled=True
+    ).astype(jnp.float32)
     feedforward_out = returned[:, :D]
     final_rows = middle + feedforward_out
     sums = jnp.stack(
@@ -434,15 +2718,11 @@
             small_grads,
         )
     ]
-    if lax.axis_size("dp") == 4 and lax.axis_size("expert") == 8:
-        dense_grads, sums_tile = dense_sum(low_grads, jnp.pad(sums[None], ((0, 7), (0, 123))))
-        total_sums = sums_tile[0, :5]
-    else:
-        summed = lax.psum_scatter(
-            jnp.concatenate(low_grads, axis=1), ("dp", "expert"), scatter_dimension=0, tiled=True
-        ).astype(jnp.float32)
-        dense_grads = jnp.split(summed, [512, 1024, 3584, 6144], axis=1)
-        total_sums = lax.psum(sums, ("dp", "expert"))
+    summed = lax.psum_scatter(
+        jnp.concatenate(low_grads, axis=1), ("dp", "expert"), scatter_dimension=0, tiled=True
+    ).astype(jnp.float32)
+    dense_grads = jnp.split(summed, [512, 1024, 3584, 6144], axis=1)
+    total_sums = lax.psum(sums, ("dp", "expert"))
     residual_norms = jnp.sqrt(total_sums[:4] / (total_sums[4] * D))
     small = dense_grads[4]
     router_end = 2 * HEADS * VE + expert_router.shape[1]
@@ -457,14 +2737,6 @@
         small[:, router_end],
         small[:, router_end + 1],
     ]
-    expert_grads = (
-        lax.psum_scatter(
-            grad_up.astype(jnp.bfloat16), "dp", scatter_dimension=1, tiled=True
-        ).astype(jnp.float32),
-        lax.psum_scatter(
-            grad_down.astype(jnp.bfloat16), "dp", scatter_dimension=2, tiled=True
-        ).astype(jnp.float32),
-    )
     return (
         final_rows.astype(jnp.bfloat16)[None],
         grad_input[None],
@@ -477,8 +2749,105 @@
         dense_grads[6],
         dense_grads[7],
         dense_grads[8],
-        expert_grads[0],
-        expert_grads[1],
+        up_grad,
+        down_grad,
+        residual_norms,
+    )
+
+
+def shards_fast(
+    hidden_in,
+    lengths,
+    value_pick,
+    output_pick,
+    expert_pick,
+    query_weight,
+    key_weight,
+    value_weight,
+    output_weight,
+    value_router,
+    output_router,
+    expert_router,
+    attention_gain,
+    feedforward_gain,
+    expert_up,
+    expert_down,
+    cotangent,
+):
+    total = expert_router.shape[1]
+    spread = HEADS * VE
+    routers = jnp.concatenate(
+        [value_router.T, output_router.T, expert_router.T, jnp.zeros((128 - 2 * spread - total, D), jnp.bfloat16)]
+    )
+    gains = jnp.stack([attention_gain, feedforward_gain]).astype(jnp.float32)
+    (
+        middle,
+        sent,
+        normed_one,
+        normed_two,
+        queries,
+        key_value,
+        probs,
+        value_all,
+        attended,
+        gates,
+        slopes,
+        cot_line,
+    ) = attend(
+        total,
+        lengths,
+        hidden_in[0],
+        cotangent[0],
+        value_pick[0].transpose(1, 2, 0),
+        output_pick[0].transpose(1, 2, 0),
+        expert_pick[0].T,
+        routers,
+        gains,
+        key_weight,
+        value_weight,
+        query_weight,
+        output_weight,
+    )
+    returned, up_grad, down_grad = expert_kernel_visit(sent, cot_line, expert_up, expert_down)
+    block_out, grad_input, grad_query, grad_key, grad_value, grad_output, small, sums = backward(
+        total,
+        lengths,
+        gates,
+        slopes,
+        routers,
+        gains,
+        returned,
+        middle,
+        cotangent[0],
+        hidden_in[0],
+        normed_one,
+        queries,
+        key_value,
+        probs,
+        value_all,
+        attended,
+        normed_two,
+        query_weight,
+        key_weight,
+        value_weight,
+        output_weight,
+    )
+    residual_norms = jnp.sqrt(sums[0, :4] / (sums[0, 4] * D))
+    router_end = 2 * spread + total
+    return (
+        block_out[None],
+        grad_input[None],
+        grad_query,
+        grad_key,
+        grad_value,
+        grad_output.T,
+        small[:, :spread],
+        small[:, spread : 2 * spread],
+        small[:, 2 * spread : router_end],
+        small[:, router_end],
+        small[:, router_end + 1],
+        up_grad,
+        down_grad,
         residual_norms,
     )
 
@@ -503,8 +2872,9 @@
         P("expert", None, None),
         P("expert", "dp", None),
     )
+    small_mesh = mesh.shape["dp"] == 4 and mesh.shape["expert"] == 8
     return jax.shard_map(
-        shards,
+        shards_fast if small_mesh else shards,
         mesh=mesh,
         in_specs=placed,
         out_specs=(

time: 576 us -> 301 us (0.52); the launches traced: 568 us -> 300 us
  waiting for transfers between devices: 257 us -> 0 us
  Pallas kernels: 90.4 us -> 278 us
  matrix products: 127 us -> 0 us
  other arithmetic: 33.4 us -> 3.5 us
  local copies, waits for them, and re-layouts: 42 us -> 16.6 us
  between operations: 16.8 us -> 2.01 us
    pallas_call x1 -> x3, Pallas kernels: 90.4 us -> 278 us  [the longest x1 120 us: expert_kernel_visit(): pl.pallas_call(visit_kernel, out_shape=[jax.ShapeDtypeStruct((tokens, 2 *...]
    reduce_scatter x5 -> x0, waiting for transfers between devices: 146 us -> none  [the longest x1 78.2 us: expert_visit(): lax.psum_scatter(jnp.concatenate([partial_out.astype(jnp.bfloat16), parti...]
    dot_general x31 -> x0, matrix products: 116 us -> none  [the longest x13 19.7 us: low_dot(): return jnp.dot(left_side, right_side, preferred_element_type=jnp.float32)]
    all_gather x4 -> x0, waiting for transfers between devices: 110 us -> none  [the longest x1 48.1 us: expert_visit(): sent_all = lax.all_gather(sent, 'expert', axis=0, tiled=True)]
    unnamed x150 -> x22, local copies, waits for them, and re-layouts: 24 us -> 10.1 us
    reduce_sum x12 -> x0, other arithmetic: 12.3 us -> none  [the longest x1 3.07 us: shards(): jnp.sum(live_mask * final_rows * final_rows)]
    concatenate x2 -> x1, other arithmetic: 8.09 us -> 1.7 us  [shards_fast(): jnp.concatenate([value_router.T, output_router.T, expert_router.T, jnp.ze...]
    convert_element_type x11 -> x1, other arithmetic: 6.87 us -> 0.61 us  [shards_fast(): gains = jnp.stack([attention_gain, feedforward_gain]).astype(jnp.float32)]
  transfers between devices with their start and end apart: 9 -> 0, of which waited for: 8 -> 0; matrix products, arithmetic and copies ran while one was open for 22% -> 0% of each run, Pallas kernels for 0% -> 0%
where the time goes in v3:
time: 301 us; the launch traced here: 300 us
  Pallas kernels  278 us (92%)
  local copies, waits for them, and re-layouts  16.6 us (6%)
  other arithmetic  3.5 us (1%)
    pallas_call x1, Pallas kernels, expert_kernel_visit(): pl.pallas_call(visit_kernel, out_shape=[jax.ShapeDtypeStruct((tokens, 2 *...  120 us
    pallas_call x1, Pallas kernels, backward(): pl.pallas_call(functools.partial(backward_kernel, total_experts), out_sha...  111 us
    pallas_call x1, Pallas kernels, attend(): pl.pallas_call(functools.partial(attend_kernel, total), out_shape=[jax.Sh...  47.5 us
    unnamed x22, local copies, waits for them, and re-layouts  10.1 us

profile of v3, /device:TPU:0, one launch (start us, length us, event | category | flops | bytes accessed | tf_op | source)
XLA Modules:
  0.0 300.1 jit_solution(11078623669819270810)
XLA Ops:
  1.3 0.1 pad.5.clone
  1.4 0.7 stack.9
  2.1 0.7 stack.10
  2.8 0.6 maximum_convert_fusion.gains
  3.4 1.7 maximum_maximum_fusion.routers
  5.1 47.5 %attend.1 = (f32[256,1024]{1,0:T(8,128)}, bf16[256,1152]{1,0:T(8,128)(2,1)}, bf16[256,1024]{1,0:T(8,128)(2,1)}, bf16[256,1024]{1,0:T(8,128)(2,1)}, bf16[256,512]...) custom-call(s32[1]{0:T(128)S(6)} %copy.43.lengths, ...), custom_call_target="tpu_custom_call" | custom-call | tf_op jit(solution)/shard_map/attend/pallas_call | solution.py:1813
  52.5 119.7 %expert_visit.1 = (f32[256,2176]{1,0:T(8,128)}, f32[6,256,128]{2,1,0:T(8,128)}, f32[6,128,256]{2,1,0:T(8,128)}) custom-call(bf16[256,1152]{1,0:T(8,128)(2,1)} %get-tuple-element.39.sent, bf16[4,256,1024]{2,1,0:T(8,128)(2,1)} %get-tuple-element.40.cot, bf16[6,1024,128]{2,1,0:T(8,128)(2,1)} %up.1, bf16[768,1024]{1,0:T(8,128)(2,1)} %bitcast.25), custom_call_target="tpu_custom_call" | custom-call | tf_op jit(solution)/shard_map/expert_visit/pallas_call | solution.py:1523
  172.3 110.8 %backward.1 = (bf16[256,1024]{1,0:T(8,128)(2,1)}, f32[256,1024]{1,0:T(8,128)}, f32[32,512]{1,0:T(8,128)}, f32[32,512]{1,0:T(8,128)}, f32[32,2560]{1,0:T(8,128)},...) custom-call(s32[1]{0:T(128)S(6)} %copy.43.lengths, f32[256,128]{1,0:T(8,128)} %get-tuple-element.37.gates, ...), custom_call_target="tpu_custom_call" | custom-call | tf_op jit(solution)/shard_map/backward/pallas_call | solution.py:2277
  283.1 1.3 slice.27
  285.0 1.2 sqrt_bitcast_fusion
  286.2 1.5 slice_reduce_fusion
  287.7 1.4 slice.23
  289.1 0.9 fusion
  290.0 0.7 copy.34
  290.7 0.7 copy.33
  291.3 1.9 copy.44
  293.2 2.4 copy.45
  295.6 0.6 copy.46
  296.2 0.6 copy.47
  296.9 0.7 copy.48
  297.6 0.7 copy.49
  298.3 0.0 copy-done.1
  298.3 0.9 copy.50
  299.2 0.9 copy.51
  (12 shorter events, 0.0 us)
Async XLA Ops:
  283.1 12.5 %copy-start.5 = (f32[32,512]{1,0:T(8,128)S(1)}, f32[32,512]{1,0:T(8,128)}, u32[]{:S(2)}) copy-start(f32[32,512]{1,0:T(8,128)} %get-tuple-element.108) | copy-start | bytes 196612
  283.1 13.2 %copy-start.4 = (f32[32,512]{1,0:T(8,128)S(1)}, f32[32,512]{1,0:T(8,128)}, u32[]{:S(2)}) copy-start(f32[32,512]{1,0:T(8,128)} %get-tuple-element.109) | copy-start | bytes 196612
  283.1 13.8 %copy-start.3 = (f32[32,2560]{1,0:T(8,128)S(1)}, f32[32,2560]{1,0:T(8,128)}, u32[]{:S(2)}) copy-start(f32[32,2560]{1,0:T(8,128)} %get-tuple-element.110) | copy-start | bytes 983044
  289.1 8.5 %copy-start.2 = (f32[32,2560]{1,0:T(8,128)S(1)}, f32[32,2560]{1,0:T(8,128)}, u32[]{:S(2)}) copy-start(f32[32,2560]{1,0:T(8,128)} %get-tuple-element.55) | copy-start | bytes 983044
  293.2 5.1 %copy-start.1 = (f32[6,256,128]{2,1,0:T(8,128)S(1)}, f32[6,256,128]{2,1,0:T(8,128)}, u32[]{:S(2)}) copy-start(f32[6,256,128]{2,1,0:T(8,128)} %get-tuple-element.117) | copy-start | bytes 2359300
  295.6 3.6 %copy-start = (f32[6,128,256]{2,1,0:T(8,128)S(1)}, f32[6,128,256]{2,1,0:T(8,128)}, u32[]{:S(2)}) copy-start(f32[6,128,256]{2,1,0:T(8,128)} %get-tuple-element.118) | copy-start | bytes 2359300

commit v4 on v1

--- a/solution.py
+++ b/solution.py
@@ -1,6 +1,10 @@
+import functools
+
 import jax
 import jax.numpy as jnp
 from jax import lax
+from jax.experimental import pallas as pl
+from jax.experimental.pallas import tpu as pltpu
 from jax.sharding import PartitionSpec as P
 
 D = 1024
@@ -9,6 +13,9 @@
 VE = 5
 
 
+MESH = pl.DeviceIdType.MESH
+ROWS = 32
+PIECE = VE * HEAD_DIM
 EPSILON = 1e-05
 NEGATIVE = -1000000000.0
 
@@ -38,6 +45,1203 @@
     scores = jnp.where(allowed[None], raw_scores * HEAD_DIM ** (-0.5), NEGATIVE)
     exp_terms = jnp.exp(scores - jnp.max(scores, axis=-1, keepdims=True))
     return exp_terms / jnp.sum(exp_terms, axis=-1, keepdims=True)
+
+
+def dot_last(left_side, right_side):
+    return lax.dot_general(
+        left_side, right_side, (((1,), (1,)), ((), ())), preferred_element_type=jnp.float32
+    )
+
+def dot_first(left_side, right_side):
+    return lax.dot_general(
+        left_side, right_side, (((0,), (0,)), ((), ())), preferred_element_type=jnp.float32
+    )
+
+
+def visit_kernel(
+    sent, cot, up, down, back_out, up_out, down_out, forward_out,
+    rows, cot_other, up_wide, chosen, cots, gated, grad_pre, forward, forward_in, gated_turned, pre_turned, partial, paired_in, chain_in, up_low, down_low, up_in, down_in,
+    row_send, row_recv, cot_send, cot_recv, pair_send, pair_recv, forward_send, forward_recv, chain_send, chain_recv, grad_send, grad_recv,
+):
+    experts = up.shape[0]
+    wide = down.shape[0]
+    hidden = wide // experts
+    dp, ex = lax.axis_index("dp"), lax.axis_index("expert")
+    y, x, z, core = dp // 2, dp % 2, ex // 2, ex % 2
+    half = z // 2
+    inner = z + half * (3 - 2 * z)
+    onward = 1 - 2 * half
+    sibling = (dp, z * 2 + 1 - core)
+    beside, behind = (y * 2 + 1 - x, ex), ((1 - y) * 2 + x, ex)
+
+    def at_z(place):
+        return (dp, place * 2 + core)
+
+    barrier = pltpu.get_barrier_semaphore()
+    for place in (sibling, beside, behind):
+        pl.semaphore_signal(barrier, inc=1, device_id=place, device_id_type=MESH)
+
+    @pl.when(z < 3)
+    def _():
+        pl.semaphore_signal(barrier, inc=1, device_id=at_z(z + 1), device_id_type=MESH)
+
+    @pl.when(z > 0)
+    def _():
+        pl.semaphore_signal(barrier, inc=1, device_id=at_z(z - 1), device_id_type=MESH)
+
+    pl.semaphore_wait(barrier, 4 + inner)
+
+    def remote(source, target, send, recv, place):
+        return pltpu.make_async_remote_copy(
+            src_ref=source, dst_ref=target, send_sem=send, recv_sem=recv, device_id=place, device_id_type=MESH
+        )
+
+    def row_copy(way, at, source=None):
+        place = (sibling, at_z(z + 1), at_z(z - 1))[way]
+        block = rows.at[at]
+        target = block if way else rows.at[4 + at]
+        return remote(block if source is None else source, target, row_send.at[way, at], row_recv.at[0 if way else 1, at], place)
+
+    def cot_copy(at):
+        return remote(cot.at[at], cot_other.at[at], cot_send.at[at], cot_recv.at[at], sibling)
+
+    own = row_copy(0, z, sent), row_copy(1, z, sent), row_copy(2, z, sent)
+
+    @pl.when(z < 3)
+    def _():
+        own[1].start()
+
+    @pl.when(z > 0)
+    def _():
+        own[2].start()
+
+    own[0].start()
+    cot_copy(z).start()
+    for k in (1, 2, 3):
+        cot_copy((z + k) % 4).start()
+    rows[z] = sent[...]
+    for e in range(experts):
+        up_wide[:, e * hidden : (e + 1) * hidden] = up[e]
+    chosen[...] = (
+        lax.broadcasted_iota(jnp.int32, (128, wide), 0)
+        == 2 * HEADS * VE + ex * experts + lax.broadcasted_iota(jnp.int32, (128, wide), 1) // hidden
+    ).astype(jnp.float32).astype(jnp.bfloat16)
+
+    def order(p):
+        later = (p + 2) // 3
+        step = p - inner // (p + 1 - later)
+        return later * (step + half * (3 - 2 * step)) + (1 - later) * z
+
+    def pair_copy(at):
+        return remote(partial.at[1, at], paired_in.at[at], pair_send.at[at], pair_recv.at[at], sibling)
+
+    spans = (pl.ds(0, D // 2), pl.ds(D // 2, D // 2 + 128))
+
+    def chain_copy(dest, slot, to, stage, part):
+        span = spans[part]
+        return remote(
+            partial.at[0, dest, :, span], chain_in.at[slot, :, span],
+            chain_send.at[stage, part], chain_recv.at[slot, part], at_z(to),
+        )
+
+    def add(target, source):
+        def some(i, carry):
+            part = pl.ds(pl.multiple_of(i * 32, 32), 32)
+            target[part, :] = (
+                target[part, :].astype(jnp.float32) + source[part, :].astype(jnp.float32)
+            ).astype(target.dtype)
+            return carry
+
+        lax.fori_loop(0, target.shape[0] // 32, some, 0)
+
+    def visit(q, carry):
+        p, other = q // 2, q % 2
+        at = order(p)
+        block = other * 4 + at
+
+        @pl.when((other == 0) & (p > 0))
+        def _():
+            row_copy(1, at).wait_recv()
+            row_copy(0, at).start()
+
+            @pl.when((at < z) & (z < 3))
+            def _():
+                row_copy(1, at).start()
+
+            @pl.when((at > z) & (z > 0))
+            def _():
+                row_copy(2, at).start()
+
+        @pl.when(other == 1)
+        def _():
+            row_copy(0, at).wait_recv()
+            cot_copy(at).wait_recv()
+            cots[...] = cot_other[at]
+
+        @pl.when(other == 0)
+        def _():
+            cots[...] = cot[at]
+
+        count = rows.shape[1]
+        places = pl.ds(pl.multiple_of(block * count, count), count)
+
+        def columns(n, gate_grad):
+            span = pl.ds(pl.multiple_of(n * 256, 256), 256)
+            pre = jnp.dot(rows[block, :, :D], up_wide[:, span], preferred_element_type=jnp.float32)
+            back = dot_last(cots[...], down[span, :])
+            mark = chosen[:, span]
+            gate = jnp.dot(rows[block, :, D:], mark, preferred_element_type=jnp.float32)
+            sig = jax.nn.sigmoid(pre)
+            act = pre * sig
+            act_low = (gate * act).astype(jnp.bfloat16)
+            pre_low = (gate * back * (sig * (1.0 + pre * (1.0 - sig)))).astype(jnp.bfloat16)
+            gated[block, :, span] = act_low
+            grad_pre[:, span] = pre_low
+            gated_turned[span, places] = act_low.T
+            pre_turned[span, places] = pre_low.T
+            return gate_grad + dot_last((act * back).astype(jnp.bfloat16), mark)
+
+        partial[other, at, :, D:] = lax.fori_loop(
+            0, wide // 256, columns, jnp.zeros((count, 128), jnp.float32)
+        ).astype(jnp.bfloat16)
+
+        def outward(n, carry):
+            span = pl.ds(pl.multiple_of(n * 256, 256), 256)
+            partial[other, at, :, span] = dot_last(grad_pre[...], up_wide[span, :]).astype(jnp.bfloat16)
+            return carry
+
+        lax.fori_loop(0, D // 256, outward, 0)
+
+        @pl.when(other == 1)
+        def _():
+            pair_copy(at).start()
+            pair_copy(at).wait_recv()
+            add(partial.at[0, at], paired_in.at[at])
+
+        @pl.when((inner == 0) & (q == 3))
+        def _():
+            chain_copy(*nearest, 0).start()
+
+        @pl.when((inner == 0) & (q == 5))
+        def _():
+            chain_copy(*next_one, 0).start()
+
+        return carry
+
+    nearest = (z + onward, z + onward, z + onward, 0)
+    farthest = (3 * (1 - half), 3 * (1 - half), z + onward, 1)
+    backward = (3 * half, 3 * half, z - onward, 2)
+    next_one = (2 - half, 2 - half + inner * (2 + half), z + onward, 3)
+    lax.fori_loop(0, 8, visit, 0)
+
+    def relay(dest, slot, to, stage, part):
+        chain_copy(dest, dest, to, stage, part).wait_recv()
+        add(partial.at[0, dest, :, spans[part]], chain_in.at[dest, :, spans[part]])
+        chain_copy(dest, slot, to, stage, part).start()
+
+    @pl.when(inner == 0)
+    def _():
+        chain_copy(*farthest, 0).start()
+        chain_copy(*farthest, 1).start()
+        chain_copy(*next_one, 1).start()
+        chain_copy(*nearest, 1).start()
+
+    tokens_all = rows.reshape(rows.shape[0] * rows.shape[1], rows.shape[2])
+    cots_own = cot.reshape(cot.shape[0] * cot.shape[1], D)
+    cots_other = cot_other.reshape(cot.shape[0] * cot.shape[1], D)
+    place = cots_own.shape[0]
+    quarter = D // 4
+
+
+    def up_copy(j):
+        return remote(up_low.at[j], up_in.at[j], grad_send.at[0, j], grad_recv.at[0, j], behind if j == 2 else beside)
+
+    def down_copy(j):
+        return remote(down_low.at[j], down_in.at[j], grad_send.at[1, j], grad_recv.at[1, j], beside if j == 1 else behind)
+
+    def weight_grads(j, carry):
+        across, aside = 1 - j % 2, 1 - j // 2
+        at = (y + across * (1 - 2 * y)) * 2 + x + aside * (1 - 2 * x)
+        span = pl.ds(pl.multiple_of(at * quarter, quarter), quarter)
+        up_low[j] = jnp.dot(
+            pre_turned[...], tokens_all[:, span], preferred_element_type=jnp.float32
+        ).astype(jnp.bfloat16)
+        down_low[j] = (
+            jnp.dot(gated_turned[:, :place], cots_own[:, span], preferred_element_type=jnp.float32)
+            + jnp.dot(gated_turned[:, place:], cots_other[:, span], preferred_element_type=jnp.float32)
+        ).astype(jnp.bfloat16)
+
+        @pl.when(j == 0)
+        def _():
+            up_copy(0).start()
+            down_copy(0).start()
+
+        @pl.when(j == 1)
+        def _():
+            up_copy(1).start()
+
+        @pl.when(j == 2)
+        def _():
+            down_copy(2).start()
+
+        return carry
+
+    def relays(*ways):
+        @pl.when(inner == 1)
+        def _():
+            for way, part in ways:
+                relay(*way, part)
+
+    def forward_copy(at):
+        return remote(forward.at[at], forward_in.at[at], forward_send.at[at], forward_recv.at[at], sibling)
+
+    def forward_block(block, carry):
+        def some(n, inside):
+            span = pl.ds(pl.multiple_of(n * 256, 256), 256)
+            value = jnp.dot(gated[block], down[:, span], preferred_element_type=jnp.float32).astype(jnp.bfloat16)
+
+            @pl.when(block >= 4)
+            def _():
+                forward[block % 4, :, span] = value
+
+            @pl.when(block < 4)
+            def _():
+                forward_out[block % 4, :, span] = value
+
+            return inside
+
+        lax.fori_loop(0, D // 256, some, 0)
+
+        @pl.when(block >= 4)
+        def _():
+            forward_copy(block % 4).start()
+
+        return carry
+
+    relays((next_one, 0))
+    lax.fori_loop(0, 1, weight_grads, 0)
+    relays((farthest, 0))
+    lax.fori_loop(1, 3, weight_grads, 0)
+    relays((farthest, 1), (backward, 0))
+    lax.fori_loop(3, 4, weight_grads, 0)
+    up_copy(0).wait()
+    add(up_low.at[2], up_in.at[0])
+    up_copy(2).start()
+    down_copy(0).wait()
+    add(down_low.at[1], down_in.at[0])
+    down_copy(1).start()
+    lax.fori_loop(4, 8, forward_block, 0)
+    relays((backward, 1), (next_one, 1))
+    lax.fori_loop(0, 4, forward_block, 0)
+    for at in range(4):
+        forward_copy(at).wait()
+        add(forward_out.at[at], forward_in.at[at])
+    up_sum = up_low[3].astype(jnp.float32)
+    down_sum = down_low[3].astype(jnp.float32)
+    for j in (1, 2):
+        up_copy(j).wait()
+        up_sum += up_in[j].astype(jnp.float32)
+        down_copy(j).wait()
+        down_sum += down_in[j].astype(jnp.float32)
+    for e in range(experts):
+        up_out[e] = up_sum[e * hidden : (e + 1) * hidden, :].T
+        down_out[e] = down_sum[e * hidden : (e + 1) * hidden, :]
+
+    for part in range(2):
+        span = spans[part]
+        chain_copy(z, z, z, 0, part).wait_recv()
+        back_out[:, span] = partial[0, z, :, span].astype(jnp.float32) + chain_in[z, :, span].astype(jnp.float32)
+
+        @pl.when(inner == 1)
+        def _():
+            chain_copy(z, 4, z, 0, part).wait_recv()
+            back_out[:, span] = back_out[:, span] + chain_in[4, :, span].astype(jnp.float32)
+
+    for at in range(4):
+        row_copy(0, at).wait_send()
+        cot_copy(at).wait_send()
+        pair_copy(at).wait_send()
+
+        @pl.when((at <= z) & (z < 3))
+        def _():
+            row_copy(1, at).wait_send()
+
+        @pl.when((at >= z) & (z > 0))
+        def _():
+            row_copy(2, at).wait_send()
+
+    for part in range(2):
+
+        @pl.when(inner == 0)
+        def _():
+            chain_copy(z, 0, z, 0, part).wait_send()
+
+        @pl.when(inner == 1)
+        def _():
+            chain_copy(z, 0, z, 2, part).wait_send()
+
+        chain_copy(z, 0, z, 1, part).wait_send()
+        chain_copy(z, 0, z, 3, part).wait_send()
+
+def expert_kernel_visit(sent, cot_line, up, down):
+    tokens = sent.shape[0]
+    experts, _, hidden = up.shape
+    wide = experts * hidden
+    low = jnp.bfloat16
+    vmem = pl.BlockSpec(memory_space=pltpu.VMEM)
+    dma = pltpu.SemaphoreType.DMA
+    f32 = jnp.float32
+    return pl.pallas_call(
+        visit_kernel,
+        out_shape=[
+            jax.ShapeDtypeStruct((tokens, D + 128), f32),
+            jax.ShapeDtypeStruct((experts, D // 4, hidden), f32),
+            jax.ShapeDtypeStruct((experts, hidden, D // 4), f32),
+            jax.ShapeDtypeStruct((4, tokens, D), low),
+        ],
+        in_specs=[vmem] * 4,
+        out_specs=[vmem] * 4,
+        scratch_shapes=[
+            pltpu.VMEM((8, tokens, D + 128), low),
+            pltpu.VMEM((4, tokens, D), low),
+            pltpu.VMEM((D, wide), low),
+            pltpu.VMEM((128, wide), low),
+            pltpu.VMEM((tokens, D), low),
+            pltpu.VMEM((8, tokens, wide), low),
+            pltpu.VMEM((tokens, wide), low),
+            pltpu.VMEM((4, tokens, D), low),
+            pltpu.VMEM((4, tokens, D), low),
+            pltpu.VMEM((wide, 8 * tokens), low),
+            pltpu.VMEM((wide, 8 * tokens), low),
+            pltpu.VMEM((2, 4, tokens, D + 128), low),
+            pltpu.VMEM((4, tokens, D + 128), low),
+            pltpu.VMEM((5, tokens, D + 128), low),
+            pltpu.VMEM((4, wide, D // 4), low),
+            pltpu.VMEM((4, wide, D // 4), low),
+            pltpu.VMEM((3, wide, D // 4), low),
+            pltpu.VMEM((3, wide, D // 4), low),
+            dma((3, 4)), dma((2, 4)), dma((4,)), dma((4,)), dma((4,)), dma((4,)), dma((4,)), dma((4,)), dma((4, 2)), dma((5, 2)), dma((2, 3)), dma((2, 3)),
+        ],
+        compiler_params=pltpu.CompilerParams(collective_id=2, has_side_effects=True, vmem_limit_bytes=58 * 2**20),
+        name="expert_visit",
+    )(sent, cot_line, up, down.reshape(wide, D))
+
+
+def attend_kernel(
+    expert_total, lengths, hidden, cot, value_pick, output_pick, expert_pick, routers, gains,
+    key_weight_at, value_weight_at, query_weight_at, output_weight_at,
+    middle, sent, normed_one, normed_two, queries, key_value, probs, value_all, attended,
+    gates, slopes, cot_line,
+    key_weight, value_weight, query_weight, output_weight, mixed, hot_turned, hot,
+    fetch, pair_send, pair_recv, cot_send, cot_recv, own_sem,
+):
+    dp, ex = lax.axis_index("dp"), lax.axis_index("expert")
+    z, core = ex // 2, ex % 2
+    half = z // 2
+    inner = z + half * (3 - 2 * z)
+    count = hidden.shape[0]
+    width = HEADS * HEAD_DIM
+    low = jnp.bfloat16
+    length = lengths[0]
+    spread = HEADS * VE
+    total = expert_total
+    weights = [
+        pltpu.make_async_copy(source, target, fetch.at[i])
+        for i, (source, target) in enumerate(
+            (
+                (key_weight_at, key_weight),
+                (value_weight_at, value_weight),
+                (query_weight_at, query_weight),
+                (output_weight_at, output_weight),
+            )
+        )
+    ]
+    for made in weights:
+        made.start()
+
+    def at_z(place):
+        return (dp, place * 2 + core)
+
+    barrier = pltpu.get_barrier_semaphore()
+    for k in (1, 2, 3):
+        pl.semaphore_signal(barrier, inc=1, device_id=((dp + k) % 4, ex), device_id_type=MESH)
+
+    @pl.when(z < 3)
+    def _():
+        pl.semaphore_signal(barrier, inc=1, device_id=at_z(z + 1), device_id_type=MESH)
+
+    @pl.when(z > 0)
+    def _():
+        pl.semaphore_signal(barrier, inc=1, device_id=at_z(z - 1), device_id_type=MESH)
+
+    pl.semaphore_wait(barrier, 4 + inner)
+
+    def cot_copy(way, at, source=None):
+        block = cot_line.at[at]
+        return pltpu.make_async_remote_copy(
+            src_ref=block if source is None else source, dst_ref=block,
+            send_sem=cot_send.at[way, at], recv_sem=cot_recv.at[at],
+            device_id=at_z(z + 1 - 2 * way), device_id_type=MESH,
+        )
+
+    def pass_on(distance):
+        @pl.when(z >= distance)
+        def _():
+            cot_copy(0, z - distance).wait_recv()
+
+        @pl.when((z >= distance) & (z < 3))
+        def _():
+            cot_copy(0, z - distance).start()
+
+        @pl.when(z + distance <= 3)
+        def _():
+            cot_copy(1, z + distance).wait_recv()
+
+        @pl.when((z + distance <= 3) & (z > 0))
+        def _():
+            cot_copy(1, z + distance).start()
+
+    @pl.when(z < 3)
+    def _():
+        cot_copy(0, z, cot).start()
+
+    @pl.when(z > 0)
+    def _():
+        cot_copy(1, z, cot).start()
+
+    keep = pltpu.make_async_copy(cot, cot_line.at[z], own_sem)
+    keep.start()
+
+    def norm(field, gain):
+        center = field - jnp.mean(field, axis=-1, keepdims=True)
+        spread = jnp.mean(center * center, axis=-1, keepdims=True)
+        return (center * lax.rsqrt(spread + EPSILON) * gain).astype(low)
+
+    parts = (pl.ds(0, width), pl.ds(width, width))
+
+    def pair_copy(step, part, block):
+        return pltpu.make_async_remote_copy(
+            src_ref=key_value.at[block, :, parts[part]], dst_ref=key_value.at[block, :, parts[part]],
+            send_sem=pair_send.at[step, part], recv_sem=pair_recv.at[block, part],
+            device_id=((dp + step) % 4, ex), device_id_type=MESH,
+        )
+
+    def send_part(part):
+        for step in (1, 2, 3):
+
+            @pl.when(dp + step < 4)
+            def _():
+                pair_copy(step, part, dp).start()
+
+    normed_one[...] = norm(hidden[...].astype(jnp.float32), gains[0:1, :])
+    weights[0].wait()
+    key_value[dp, :, parts[0]] = jnp.dot(
+        normed_one[...], key_weight[...], preferred_element_type=jnp.float32
+    ).astype(low)
+    send_part(0)
+
+    hot_turned[...] = jnp.zeros(hot_turned.shape, jnp.float32)
+
+    def mark(picks, base, size):
+        place = lax.broadcasted_iota(jnp.int32, (size, count), 0)
+        found = jnp.zeros((size, count), jnp.float32)
+        for pick in picks:
+            found = jnp.where(place == pick, 1.0, found)
+        hot_turned[base : base + size, :] = found
+
+    mark([value_pick[h, i : i + 1, :] + h * VE for h in range(HEADS) for i in range(value_pick.shape[1])], 0, spread)
+    mark(
+        [output_pick[h, i : i + 1, :] + h * VE for h in range(HEADS) for i in range(output_pick.shape[1])],
+        spread,
+        spread,
+    )
+    mark([expert_pick[i : i + 1, :] for i in range(expert_pick.shape[0])], 2 * spread, total)
+    hot[...] = hot_turned[...].T
+    sig = jax.nn.sigmoid(dot_last(normed_one[...], routers[...]))
+    gates[...] = sig * hot[...]
+    slopes[...] = gates[...] * (1.0 - sig)
+    weights[1].wait()
+
+    def values(n, carry):
+        span = pl.ds(pl.multiple_of(n * 256, 256), 256)
+        value_all[:, span] = jnp.dot(
+            hidden[...], value_weight[:, span], preferred_element_type=jnp.float32
+        ).astype(low)
+        return carry
+
+    lax.fori_loop(0, HEADS * VE * HEAD_DIM // 256, values, 0)
+    for h in range(HEADS):
+        row = jnp.zeros((count, HEAD_DIM), jnp.float32)
+        for e in range(h * VE, (h + 1) * VE):
+            row += gates[:, e : e + 1] * value_all[:, e * HEAD_DIM : (e + 1) * HEAD_DIM].astype(jnp.float32)
+        key_value[dp, :, width + h * HEAD_DIM : width + (h + 1) * HEAD_DIM] = row.astype(low)
+    send_part(1)
+
+    weights[2].wait()
+    queries[...] = jnp.dot(normed_one[...], query_weight[...], preferred_element_type=jnp.float32).astype(low)
+    for block in range(4):
+
+        @pl.when(block > dp)
+        def _():
+            key_value[block] = jnp.zeros((count, 2 * width), low)
+
+    pass_on(1)
+
+    def wait_part(part):
+        for block in range(3):
+
+            @pl.when(block < dp)
+            def _():
+                pair_copy(1, part, block).wait_recv()
+
+    wait_part(0)
+    pair_all = key_value.reshape(4 * count, 2 * width)
+    query_pos = dp * count + lax.broadcasted_iota(jnp.int32, (count, 4 * count), 0)
+    key_pos = lax.broadcasted_iota(jnp.int32, (count, 4 * count), 1)
+    allowed = (key_pos <= query_pos) & (key_pos < length)
+
+    def score(h, carry):
+        span = pl.ds(pl.multiple_of(h * HEAD_DIM, HEAD_DIM), HEAD_DIM)
+        raw = dot_last(queries[:, span], pair_all[:, span])
+        scores = jnp.where(allowed, raw * HEAD_DIM ** (-0.5), NEGATIVE)
+        terms = jnp.exp(scores - jnp.max(scores, axis=-1, keepdims=True))
+        probs[h] = (terms * (1.0 / jnp.sum(terms, axis=-1, keepdims=True))).astype(low)
+        return carry
+
+    lax.fori_loop(0, HEADS, score, 0)
+    wait_part(1)
+    pass_on(2)
+
+    def collect(h, carry):
+        span = pl.ds(pl.multiple_of(h * HEAD_DIM, HEAD_DIM), HEAD_DIM)
+        value_span = pl.ds(pl.multiple_of(width + h * HEAD_DIM, HEAD_DIM), HEAD_DIM)
+        attended[:, span] = jnp.dot(probs[h], pair_all[:, value_span], preferred_element_type=jnp.float32)
+        return carry
+
+    lax.fori_loop(0, HEADS, collect, 0)
+    for h in range(HEADS):
+        row = attended[:, h * HEAD_DIM : (h + 1) * HEAD_DIM]
+        for e in range(h * VE, (h + 1) * VE):
+            mixed[:, e * HEAD_DIM : (e + 1) * HEAD_DIM] = (gates[:, spread + e : spread + e + 1] * row).astype(low)
+
+    place = dp * count + lax.broadcasted_iota(jnp.int32, (count, 1), 0)
+    live = jnp.where(place < length, 1.0, 0.0)
+    weights[3].wait()
+
+    def outward(n, carry):
+        span = pl.ds(pl.multiple_of(n * 256, 256), 256)
+        branch = jnp.dot(mixed[...], output_weight[:, span], preferred_element_type=jnp.float32)
+        middle[:, span] = hidden[:, span].astype(jnp.float32) + live * branch
+        return carry
+
+    lax.fori_loop(0, D // 256, outward, 0)
+    sent[:, :D] = middle[...].astype(low)
+    normed_two[...] = norm(middle[...], gains[1:2, :])
+    sig = jax.nn.sigmoid(dot_last(normed_two[...], routers[...]))
+    gate = sig * hot[...] * live
+    sent[:, D:] = gate.astype(low)
+    lane = lax.broadcasted_iota(jnp.int32, (count, 128), 1)
+    slopes[...] = jnp.where(lane < 2 * spread, slopes[...], gate * (1.0 - sig))
+
+    pass_on(3)
+    keep.wait()
+    for part in range(2):
+        for step in (1, 2, 3):
+
+            @pl.when(dp + step < 4)
+            def _():
+                pair_copy(step, part, dp).wait_send()
+
+    for at in range(4):
+
+        @pl.when((at <= z) & (z < 3))
+        def _():
+            cot_copy(0, at).wait_send()
+
+        @pl.when((at >= z) & (z > 0))
+        def _():
+            cot_copy(1, at).wait_send()
+
+
+def attend(total, lengths, *operands):
+    count = operands[0].shape[0]
+    low, full = jnp.bfloat16, jnp.float32
+    vmem = pl.BlockSpec(memory_space=pltpu.VMEM)
+    anywhere = pl.BlockSpec(memory_space=pl.ANY)
+    dma = pltpu.SemaphoreType.DMA
+    width, wide = HEADS * HEAD_DIM, HEADS * VE * HEAD_DIM
+    shapes = [
+        ((count, D), full),
+        ((count, D + 128), low),
+        ((count, D), low),
+        ((count, D), low),
+        ((count, width), low),
+        ((4, count, 2 * width), low),
+        ((HEADS, count, 4 * count), low),
+        ((count, wide), low),
+        ((count, width), full),
+        ((count, 128), full),
+        ((count, 128), full),
+        ((4, count, D), low),
+    ]
+    return pl.pallas_call(
+        functools.partial(attend_kernel, total),
+        out_shape=[jax.ShapeDtypeStruct(*shape) for shape in shapes],
+        in_specs=[pl.BlockSpec(memory_space=pltpu.SMEM)] + [vmem] * (len(operands) - 4) + [anywhere] * 4,
+        out_specs=[vmem] * len(shapes),
+        scratch_shapes=[pltpu.VMEM(a.shape, a.dtype) for a in operands[-4:]]
+        + [
+            pltpu.VMEM((count, wide), low),
+            pltpu.VMEM((128, count), full),
+            pltpu.VMEM((count, 128), full),
+            dma((4,)),
+            dma((4, 2)),
+            dma((4, 2)),
+            dma((2, 4)),
+            dma((4,)),
+            dma,
+        ],
+        compiler_params=pltpu.CompilerParams(
+            collective_id=1, has_side_effects=True, vmem_limit_bytes=58 * 2**20
+        ),
+        name="attend",
+    )(lengths, *operands)
+
+
+def backward_kernel(
+    total_experts, lengths, gates, slopes, routers, gains,
+    forward_at, returned_at, middle_at, cot_at, hidden_at, normed_one_at, queries_at, key_value_at, probs_at, value_all_at,
+    attended_at, normed_two_at, query_weight_at, key_weight_at, value_weight_at, output_weight_at,
+    block_out, grad_in, out_query, out_key, out_value, out_output, out_small, sums_out,
+    forward, returned, middle, cot, hidden, normed_one, queries, key_value, probs, value_all,
+    attended, normed_two, query_weight, key_weight, value_part, output_part,
+    branch, branch_turned, one_turned, hidden_turned, grad_att, grad_query, leave, arrive, grad_key,
+    grad_each, grad_middle, grad_one, logit_one, logit_two, small_turned, mixed,
+    grads, grads_small, core_in, plane_in, last_in, sums_in, forward_in,
+    fetch, part_fetch, leave_send, leave_recv, send, recv, forward_send, forward_recv,
+):
+    dp, ex = lax.axis_index("dp"), lax.axis_index("expert")
+    y, x, z, core = dp // 2, dp % 2, ex // 2, ex % 2
+    count = hidden.shape[0]
+    width = HEADS * HEAD_DIM
+    low, full = jnp.bfloat16, jnp.float32
+    length = lengths[0]
+    sibling = (dp, z * 2 + 1 - core)
+    beside = (y * 2 + 1 - x, ex)
+    behind = ((1 - y) * 2 + x, ex)
+    across = ((1 - y) * 2 + 1 - x, ex)
+    line = [(dp, ((z + k) % 4) * 2 + core) for k in (1, 2, 3)]
+    barrier = pltpu.get_barrier_semaphore()
+    for place in (sibling, beside, behind, across, *line):
+        pl.semaphore_signal(barrier, inc=1, device_id=place, device_id_type=MESH)
+
+    held = dict(
+        forward=(forward_at, forward),
+        returned=(returned_at, returned),
+        middle=(middle_at, middle),
+        cot=(cot_at, cot),
+        hidden=(hidden_at, hidden),
+        attended=(attended_at, attended),
+        key_value=(key_value_at, key_value),
+        probs=(probs_at, probs),
+        queries=(queries_at, queries),
+        normed_one=(normed_one_at, normed_one),
+        query_weight=(query_weight_at, query_weight),
+        value_all=(value_all_at, value_all),
+        key_weight=(key_weight_at, key_weight),
+        normed_two=(normed_two_at, normed_two),
+    )
+    got = {
+        name: pltpu.make_async_copy(source, target, fetch.at[i])
+        for i, (name, (source, target)) in enumerate(held.items())
+    }
+
+    def output_copy(n):
+        return pltpu.make_async_copy(
+            output_weight_at.at[pl.ds(n * PIECE, PIECE)], output_part.at[n % 2], part_fetch.at[0, n % 2]
+        )
+
+    def value_copy(n):
+        return pltpu.make_async_copy(
+            value_weight_at.at[:, pl.ds(n * PIECE, PIECE)], value_part.at[n % 2], part_fetch.at[1, n % 2]
+        )
+
+    first_held = ("forward", "returned", "middle", "cot", "hidden")
+    for name in first_held:
+        got[name].start()
+    for n in range(2):
+        output_copy(n).start()
+    for name in held:
+        if name not in first_held:
+            got[name].start()
+    for n in range(2):
+        value_copy(n).start()
+
+    pieces = (
+        [(out_output, PIECE * n, PIECE, n) for n in range(HEADS)]
+        + [(out_query, 0, width, 4)]
+        + [(out_value, PIECE * n, PIECE, n) for n in range(HEADS)]
+        + [(out_key, 0, width, 5), (out_small, 0, 128, None)]
+    )
+    along_line = (0, 1)
+    in_plane = [i for i in range(len(pieces)) if i not in along_line]
+    x_first = {i: n % 2 == 0 for n, i in enumerate(in_plane)}
+
+    def remote(source, target, slot, place):
+        return pltpu.make_async_remote_copy(
+            src_ref=source, dst_ref=target, send_sem=send.at[slot], recv_sem=recv.at[slot],
+            device_id=place, device_id_type=MESH,
+        )
+
+    def add(target, source):
+        target[...] = (target[...].astype(full) + source[...].astype(full)).astype(target.dtype)
+
+    def own(i):
+        slot = pieces[i][3]
+        return grads_small if slot is None else grads.at[slot, :, :, :, :, columns(i)]
+
+    def columns(i):
+        return pl.ds(0, pieces[i][2])
+
+    started = {}
+
+    def begin(key, source, target, slot, place):
+        started[key] = remote(source, target, slot, place)
+        started[key].start()
+
+    def halve_core(i):
+        begin((i, 0), own(i).at[:, :, 1 - core], core_in.at[i, :, :, :, columns(i)], (i, 0), sibling)
+
+    def halve_near(i):
+        span = columns(i)
+        started[i, 0].wait()
+        add(core_in.at[i, :, :, :, span], own(i).at[:, :, core])
+        if i in along_line:
+            for k in (1, 2, 3):
+                begin(
+                    (i, k), core_in.at[i, :, (z + k) % 4, :, span],
+                    plane_in.at[i, pl.ds(4 * k - 4, 4), :, span], (i, k), line[k - 1],
+                )
+            return
+        for part in range(2):
+            if x_first[i]:
+                source = core_in.at[i, part * 2 + 1 - x, :, :, span]
+            else:
+                source = core_in.at[i, (1 - y) * 2 + part, :, :, span]
+            target = plane_in.at[i, pl.ds(part * 4, 4), :, span]
+            begin((i, 1 + part), source, target, (i, 1 + part), beside if x_first[i] else behind)
+
+    def halve_far(i):
+        span = columns(i)
+        if i in along_line:
+            held = core_in.at[i, :, z, :, span]
+            for k in (1, 2, 3):
+                started[i, k].wait()
+                add(held, plane_in.at[i, pl.ds(4 * k - 4, 4), :, span])
+            for part in range(2):
+                begin(
+                    (i, 4 + part), core_in.at[i, part * 2 + 1 - x, z, :, span],
+                    last_in.at[i, part, :, span], (i, 4 + part), beside,
+                )
+            return
+        for part in range(2):
+            started[i, 1 + part].wait()
+            kept = part * 2 + x if x_first[i] else y * 2 + part
+            add(plane_in.at[i, pl.ds(part * 4, 4), :, span], core_in.at[i, kept, :, :, span])
+        other = 1 - y if x_first[i] else 1 - x
+        begin(
+            (i, 3), plane_in.at[i, pl.ds(other * 4, 4), :, span], plane_in.at[i, pl.ds(8, 4), :, span],
+            (i, 3), behind if x_first[i] else beside,
+        )
+
+    def spread(i):
+        span = columns(i)
+        if i in along_line:
+            for part in range(2):
+                started[i, 4 + part].wait()
+                add(last_in.at[i, part, :, span], core_in.at[i, part * 2 + x, z, :, span])
+            begin((i, 6), last_in.at[i, 1 - y, :, span], last_in.at[i, 2, :, span], (i, 6), behind)
+            return
+        started[i, 3].wait()
+        add(plane_in.at[i, pl.ds(8, 4), :, span], plane_in.at[i, pl.ds((y if x_first[i] else x) * 4, 4), :, span])
+        for k in (1, 2, 3):
+            begin(
+                (i, 3 + k), plane_in.at[i, 8 + (z + k) % 4, :, span],
+                last_in.at[i, k - 1, :, span], (i, 3 + k), line[k - 1],
+            )
+
+    def finish(i):
+        out, start, size, _ = pieces[i]
+        span = columns(i)
+        if i in along_line:
+            started[i, 6].wait()
+            total = last_in[i, y, :, span].astype(full) + last_in[i, 2, :, span].astype(full)
+        else:
+            total = plane_in[i, 8 + z, :, span].astype(full)
+            for k in (1, 2, 3):
+                started[i, 3 + k].wait()
+                total = total + last_in[i, k - 1, :, span].astype(full)
+        out[:, pl.ds(start, size)] = total
+
+    rows_each = 64
+    lane = lax.broadcasted_iota(jnp.int32, (1, 128), 1)
+    for name in first_held:
+        got[name].wait()
+    logit_two[...] = (returned[:, D:] * slopes[...]).astype(low)
+
+    half = z // 2
+    inner = z + half * (3 - 2 * z)
+    onward = 1 - 2 * half
+    nearest = (z + onward, z + onward, z + onward, 0)
+    farthest = (3 * (1 - half), 3 * (1 - half), z + onward, 1)
+    backward = (3 * half, 3 * half, z - onward, 2)
+    next_one = (2 - half, 2 - half + inner * (2 + half), z + onward, 3)
+
+    def forward_copy(dest, slot, to, stage, part):
+        span = pl.ds(part * (D // 2), D // 2)
+        return pltpu.make_async_remote_copy(
+            src_ref=forward.at[dest, :, span], dst_ref=forward_in.at[slot, :, span],
+            send_sem=forward_send.at[stage, part], recv_sem=forward_recv.at[slot, part],
+            device_id=(dp, to * 2 + core), device_id_type=MESH,
+        )
+
+    def relays(*ways):
+        @pl.when(inner == 1)
+        def _():
+            for (dest, slot, to, stage), part in ways:
+                span = pl.ds(part * (D // 2), D // 2)
+                forward_copy(dest, dest, to, stage, part).wait_recv()
+                add(forward.at[dest, :, span], forward_in.at[dest, :, span])
+                forward_copy(dest, slot, to, stage, part).start()
+
+    pl.semaphore_wait(barrier, 7)
+
+    @pl.when(inner == 0)
+    def _():
+        for way in (farthest, next_one, nearest):
+            for part in range(2):
+                forward_copy(*way, part).start()
+
+    def live_rows(start):
+        place = dp * count + start + lax.broadcasted_iota(jnp.int32, (rows_each, 1), 0)
+        return jnp.where(place < length, 1.0, 0.0)
+
+    def norm_back(field, grad, gain):
+        center = field - jnp.mean(field, axis=-1, keepdims=True)
+        scale = lax.rsqrt(jnp.mean(center * center, axis=-1, keepdims=True) + EPSILON)
+        unit = center * scale
+        part = grad * gain
+        back = scale * (
+            part
+            - jnp.mean(part, axis=-1, keepdims=True)
+            - unit * jnp.mean(part * unit, axis=-1, keepdims=True)
+        )
+        return back, jnp.sum(grad * unit, axis=0, keepdims=True)
+
+    def first_rows(n, gain_sum):
+        start = pl.multiple_of(n * rows_each, rows_each)
+        rows = pl.ds(start, rows_each)
+        grad = jnp.dot(logit_two[rows, :], routers[...], preferred_element_type=full)
+        back, gain_part = norm_back(middle[rows, :], grad, gains[1:2, :])
+        total = cot[rows, :].astype(full) + returned[rows, :D] + back
+        grad_middle[rows, :] = total
+        branch[rows, :] = (live_rows(start) * total).astype(low)
+        return gain_sum + gain_part
+
+    gain_two_sum = lax.fori_loop(0, count // rows_each, first_rows, jnp.zeros((1, D), full))
+    relays((farthest, 0))
+
+    def square(field, live, at):
+        total = jnp.sum(jnp.sum(field * field, axis=1, keepdims=True) * live, axis=0, keepdims=True)
+        return jnp.where(lane == at, total, 0.0)
+
+    def last_rows(n, sums):
+        start = pl.multiple_of(n * rows_each, rows_each)
+        rows = pl.ds(start, rows_each)
+        live = live_rows(start)
+        field = middle[rows, :]
+        step = forward[z, rows, :].astype(full)
+        final = field + step
+        block_out[rows, :] = final.astype(low)
+        source = hidden[rows, :].astype(full)
+        one = jnp.ones((rows_each, 1), full)
+        sums += square(source, live, 0) + square(field - source, one, 1)
+        sums += square(step, one, 2) + square(final, live, 3)
+        return sums + jnp.where(lane == 4, jnp.sum(live, axis=0, keepdims=True), 0.0)
+
+    def output_rows():
+        for part in range(2):
+            span = pl.ds(part * (D // 2), D // 2)
+            forward_copy(z, z, z, 0, part).wait_recv()
+            add(forward.at[z, :, span], forward_in.at[z, :, span])
+
+            @pl.when(inner == 1)
+            def _():
+                forward_copy(z, 4, z, 0, part).wait_recv()
+                add(forward.at[z, :, span], forward_in.at[4, :, span])
+
+        sums = lax.fori_loop(0, count // rows_each, last_rows, jnp.zeros((1, 128), full))
+        sums_in[0] = jnp.broadcast_to(sums, (8, 128))
+
+    def weight_grad(i, turned, right):
+        def some(n, carry):
+            rows = pl.ds(pl.multiple_of(n * 256, 256), 256)
+            value = jnp.dot(turned[rows, :], right, preferred_element_type=full).astype(low)
+            own(i)[n] = value.reshape(4, 2, ROWS, pieces[i][2])
+            return carry
+
+        lax.fori_loop(0, D // 256, some, 0)
+        halve_core(i)
+
+    got["attended"].wait()
+    spread_count = HEADS * VE
+
+    def head_of(c):
+        return slice((c // VE) * HEAD_DIM, (c // VE + 1) * HEAD_DIM)
+
+    logit_one[...] = jnp.zeros(logit_one.shape, full)
+    grad_att[...] = jnp.zeros(grad_att.shape, full)
+    for n in range(HEADS):
+        output_copy(n).wait()
+        for j in range(VE):
+            c = VE * n + j
+            grad_mixed = dot_last(branch[...], output_part[n % 2, j * HEAD_DIM : (j + 1) * HEAD_DIM, :])
+            col = spread_count + c
+            grad_att[:, head_of(c)] += gates[:, col : col + 1] * grad_mixed
+            dots = jnp.sum(attended[:, head_of(c)] * grad_mixed, axis=1, keepdims=True)
+            logit_one[:, col : col + 1] = dots * slopes[:, col : col + 1]
+        if n + 2 < HEADS:
+            output_copy(n + 2).start()
+    relays((farthest, 1), (backward, 0))
+
+    pair_all = key_value.reshape(4 * count, 2 * width)
+    for name in ("key_value", "probs", "queries"):
+        got[name].wait()
+
+    def leave_copy(k, h):
+        rows = pl.ds(h * 2 * HEAD_DIM, 2 * HEAD_DIM)
+        return pltpu.make_async_remote_copy(
+            src_ref=leave.at[(dp + 4 - k) % 4, rows], dst_ref=arrive.at[k - 1, rows],
+            send_sem=leave_send.at[k - 1, h], recv_sem=leave_recv.at[k - 1, h],
+            device_id=((dp + 4 - k) % 4, ex), device_id_type=MESH,
+        )
+
+    def head(h, carry):
+        start = pl.multiple_of(h * HEAD_DIM, HEAD_DIM)
+        span = pl.ds(start, HEAD_DIM)
+        grad = grad_att[:, span].astype(low)
+        prob = probs[h].astype(full)
+        grad_prob = dot_last(grad, pair_all[:, pl.ds(width + start, HEAD_DIM)])
+        dots = jnp.sum(prob * grad_prob, axis=-1, keepdims=True)
+        grad_score = (prob * (grad_prob - dots) * HEAD_DIM ** (-0.5)).astype(low)
+        grad_query[:, span] = jnp.dot(grad_score, pair_all[:, span], preferred_element_type=full).astype(low)
+        key_part = dot_first(queries[:, span], grad_score).astype(low)
+        value_part_all = dot_first(grad, probs[h]).astype(low)
+        key_rows = pl.ds(pl.multiple_of(2 * h * HEAD_DIM, 2 * HEAD_DIM), HEAD_DIM)
+        value_rows = pl.ds(pl.multiple_of((2 * h + 1) * HEAD_DIM, HEAD_DIM), HEAD_DIM)
+        for j in range(4):
+            leave[j, key_rows, :] = key_part[:, j * count : (j + 1) * count]
+            leave[j, value_rows, :] = value_part_all[:, j * count : (j + 1) * count]
+        for k in (1, 2, 3):
+
+            @pl.when(dp >= k)
+            def _():
+                leave_copy(k, h).start()
+
+        return carry
+
+    lax.fori_loop(0, HEADS, head, 0)
+
+    relays((backward, 1), (next_one, 0), (next_one, 1))
+    branch_turned[...] = branch[...].T
+    for n in range(HEADS):
+        for j in range(VE):
+            c = VE * n + j
+            gate = gates[:, spread_count + c : spread_count + c + 1]
+            mixed[:, j * HEAD_DIM : (j + 1) * HEAD_DIM] = (gate * attended[:, head_of(c)]).astype(low)
+        weight_grad(n, branch_turned, mixed[...])
+        if n:
+            halve_near(n - 1)
+    for name in ("normed_one", "query_weight"):
+        got[name].wait()
+    one_turned[...] = normed_one[...].T
+    weight_grad(4, one_turned, grad_query[...])
+    halve_near(3)
+    hidden_turned[...] = hidden[...].T
+    grad_one[...] = dot_last(grad_query[...], query_weight[...])
+    halve_near(4)
+    got["value_all"].wait()
+
+    for h in range(HEADS):
+        rows = pl.ds(h * 2 * HEAD_DIM, 2 * HEAD_DIM)
+        total = leave[dp, rows, :].astype(full)
+        for k in (1, 2, 3):
+
+            @pl.when(dp + k < 4)
+            def _():
+                leave_copy(k, h).wait_recv()
+
+            @pl.when(dp + k >= 4)
+            def _():
+                arrive[k - 1, rows, :] = jnp.zeros((2 * HEAD_DIM, count), low)
+
+            total += arrive[k - 1, rows, :].astype(full)
+        turned = total.T
+        grad_key[:, h * HEAD_DIM : (h + 1) * HEAD_DIM] = turned[:, :HEAD_DIM].astype(low)
+        grad = turned[:, HEAD_DIM:].astype(low).astype(full)
+        for c in range(h * VE, (h + 1) * VE):
+            here = slice(c * HEAD_DIM, (c + 1) * HEAD_DIM)
+            grad_each[:, here] = (gates[:, c : c + 1] * grad).astype(low)
+            dots = jnp.sum(value_all[:, here].astype(full) * grad, axis=1, keepdims=True)
+            logit_one[:, c : c + 1] = dots * slopes[:, c : c + 1]
+        weight_grad(5 + h, hidden_turned, grad_each[:, h * PIECE : (h + 1) * PIECE])
+        if h:
+            halve_near(4 + h)
+    weight_grad(9, one_turned, grad_key[...])
+    halve_near(8)
+    got["key_weight"].wait()
+    grad_one[...] += dot_last(grad_key[...], key_weight[...])
+    halve_near(9)
+    halve_far(2)
+    grad_one[...] += jnp.dot(logit_one[...].astype(low), routers[...], preferred_element_type=full)
+
+    def first_norm(n, gain_sum):
+        rows = pl.ds(pl.multiple_of(n * rows_each, rows_each), rows_each)
+        back, gain_part = norm_back(hidden[rows, :].astype(full), grad_one[rows, :], gains[0:1, :])
+        grad_in[rows, :] = grad_middle[rows, :] + back
+        return gain_sum + gain_part
+
+    gain_one_sum = lax.fori_loop(0, count // rows_each, first_norm, jnp.zeros((1, D), full))
+    halve_far(3)
+    got["normed_two"].wait()
+    small_turned[...] = dot_first(logit_one[...].astype(low), normed_one[...]) + dot_first(
+        logit_two[...], normed_two[...]
+    )
+    small_rows = 2 * spread_count + total_experts
+    small_turned[small_rows : small_rows + 1, :] = gain_one_sum
+    small_turned[small_rows + 1 : small_rows + 2, :] = gain_two_sum
+    grads_small[...] = small_turned[...].T.astype(low).reshape(grads_small.shape)
+    halve_core(10)
+    spread(2)
+    halve_far(4)
+    output_rows()
+
+    rounds = [[sibling], [beside], [behind], line]
+    offset = [1, 2, 3, 4]
+
+    def sum_start(r):
+        for j, place in enumerate(rounds[r]):
+            begin(("sum", r, j), sums_in.at[0], sums_in.at[offset[r] + j], (len(pieces) + j, r), place)
+
+    def sum_end(r):
+        for j in range(len(rounds[r])):
+            started["sum", r, j].wait()
+        total = sums_in[0]
+        for j in range(len(rounds[r])):
+            total = total + sums_in[offset[r] + j]
+        sums_in[0] = total
+
+    def value_side(n):
+        value_copy(n).wait()
+        grad_in[...] += dot_last(grad_each[:, n * PIECE : (n + 1) * PIECE], value_part[n % 2])
+        if n + 2 < HEADS:
+            value_copy(n + 2).start()
+
+    for action, i in (
+        (sum_start, 0), (halve_near, 10), (spread, 3),
+        (value_side, 0), (sum_end, 0), (sum_start, 1), (halve_far, 5), (halve_far, 0), (spread, 4), (finish, 2),
+        (value_side, 1), (sum_end, 1), (sum_start, 2), (halve_far, 6), (spread, 0), (finish, 3), (spread, 5),
+        (value_side, 2), (sum_end, 2), (sum_start, 3), (halve_far, 7), (finish, 4), (spread, 6),
+        (value_side, 3), (finish, 0), (halve_far, 1), (halve_far, 8), (finish, 5), (spread, 7), (sum_end, 3),
+        (spread, 1), (halve_far, 9), (finish, 6), (spread, 8), (halve_far, 10), (finish, 7), (finish, 1), (spread, 9),
+        (spread, 10), (finish, 8), (finish, 9), (finish, 10),
+    ):
+        action(i)
+    sums_out[...] = sums_in[0]
+    for h in range(HEADS):
+        for k in (1, 2, 3):
+
+            @pl.when(dp >= k)
+            def _():
+                leave_copy(k, h).wait_send()
+
+    for part in range(2):
+        forward_copy(z, 0, z, 1, part).wait_send()
+        forward_copy(z, 0, z, 3, part).wait_send()
+
+        @pl.when(inner == 0)
+        def _():
+            forward_copy(z, 0, z, 0, part).wait_send()
+
+        @pl.when(inner == 1)
+        def _():
+            forward_copy(z, 0, z, 2, part).wait_send()
+
+
+def backward(total_experts, lengths, gates, slopes, routers, gains, *arrays):
+    low, full = jnp.bfloat16, jnp.float32
+    count = gates.shape[0]
+    width, wide = HEADS * HEAD_DIM, HEADS * VE * HEAD_DIM
+    vmem = pl.BlockSpec(memory_space=pltpu.VMEM)
+    anywhere = pl.BlockSpec(memory_space=pl.ANY)
+    dma = pltpu.SemaphoreType.DMA
+    whole = [pltpu.VMEM(a.shape, a.dtype) for a in arrays[:14]]
+    n = 11
+    return pl.pallas_call(
+        functools.partial(backward_kernel, total_experts),
+        out_shape=[
+            jax.ShapeDtypeStruct((count, D), low),
+            jax.ShapeDtypeStruct((count, D), full),
+            jax.ShapeDtypeStruct((ROWS, width), full),
+            jax.ShapeDtypeStruct((ROWS, width), full),
+            jax.ShapeDtypeStruct((ROWS, wide), full),
+            jax.ShapeDtypeStruct((ROWS, wide), full),
+            jax.ShapeDtypeStruct((ROWS, 128), full),
+            jax.ShapeDtypeStruct((8, 128), full),
+        ],
+        in_specs=[pl.BlockSpec(memory_space=pltpu.SMEM)] + [vmem] * 4 + [anywhere] * len(arrays),
+        out_specs=[vmem] * 8,
+        scratch_shapes=whole
+        + [
+            pltpu.VMEM((2, D, PIECE), low),
+            pltpu.VMEM((2, PIECE, D), low),
+            pltpu.VMEM((count, D), low),
+            pltpu.VMEM((D, count), low),
+            pltpu.VMEM((D, count), low),
+            pltpu.VMEM((D, count), low),
+            pltpu.VMEM((count, width), full),
+            pltpu.VMEM((count, width), low),
+            pltpu.VMEM((4, 2 * width, count), low),
+            pltpu.VMEM((3, 2 * width, count), low),
+            pltpu.VMEM((count, width), low),
+            pltpu.VMEM((count, wide), low),
+            pltpu.VMEM((count, D), full),
+            pltpu.VMEM((count, D), full),
+            pltpu.VMEM((count, 128), full),
+            pltpu.VMEM((count, 128), low),
+            pltpu.VMEM((128, D), full),
+            pltpu.VMEM((count, PIECE), low),
+            pltpu.VMEM((6, 4, 4, 2, ROWS, PIECE), low),
+            pltpu.VMEM((4, 4, 2, ROWS, 128), low),
+            pltpu.VMEM((n, 4, 4, ROWS, PIECE), low),
+            pltpu.VMEM((n, 12, ROWS, PIECE), low),
+            pltpu.VMEM((n, 3, ROWS, PIECE), low),
+            pltpu.VMEM((7, 8, 128), full),
+            pltpu.VMEM((5, count, D), low),
+            dma((14,)),
+            dma((2, 2)),
+            dma((3, HEADS)),
+            dma((3, HEADS)),
+            dma((n + 3, 7)),
+            dma((n + 3, 7)),
+            dma((4, 2)),
+            dma((5, 2)),
+        ],
+        compiler_params=pltpu.CompilerParams(
+            collective_id=3, has_side_effects=True, vmem_limit_bytes=62 * 2**20
+        ),
+        name="backward",
+    )(lengths, gates, slopes, routers, gains, *arrays)
 
 
 def expert_visit(sent, cotangent, expert_up, expert_down):
@@ -160,33 +1364,33 @@
         returned, grad_up, grad_down = expert_visit(*item, expert_up, expert_down)
         return (grads[0] + grad_up, grads[1] + grad_down), returned
 
-    if rounds == 1:
-        returned, grad_up, grad_down = expert_visit(sent, cotangent[0], expert_up, expert_down)
-    else:
-        zeros = jnp.zeros(expert_up.shape, jnp.float32), jnp.zeros(expert_down.shape, jnp.float32)
-        (grad_up, grad_down), returned = lax.scan(
-            visit,
-            zeros,
-            (
-                sent.reshape(rounds, -1, sent.shape[1]),
-                cotangent[0].reshape(rounds, -1, D),
-            ),
-        )
-        returned = returned.reshape(row_count, -1)
-    returned = returned.astype(jnp.float32)
+    zeros = jnp.zeros(expert_up.shape, jnp.float32), jnp.zeros(expert_down.shape, jnp.float32)
+    (up_grad, down_grad), returned = lax.scan(
+        visit,
+        zeros,
+        (
+            sent.reshape(rounds, -1, sent.shape[1]),
+            cotangent[0].reshape(rounds, -1, D),
+        ),
+    )
+    returned = returned.reshape(row_count, -1).astype(jnp.float32)
+    up_grad = lax.psum_scatter(
+        up_grad.astype(jnp.bfloat16), "dp", scatter_dimension=1, tiled=True
+    ).astype(jnp.float32)
+    down_grad = lax.psum_scatter(
+        down_grad.astype(jnp.bfloat16), "dp", scatter_dimension=2, tiled=True
+    ).astype(jnp.float32)
     feedforward_out = returned[:, :D]
     final_rows = middle + feedforward_out
-    total_sums = lax.psum(
-        (
+    sums = jnp.stack(
+        [
             jnp.sum(live_mask * input_full * input_full),
             jnp.sum(attention_out * attention_out),
             jnp.sum(feedforward_out * feedforward_out),
             jnp.sum(live_mask * final_rows * final_rows),
             jnp.sum(live_mask),
-        ),
-        ("dp", "expert"),
-    )
-    residual_norms = jnp.sqrt(jnp.stack(total_sums[:4]) / (total_sums[4] * D))
+        ]
+    )
     grad_final = cotangent[0].astype(jnp.float32)
     grad_middle = grad_final + returned[:, D : 2 * D]
     grad_logit = (
@@ -279,39 +1483,47 @@
         + jnp.einsum("tm,dm->td", grad_value_each, value_weight, preferred_element_type=jnp.float32)
         + grad_input_norm
     )
-    parts = (
-        grad_query_weight,
-        grad_key_weight,
-        grad_value_weight,
-        grad_output_weight,
-        grad_value_router,
-        grad_output_router,
-        grad_expert_router,
-        grad_gain_one[:, None],
-        grad_gain_two[:, None],
-    )
+    small_grads = jnp.concatenate(
+        [
+            grad_value_router,
+            grad_output_router,
+            grad_expert_router,
+            grad_gain_one[:, None],
+            grad_gain_two[:, None],
+        ],
+        axis=1,
+    )
+    small_count = small_grads.shape[1]
+    small_grads = jnp.pad(small_grads, ((0, 0), (0, -small_count % 128)))
+    low_grads = [
+        part.astype(jnp.bfloat16)
+        for part in (
+            grad_query_weight,
+            grad_key_weight,
+            grad_value_weight,
+            grad_output_weight,
+            small_grads,
+        )
+    ]
     summed = lax.psum_scatter(
-        jnp.concatenate([part.astype(jnp.bfloat16) for part in parts], axis=1),
-        ("dp", "expert"),
-        scatter_dimension=0,
-        tiled=True,
+        jnp.concatenate(low_grads, axis=1), ("dp", "expert"), scatter_dimension=0, tiled=True
     ).astype(jnp.float32)
-    dense_grads = []
-    start = 0
-    for part in parts:
-        dense_grads.append(summed[:, start : start + part.shape[1]])
-        start += part.shape[1]
-    dense_grads[3] = dense_grads[3].T
-    dense_grads[7] = dense_grads[7][:, 0]
-    dense_grads[8] = dense_grads[8][:, 0]
-    expert_grads = (
-        lax.psum_scatter(
-            grad_up.astype(jnp.bfloat16), "dp", scatter_dimension=1, tiled=True
-        ).astype(jnp.float32),
-        lax.psum_scatter(
-            grad_down.astype(jnp.bfloat16), "dp", scatter_dimension=2, tiled=True
-        ).astype(jnp.float32),
-    )
+    dense_grads = jnp.split(summed, [512, 1024, 3584, 6144], axis=1)
+    total_sums = lax.psum(sums, ("dp", "expert"))
+    residual_norms = jnp.sqrt(total_sums[:4] / (total_sums[4] * D))
+    small = dense_grads[4]
+    router_end = 2 * HEADS * VE + expert_router.shape[1]
+    dense_grads = [
+        dense_grads[0],
+        dense_grads[1],
+        dense_grads[2],
+        dense_grads[3].T,
+        small[:, : HEADS * VE],
+        small[:, HEADS * VE : 2 * HEADS * VE],
+        small[:, 2 * HEADS * VE : router_end],
+        small[:, router_end],
+        small[:, router_end + 1],
+    ]
     return (
         final_rows.astype(jnp.bfloat16)[None],
         grad_input[None],
@@ -324,9 +1536,158 @@
         dense_grads[6],
         dense_grads[7],
         dense_grads[8],
-        expert_grads[0],
-        expert_grads[1],
+        up_grad,
+        down_grad,
         residual_norms,
+    )
+
+
+def deliver_kernel(total, sums, small, *refs):
+    count = (len(refs) - 7) // 3
+    sources, targets = refs[:count], refs[count : 2 * count]
+    value_out, output_out, expert_out, gains_out, norms_out = refs[2 * count : 2 * count + 5]
+    held = refs[2 * count + 5 : -2]
+    inward, outward = refs[-2:]
+    arrived = [pltpu.make_async_copy(a, b, inward.at[i]) for i, (a, b) in enumerate(zip(sources, held))]
+    left = [pltpu.make_async_copy(a, b, outward.at[i]) for i, (a, b) in enumerate(zip(held, targets))]
+    for made in arrived:
+        made.start()
+    spread = HEADS * VE
+    turned = jnp.concatenate([small[...], jnp.zeros((128 - ROWS, 128), jnp.float32)]).T
+    value_out[...] = turned[:spread, :ROWS]
+    output_out[...] = turned[spread : 2 * spread, :ROWS]
+    expert_out[...] = small[:, 2 * spread : 2 * spread + total]
+    gains_out[...] = turned[2 * spread + total : 2 * spread + total + 2, :ROWS]
+    row = sums[0:1, :]
+    norms_out[...] = jnp.sqrt(row[:, :4] / (row[:, 4:5] * D))
+    for one, other in zip(arrived, left):
+        one.wait()
+        other.start()
+    for made in left:
+        made.wait()
+
+
+def deliver(total, sums, small, *arrays):
+    full = jnp.float32
+    vmem = pl.BlockSpec(memory_space=pltpu.VMEM)
+    anywhere = pl.BlockSpec(memory_space=pl.ANY)
+    spread = HEADS * VE
+    return pl.pallas_call(
+        functools.partial(deliver_kernel, total),
+        out_shape=[jax.ShapeDtypeStruct(a.shape, a.dtype) for a in arrays]
+        + [
+            jax.ShapeDtypeStruct((spread, ROWS), full),
+            jax.ShapeDtypeStruct((spread, ROWS), full),
+            jax.ShapeDtypeStruct((ROWS, total), full),
+            jax.ShapeDtypeStruct((2, ROWS), full),
+            jax.ShapeDtypeStruct((1, 4), full),
+        ],
+        in_specs=[vmem] * 2 + [anywhere] * len(arrays),
+        out_specs=[anywhere] * len(arrays) + [vmem] * 5,
+        scratch_shapes=[pltpu.VMEM(a.shape, a.dtype) for a in arrays]
+        + [pltpu.SemaphoreType.DMA((len(arrays),))] * 2,
+        compiler_params=pltpu.CompilerParams(vmem_limit_bytes=63 * 2**20),
+        name="deliver",
+    )(sums, small, *arrays)
+
+
+def shards_fast(
+    hidden_in,
+    lengths,
+    value_pick,
+    output_pick,
+    expert_pick,
+    query_weight,
+    key_weight,
+    value_weight,
+    output_weight,
+    value_router,
+    output_router,
+    expert_router,
+    attention_gain,
+    feedforward_gain,
+    expert_up,
+    expert_down,
+    cotangent,
+):
+    total = expert_router.shape[1]
+    spread = HEADS * VE
+    routers = jnp.concatenate(
+        [value_router.T, output_router.T, expert_router.T, jnp.zeros((128 - 2 * spread - total, D), jnp.bfloat16)]
+    )
+    gains = jnp.stack([attention_gain, feedforward_gain]).astype(jnp.float32)
+    (
+        middle,
+        sent,
+        normed_one,
+        normed_two,
+        queries,
+        key_value,
+        probs,
+        value_all,
+        attended,
+        gates,
+        slopes,
+        cot_line,
+    ) = attend(
+        total,
+        lengths,
+        hidden_in[0],
+        cotangent[0],
+        value_pick[0].transpose(1, 2, 0),
+        output_pick[0].transpose(1, 2, 0),
+        expert_pick[0].T,
+        routers,
+        gains,
+        key_weight,
+        value_weight,
+        query_weight,
+        output_weight,
+    )
+    returned, up_grad, down_grad, forward = expert_kernel_visit(sent, cot_line, expert_up, expert_down)
+    block_out, grad_input, grad_query, grad_key, grad_value, grad_output, small, sums = backward(
+        total,
+        lengths,
+        gates,
+        slopes,
+        routers,
+        gains,
+        forward,
+        returned,
+        middle,
+        cotangent[0],
+        hidden_in[0],
+        normed_one,
+        queries,
+        key_value,
+        probs,
+        value_all,
+        attended,
+        normed_two,
+        query_weight,
+        key_weight,
+        value_weight,
+        output_weight,
+    )
+    kept = (block_out, grad_input, grad_query, grad_key, grad_value, grad_output, up_grad, down_grad)
+    delivered = deliver(total, sums, small, *kept)
+    block_out, grad_input, grad_query, grad_key, grad_value, grad_output, up_grad, down_grad = delivered[:8]
+    value_small, output_small, expert_small, gain_grads, norms = delivered[8:]
+    return (
+        block_out[None],
+        grad_input[None],
+        grad_query,
+        grad_key,
+        grad_value,
+        grad_output.T,
+        value_small.T,
+        output_small.T,
+        expert_small,
+        gain_grads[0],
+        gain_grads[1],
+        up_grad,
+        down_grad,
+        norms[0],
     )
 
 
@@ -350,8 +1711,9 @@
         P("expert", None, None),
         P("expert", "dp", None),
     )
+    small_mesh = mesh.shape["dp"] == 4 and mesh.shape["expert"] == 8
     return jax.shard_map(
-        shards,
+        shards_fast if small_mesh else shards,
         mesh=mesh,
         in_specs=placed,
         out_specs=(

time: 660 us -> 259 us (0.39); the launches traced: 650 us -> 259 us
  waiting for transfers between devices: 316 us -> 0 us
  Pallas kernels: 0 us -> 252 us
  matrix products: 125 us -> 0 us
  local copies, waits for them, and re-layouts: 115 us -> 2.72 us
  blocking collectives: 39.9 us -> 0 us
  other arithmetic: 36.3 us -> 2.31 us
  between operations: 16.9 us -> 1.33 us
    pallas_call x0 -> x4, Pallas kernels: none -> 252 us  [the longest x1 105 us: backward(): pl.pallas_call(functools.partial(backward_kernel, total_experts), out_sha...]
    dot_general x31 -> x0, matrix products: 114 us -> none  [the longest x13 21 us: low_dot(): return jnp.dot(left_side, right_side, preferred_element_type=jnp.float32)]
    all_gather x4 -> x0, waiting for transfers between devices: 111 us -> none  [the longest x1 48.4 us: expert_visit(): sent_all = lax.all_gather(sent, 'expert', axis=0, tiled=True)]
    unnamed x11 -> x0, waiting for transfers between devices: 110 us -> none
    reduce_scatter x5 -> x0, waiting for transfers between devices: 94.8 us -> none  [the longest x1 94.8 us: expert_visit(): lax.psum_scatter(jnp.concatenate([partial_out.astype(jnp.bfloat16), parti...]
    concatenate x1, local copies, waits for them, and re-layouts: 57.9 us -> 0.08 us  [shards_fast(): jnp.concatenate([value_router.T, output_router.T, expert_router.T, jnp.ze...]
    unnamed x158 -> x0, local copies, waits for them, and re-layouts: 44.8 us -> none
    psum x1 -> x0, blocking collectives: 39.9 us -> none  [shards(): lax.psum((jnp.sum(live_mask * input_full * input_full), jnp.sum(attention...]
  transfers between devices with their start and end apart: 10 -> 0, of which waited for: 6 -> 0; matrix products, arithmetic and copies ran while one was open for 31% -> 0% of each run, Pallas kernels for 0% -> 0%
where the time goes in v4:
time: 259 us
  Pallas kernels  252 us (97%)
  local copies, waits for them, and re-layouts  2.72 us (1%)
    pallas_call x1, Pallas kernels, backward(): pl.pallas_call(functools.partial(backward_kernel, total_experts), out_sha...  105 us
    pallas_call x1, Pallas kernels, expert_kernel_visit(): pl.pallas_call(visit_kernel, out_shape=[jax.ShapeDtypeStruct((tokens, D +...  94.9 us
    pallas_call x1, Pallas kernels, attend(): pl.pallas_call(functools.partial(attend_kernel, total), out_shape=[jax.Sh...  47.4 us

profile of v4, /device:TPU:0, one launch (start us, length us, event | category | flops | bytes accessed | tf_op | source)
XLA Modules:
  0.0 258.6 jit_solution(10260458952824260730)
XLA Ops:
  1.3 0.1 pad.5.clone
  1.4 0.7 stack.9
  2.1 0.7 stack.10
  2.8 0.6 maximum_convert_fusion.gains
  3.4 1.7 maximum_maximum_fusion.routers
  5.1 47.4 %attend.1 = (f32[256,1024]{1,0:T(8,128)}, bf16[256,1152]{1,0:T(8,128)(2,1)}, bf16[256,1024]{1,0:T(8,128)(2,1)}, bf16[256,1024]{1,0:T(8,128)(2,1)}, bf16[256,512]...) custom-call(s32[1]{0:T(128)S(6)} %copy.31.lengths, ...), custom_call_target="tpu_custom_call" | custom-call | tf_op jit(solution)/shard_map/attend/pallas_call | solution.py:687
  52.5 94.9 %expert_visit.1 = (f32[256,1152]{1,0:T(8,128)}, f32[6,256,128]{2,1,0:T(8,128)}, f32[6,128,256]{2,1,0:T(8,128)}, bf16[4,256,1024]{2,1,0:T(8,128)(2,1)}) custom-call(bf16[256,1152]{1,0:T(8,128)(2,1)} %get-tuple-element.53.sent, bf16[4,256,1024]{2,1,0:T(8,128)(2,1)} %get-tuple-element.54.cot, bf16[6,1024,128]{2,1,0:T(8,128)(2,1)} %up.1, bf16[768,1024]{1,0:T(8,128)(2,1)} %bitcast.29), custom_call_target="tpu_custom_call" | custom-call | tf_op jit(solution)/shard_map/expert_visit/pallas_call | solution.py:394
  147.4 105.3 %backward.1 = (bf16[256,1024]{1,0:T(8,128)(2,1)}, f32[256,1024]{1,0:T(8,128)}, f32[32,512]{1,0:T(8,128)}, f32[32,512]{1,0:T(8,128)}, f32[32,2560]{1,0:T(8,128)},...) custom-call(s32[1]{0:T(128)S(6)} %copy.31.lengths, f32[256,128]{1,0:T(8,128)} %get-tuple-element.51.gates, ...), custom_call_target="tpu_custom_call" | custom-call | tf_op jit(solution)/shard_map/backward/pallas_call | solution.py:1190
  252.7 4.6 %deliver.1 = (bf16[256,1024]{1,0:T(8,128)(2,1)}, f32[256,1024]{1,0:T(8,128)}, f32[32,512]{1,0:T(8,128)}, f32[32,512]{1,0:T(8,128)}, f32[32,2560]{1,0:T(8,128)}, ...) custom-call(f32[8,128]{1,0:T(8,128)} %get-tuple-element.65.sums, ...), custom_call_target="tpu_custom_call" | custom-call | tf_op jit(solution)/shard_map/deliver/pallas_call | solution.py:1575
  257.3 1.3 slice_bitcast_fusion
  (1 shorter events, 0.0 us)

commit v5 on v4

--- a/solution.py
+++ b/solution.py
@@ -59,9 +59,9 @@
 
 
 def visit_kernel(
-    sent, cot, up, down, back_out, up_out, down_out, forward_out,
-    rows, cot_other, up_wide, chosen, cots, gated, grad_pre, forward, forward_in, gated_turned, pre_turned, partial, paired_in, chain_in, up_low, down_low, up_in, down_in,
-    row_send, row_recv, cot_send, cot_recv, pair_send, pair_recv, forward_send, forward_recv, chain_send, chain_recv, grad_send, grad_recv,
+    sent, cot_at, up_at, down_at, back_out, weights_out, weights_kept, forward_out,
+    cot, up, down, rows, cot_other, up_wide, chosen, cots, gated, grad_pre, forward, forward_in, gated_turned, pre_turned, partial, paired_in, chain_in, up_low, down_low, up_in, down_in,
+    fetch, row_send, row_recv, half_send, half_recv, cot_send, cot_recv, pair_send, pair_recv, forward_send, forward_recv, chain_send, chain_recv, grad_send, grad_recv,
 ):
     experts = up.shape[0]
     wide = down.shape[0]
@@ -77,6 +77,12 @@
     def at_z(place):
         return (dp, place * 2 + core)
 
+    fetched = [
+        pltpu.make_async_copy(source, target, fetch.at[i])
+        for i, (source, target) in enumerate(((cot_at, cot), (up_at, up), (down_at, down)))
+    ]
+    for made in fetched:
+        made.start()
     barrier = pltpu.get_barrier_semaphore()
     for place in (sibling, beside, behind):
         pl.semaphore_signal(barrier, inc=1, device_id=place, device_id_type=MESH)
@@ -96,26 +102,33 @@
             src_ref=source, dst_ref=target, send_sem=send, recv_sem=recv, device_id=place, device_id_type=MESH
         )
 
-    def row_copy(way, at, source=None):
-        place = (sibling, at_z(z + 1), at_z(z - 1))[way]
-        block = rows.at[at]
-        target = block if way else rows.at[4 + at]
-        return remote(block if source is None else source, target, row_send.at[way, at], row_recv.at[0 if way else 1, at], place)
+    def row_copy(at, source=None):
+        block = rows.at[at] if source is None else source
+        return remote(block, rows.at[4 + at], row_send.at[at], row_recv.at[at], sibling)
+
+    def half_copy(way, at, part, source=None):
+        span = pl.ds(part * (rows.shape[1] // 2), rows.shape[1] // 2)
+        block = rows.at[at] if source is None else source
+        return remote(
+            block.at[span], rows.at[at, span], half_send.at[way, at, part], half_recv.at[at, part], at_z(z + 1 - 2 * way)
+        )
 
     def cot_copy(at):
         return remote(cot.at[at], cot_other.at[at], cot_send.at[at], cot_recv.at[at], sibling)
 
-    own = row_copy(0, z, sent), row_copy(1, z, sent), row_copy(2, z, sent)
-
     @pl.when(z < 3)
     def _():
-        own[1].start()
+        for part in range(2):
+            half_copy(0, z, part, sent).start()
 
     @pl.when(z > 0)
     def _():
-        own[2].start()
-
-    own[0].start()
+        for part in range(2):
+            half_copy(1, z, part, sent).start()
+
+    row_copy(z, sent).start()
+    for made in fetched:
+        made.wait()
     cot_copy(z).start()
     for k in (1, 2, 3):
         cot_copy((z + k) % 4).start()
@@ -135,12 +148,14 @@
     def pair_copy(at):
         return remote(partial.at[1, at], paired_in.at[at], pair_send.at[at], pair_recv.at[at], sibling)
 
-    spans = (pl.ds(0, D // 2), pl.ds(D // 2, D // 2 + 128))
+    parts = 4
+    size = rows.shape[1] // parts
+    spans = [pl.ds(i * size, size) for i in range(parts)]
 
     def chain_copy(dest, slot, to, stage, part):
         span = spans[part]
         return remote(
-            partial.at[0, dest, :, span], chain_in.at[slot, :, span],
+            partial.at[0, dest, span], chain_in.at[slot, span],
             chain_send.at[stage, part], chain_recv.at[slot, part], at_z(to),
         )
 
@@ -154,6 +169,36 @@
 
         lax.fori_loop(0, target.shape[0] // 32, some, 0)
 
+    def forward_copy(at):
+        return remote(forward.at[at], forward_in.at[at], forward_send.at[at], forward_recv.at[at], sibling)
+
+    def forward_block(block):
+        at = block % 4
+        def some(n, inside):
+            span = pl.ds(pl.multiple_of(n * 256, 256), 256)
+            value = jnp.dot(gated[block], down[:, span], preferred_element_type=jnp.float32).astype(jnp.bfloat16)
+
+            @pl.when(block >= 4)
+            def _():
+                forward[at, :, span] = value
+
+            @pl.when(block < 4)
+            def _():
+                forward_out[at, :, span] = value
+
+            return inside
+
+        lax.fori_loop(0, D // 256, some, 0)
+
+        @pl.when(block >= 4)
+        def _():
+            forward_copy(at).start()
+
+    def relay(dest, slot, to, stage, part):
+        chain_copy(dest, dest, to, stage, part).wait_recv()
+        add(partial.at[0, dest, spans[part]], chain_in.at[dest, spans[part]])
+        chain_copy(dest, slot, to, stage, part).start()
+
     def visit(q, carry):
         p, other = q // 2, q % 2
         at = order(p)
@@ -161,26 +206,33 @@
 
         @pl.when((other == 0) & (p > 0))
         def _():
-            row_copy(1, at).wait_recv()
-            row_copy(0, at).start()
-
-            @pl.when((at < z) & (z < 3))
-            def _():
-                row_copy(1, at).start()
-
-            @pl.when((at > z) & (z > 0))
-            def _():
-                row_copy(2, at).start()
+            for part in range(2):
+                half_copy(0, at, part).wait_recv()
+
+                @pl.when((at < z) & (z < 3))
+                def _():
+                    half_copy(0, at, part).start()
+
+                @pl.when((at > z) & (z > 0))
+                def _():
+                    half_copy(1, at, part).start()
+
+            row_copy(at).start()
 
         @pl.when(other == 1)
         def _():
-            row_copy(0, at).wait_recv()
+            row_copy(at).wait_recv()
             cot_copy(at).wait_recv()
             cots[...] = cot_other[at]
 
         @pl.when(other == 0)
         def _():
             cots[...] = cot[at]
+
+        @pl.when((inner == 1) & (q == 7))
+        def _():
+            relay(*next_one, 0)
+            relay(*next_one, 1)
 
         count = rows.shape[1]
         places = pl.ds(pl.multiple_of(block * count, count), count)
@@ -220,11 +272,17 @@
 
         @pl.when((inner == 0) & (q == 3))
         def _():
-            chain_copy(*nearest, 0).start()
+            for part in range(parts):
+                chain_copy(*nearest, part).start()
 
         @pl.when((inner == 0) & (q == 5))
         def _():
-            chain_copy(*next_one, 0).start()
+            for part in range(parts):
+                chain_copy(*next_one, part).start()
+
+        @pl.when(q < 6)
+        def _():
+            forward_block(block)
 
         return carry
 
@@ -234,18 +292,10 @@
     next_one = (2 - half, 2 - half + inner * (2 + half), z + onward, 3)
     lax.fori_loop(0, 8, visit, 0)
 
-    def relay(dest, slot, to, stage, part):
-        chain_copy(dest, dest, to, stage, part).wait_recv()
-        add(partial.at[0, dest, :, spans[part]], chain_in.at[dest, :, spans[part]])
-        chain_copy(dest, slot, to, stage, part).start()
-
     @pl.when(inner == 0)
     def _():
-        chain_copy(*farthest, 0).start()
-        chain_copy(*farthest, 1).start()
-        chain_copy(*next_one, 1).start()
-        chain_copy(*nearest, 1).start()
-
+        for part in range(parts):
+            chain_copy(*farthest, part).start()
     tokens_all = rows.reshape(rows.shape[0] * rows.shape[1], rows.shape[2])
     cots_own = cot.reshape(cot.shape[0] * cot.shape[1], D)
     cots_other = cot_other.reshape(cot.shape[0] * cot.shape[1], D)
@@ -259,32 +309,24 @@
     def down_copy(j):
         return remote(down_low.at[j], down_in.at[j], grad_send.at[1, j], grad_recv.at[1, j], beside if j == 1 else behind)
 
-    def weight_grads(j, carry):
-        across, aside = 1 - j % 2, 1 - j // 2
-        at = (y + across * (1 - 2 * y)) * 2 + x + aside * (1 - 2 * x)
-        span = pl.ds(pl.multiple_of(at * quarter, quarter), quarter)
+    def span_of(j):
+        at = (y + (1 - j % 2) * (1 - 2 * y)) * 2 + x + (1 - j // 2) * (1 - 2 * x)
+        return pl.ds(pl.multiple_of(at * quarter, quarter), quarter)
+
+    def up_quarter(j):
         up_low[j] = jnp.dot(
-            pre_turned[...], tokens_all[:, span], preferred_element_type=jnp.float32
+            pre_turned[...], tokens_all[:, span_of(j)], preferred_element_type=jnp.float32
         ).astype(jnp.bfloat16)
+        if j < 2:
+            up_copy(j).start()
+
+    def down_quarter(j):
         down_low[j] = (
-            jnp.dot(gated_turned[:, :place], cots_own[:, span], preferred_element_type=jnp.float32)
-            + jnp.dot(gated_turned[:, place:], cots_other[:, span], preferred_element_type=jnp.float32)
+            jnp.dot(gated_turned[:, :place], cots_own[:, span_of(j)], preferred_element_type=jnp.float32)
+            + jnp.dot(gated_turned[:, place:], cots_other[:, span_of(j)], preferred_element_type=jnp.float32)
         ).astype(jnp.bfloat16)
-
-        @pl.when(j == 0)
-        def _():
-            up_copy(0).start()
-            down_copy(0).start()
-
-        @pl.when(j == 1)
-        def _():
-            up_copy(1).start()
-
-        @pl.when(j == 2)
-        def _():
-            down_copy(2).start()
-
-        return carry
+        if j in (0, 2):
+            down_copy(j).start()
 
     def relays(*ways):
         @pl.when(inner == 1)
@@ -292,85 +334,68 @@
             for way, part in ways:
                 relay(*way, part)
 
-    def forward_copy(at):
-        return remote(forward.at[at], forward_in.at[at], forward_send.at[at], forward_recv.at[at], sibling)
-
-    def forward_block(block, carry):
-        def some(n, inside):
-            span = pl.ds(pl.multiple_of(n * 256, 256), 256)
-            value = jnp.dot(gated[block], down[:, span], preferred_element_type=jnp.float32).astype(jnp.bfloat16)
-
-            @pl.when(block >= 4)
-            def _():
-                forward[block % 4, :, span] = value
-
-            @pl.when(block < 4)
-            def _():
-                forward_out[block % 4, :, span] = value
-
-            return inside
-
-        lax.fori_loop(0, D // 256, some, 0)
-
-        @pl.when(block >= 4)
-        def _():
-            forward_copy(block % 4).start()
-
-        return carry
-
-    relays((next_one, 0))
-    lax.fori_loop(0, 1, weight_grads, 0)
-    relays((farthest, 0))
-    lax.fori_loop(1, 3, weight_grads, 0)
-    relays((farthest, 1), (backward, 0))
-    lax.fori_loop(3, 4, weight_grads, 0)
-    up_copy(0).wait()
-    add(up_low.at[2], up_in.at[0])
-    up_copy(2).start()
-    down_copy(0).wait()
-    add(down_low.at[1], down_in.at[0])
-    down_copy(1).start()
-    lax.fori_loop(4, 8, forward_block, 0)
-    relays((backward, 1), (next_one, 1))
-    lax.fori_loop(0, 4, forward_block, 0)
-    for at in range(4):
+    def forward_add(p):
+        at = order(p)
         forward_copy(at).wait()
         add(forward_out.at[at], forward_in.at[at])
-    up_sum = up_low[3].astype(jnp.float32)
-    down_sum = down_low[3].astype(jnp.float32)
-    for j in (1, 2):
-        up_copy(j).wait()
-        up_sum += up_in[j].astype(jnp.float32)
-        down_copy(j).wait()
-        down_sum += down_in[j].astype(jnp.float32)
-    for e in range(experts):
-        up_out[e] = up_sum[e * hidden : (e + 1) * hidden, :].T
-        down_out[e] = down_sum[e * hidden : (e + 1) * hidden, :]
-
-    for part in range(2):
+
+    relays((next_one, 2), (next_one, 3))
+    up_quarter(0)
+    down_quarter(0)
+    relays((farthest, 0))
+    up_quarter(1)
+    relays((farthest, 1))
+    down_quarter(2)
+    relays((backward, 0), (farthest, 2))
+    forward_block(4 + order(3))
+    relays((backward, 1), (farthest, 3))
+    up_quarter(2)
+    relays((backward, 2))
+    forward_add(0)
+    forward_add(1)
+    down_quarter(1)
+    relays((backward, 3))
+    forward_block(order(3))
+    up_quarter(3)
+    down_quarter(3)
+    forward_add(2)
+    forward_add(3)
+    for part in range(parts):
         span = spans[part]
         chain_copy(z, z, z, 0, part).wait_recv()
-        back_out[:, span] = partial[0, z, :, span].astype(jnp.float32) + chain_in[z, :, span].astype(jnp.float32)
+        back_out[span, :] = partial[0, z, span, :].astype(jnp.float32) + chain_in[z, span, :].astype(jnp.float32)
 
         @pl.when(inner == 1)
         def _():
             chain_copy(z, 4, z, 0, part).wait_recv()
-            back_out[:, span] = back_out[:, span] + chain_in[4, :, span].astype(jnp.float32)
+            back_out[span, :] = back_out[span, :] + chain_in[4, span, :].astype(jnp.float32)
+
+    ends = (
+        (up_copy(0), up_low, 2, up_in, 0, weights_out.at[0]),
+        (up_copy(1), up_low, 3, up_in, 1, weights_kept.at[0]),
+        (down_copy(0), down_low, 1, down_in, 0, weights_out.at[1]),
+        (down_copy(2), down_low, 3, down_in, 2, weights_kept.at[1]),
+    )
+    for made, mine, j, other, slot, target in ends:
+        made.wait()
+        target[...] = mine[j]
+        add(target, other.at[slot])
 
     for at in range(4):
-        row_copy(0, at).wait_send()
+        row_copy(at).wait_send()
         cot_copy(at).wait_send()
         pair_copy(at).wait_send()
-
-        @pl.when((at <= z) & (z < 3))
-        def _():
-            row_copy(1, at).wait_send()
-
-        @pl.when((at >= z) & (z > 0))
-        def _():
-            row_copy(2, at).wait_send()
-
-    for part in range(2):
+        for part in range(2):
+
+            @pl.when((at <= z) & (z < 3))
+            def _():
+                half_copy(0, at, part).wait_send()
+
+            @pl.when((at >= z) & (z > 0))
+            def _():
+                half_copy(1, at, part).wait_send()
+
+    for part in range(parts):
 
         @pl.when(inner == 0)
         def _():
@@ -395,13 +420,16 @@
         visit_kernel,
         out_shape=[
             jax.ShapeDtypeStruct((tokens, D + 128), f32),
-            jax.ShapeDtypeStruct((experts, D // 4, hidden), f32),
-            jax.ShapeDtypeStruct((experts, hidden, D // 4), f32),
+            jax.ShapeDtypeStruct((2, wide, D // 4), low),
+            jax.ShapeDtypeStruct((2, wide, D // 4), low),
             jax.ShapeDtypeStruct((4, tokens, D), low),
         ],
-        in_specs=[vmem] * 4,
+        in_specs=[vmem] + [pl.BlockSpec(memory_space=pl.ANY)] * 3,
         out_specs=[vmem] * 4,
         scratch_shapes=[
+            pltpu.VMEM((4, tokens, D), low),
+            pltpu.VMEM((experts, D, hidden), low),
+            pltpu.VMEM((wide, D), low),
             pltpu.VMEM((8, tokens, D + 128), low),
             pltpu.VMEM((4, tokens, D), low),
             pltpu.VMEM((D, wide), low),
@@ -420,7 +448,7 @@
             pltpu.VMEM((4, wide, D // 4), low),
             pltpu.VMEM((3, wide, D // 4), low),
             pltpu.VMEM((3, wide, D // 4), low),
-            dma((3, 4)), dma((2, 4)), dma((4,)), dma((4,)), dma((4,)), dma((4,)), dma((4,)), dma((4,)), dma((4, 2)), dma((5, 2)), dma((2, 3)), dma((2, 3)),
+            dma((3,)), dma((4,)), dma((4,)), dma((2, 4, 2)), dma((4, 2)), dma((4,)), dma((4,)), dma((4,)), dma((4,)), dma((4,)), dma((4,)), dma((4, 4)), dma((5, 4)), dma((2, 3)), dma((2, 3)),
         ],
         compiler_params=pltpu.CompilerParams(collective_id=2, has_side_effects=True, vmem_limit_bytes=58 * 2**20),
         name="expert_visit",
@@ -430,10 +458,12 @@
 def attend_kernel(
     expert_total, lengths, hidden, cot, value_pick, output_pick, expert_pick, routers, gains,
     key_weight_at, value_weight_at, query_weight_at, output_weight_at,
+    middle_at, sent_at, normed_one_at, normed_two_at, queries_at, key_value_at, probs_at, value_all_at, attended_at,
+    gates_at, slopes_at, cot_line_at,
     middle, sent, normed_one, normed_two, queries, key_value, probs, value_all, attended,
     gates, slopes, cot_line,
     key_weight, value_weight, query_weight, output_weight, mixed, hot_turned, hot,
-    fetch, pair_send, pair_recv, cot_send, cot_recv, own_sem,
+    fetch, leave, pair_send, pair_recv, cot_send, cot_recv, own_sem,
 ):
     dp, ex = lax.axis_index("dp"), lax.axis_index("expert")
     z, core = ex // 2, ex % 2
@@ -458,6 +488,12 @@
     ]
     for made in weights:
         made.start()
+    results = (
+        (middle, middle_at), (sent, sent_at), (normed_one, normed_one_at), (normed_two, normed_two_at),
+        (queries, queries_at), (key_value, key_value_at), (probs, probs_at), (value_all, value_all_at),
+        (attended, attended_at), (gates, gates_at), (slopes, slopes_at), (cot_line, cot_line_at),
+    )
+    leaving = [pltpu.make_async_copy(source, target, leave.at[i]) for i, (source, target) in enumerate(results)]
 
     def at_z(place):
         return (dp, place * 2 + core)
@@ -534,6 +570,7 @@
                 pair_copy(step, part, dp).start()
 
     normed_one[...] = norm(hidden[...].astype(jnp.float32), gains[0:1, :])
+    leaving[2].start()
     weights[0].wait()
     key_value[dp, :, parts[0]] = jnp.dot(
         normed_one[...], key_weight[...], preferred_element_type=jnp.float32
@@ -570,6 +607,7 @@
         return carry
 
     lax.fori_loop(0, HEADS * VE * HEAD_DIM // 256, values, 0)
+    leaving[7].start()
     for h in range(HEADS):
         row = jnp.zeros((count, HEAD_DIM), jnp.float32)
         for e in range(h * VE, (h + 1) * VE):
@@ -579,6 +617,7 @@
 
     weights[2].wait()
     queries[...] = jnp.dot(normed_one[...], query_weight[...], preferred_element_type=jnp.float32).astype(low)
+    leaving[4].start()
     for block in range(4):
 
         @pl.when(block > dp)
@@ -609,7 +648,10 @@
         return carry
 
     lax.fori_loop(0, HEADS, score, 0)
+    leaving[6].start()
+    leaving[9].start()
     wait_part(1)
+    leaving[5].start()
     pass_on(2)
 
     def collect(h, carry):
@@ -619,6 +661,7 @@
         return carry
 
     lax.fori_loop(0, HEADS, collect, 0)
+    leaving[8].start()
     for h in range(HEADS):
         row = attended[:, h * HEAD_DIM : (h + 1) * HEAD_DIM]
         for e in range(h * VE, (h + 1) * VE):
@@ -635,6 +678,7 @@
         return carry
 
     lax.fori_loop(0, D // 256, outward, 0)
+    leaving[0].start()
     sent[:, :D] = middle[...].astype(low)
     normed_two[...] = norm(middle[...], gains[1:2, :])
     sig = jax.nn.sigmoid(dot_last(normed_two[...], routers[...]))
@@ -643,8 +687,11 @@
     lane = lax.broadcasted_iota(jnp.int32, (count, 128), 1)
     slopes[...] = jnp.where(lane < 2 * spread, slopes[...], gate * (1.0 - sig))
 
+    for i in (1, 3, 10):
+        leaving[i].start()
     pass_on(3)
     keep.wait()
+    leaving[11].start()
     for part in range(2):
         for step in (1, 2, 3):
 
@@ -661,6 +708,9 @@
         @pl.when((at >= z) & (z > 0))
         def _():
             cot_copy(1, at).wait_send()
+
+    for made in leaving:
+        made.wait()
 
 
 def attend(total, lengths, *operands):
@@ -688,13 +738,15 @@
         functools.partial(attend_kernel, total),
         out_shape=[jax.ShapeDtypeStruct(*shape) for shape in shapes],
         in_specs=[pl.BlockSpec(memory_space=pltpu.SMEM)] + [vmem] * (len(operands) - 4) + [anywhere] * 4,
-        out_specs=[vmem] * len(shapes),
-        scratch_shapes=[pltpu.VMEM(a.shape, a.dtype) for a in operands[-4:]]
+        out_specs=[anywhere] * len(shapes),
+        scratch_shapes=[pltpu.VMEM(*shape) for shape in shapes]
+        + [pltpu.VMEM(a.shape, a.dtype) for a in operands[-4:]]
         + [
             pltpu.VMEM((count, wide), low),
             pltpu.VMEM((128, count), full),
             pltpu.VMEM((count, 128), full),
             dma((4,)),
+            dma((len(shapes),)),
             dma((4, 2)),
             dma((4, 2)),
             dma((2, 4)),
@@ -710,15 +762,15 @@
 
 def backward_kernel(
     total_experts, lengths, gates, slopes, routers, gains,
-    forward_at, returned_at, middle_at, cot_at, hidden_at, normed_one_at, queries_at, key_value_at, probs_at, value_all_at,
+    weights_at, forward_at, returned_at, middle_at, cot_at, hidden_at, normed_one_at, queries_at, key_value_at, probs_at, value_all_at,
     attended_at, normed_two_at, query_weight_at, key_weight_at, value_weight_at, output_weight_at,
-    block_out, grad_in, out_query, out_key, out_value, out_output, out_small, sums_out,
-    forward, returned, middle, cot, hidden, normed_one, queries, key_value, probs, value_all,
+    block_out, grad_in, out_query, out_key, out_value, out_output, out_small, weights_in,
+    weights, forward, returned, middle, cot, hidden, normed_one, queries, key_value, probs, value_all,
     attended, normed_two, query_weight, key_weight, value_part, output_part,
     branch, branch_turned, one_turned, hidden_turned, grad_att, grad_query, leave, arrive, grad_key,
-    grad_each, grad_middle, grad_one, logit_one, logit_two, small_turned, mixed,
-    grads, grads_small, core_in, plane_in, last_in, sums_in, forward_in,
-    fetch, part_fetch, leave_send, leave_recv, send, recv, forward_send, forward_recv,
+    grad_each, grad_middle, logit_one, logit_two, small_turned, mixed,
+    grads, grads_small, core_in, plane_in, last_in, forward_in,
+    fetch, part_fetch, leave_send, leave_recv, send, recv, forward_send, forward_recv, weights_send, weights_recv,
 ):
     dp, ex = lax.axis_index("dp"), lax.axis_index("expert")
     y, x, z, core = dp // 2, dp % 2, ex // 2, ex % 2
@@ -736,6 +788,7 @@
         pl.semaphore_signal(barrier, inc=1, device_id=place, device_id_type=MESH)
 
     held = dict(
+        weights=(weights_at, weights),
         forward=(forward_at, forward),
         returned=(returned_at, returned),
         middle=(middle_at, middle),
@@ -766,7 +819,7 @@
             value_weight_at.at[:, pl.ds(n * PIECE, PIECE)], value_part.at[n % 2], part_fetch.at[1, n % 2]
         )
 
-    first_held = ("forward", "returned", "middle", "cot", "hidden")
+    first_held = ("weights", "forward", "returned", "middle", "cot", "hidden")
     for name in first_held:
         got[name].start()
     for n in range(2):
@@ -898,9 +951,9 @@
     next_one = (2 - half, 2 - half + inner * (2 + half), z + onward, 3)
 
     def forward_copy(dest, slot, to, stage, part):
-        span = pl.ds(part * (D // 2), D // 2)
+        span = pl.ds(part * (count // 2), count // 2)
         return pltpu.make_async_remote_copy(
-            src_ref=forward.at[dest, :, span], dst_ref=forward_in.at[slot, :, span],
+            src_ref=forward.at[dest, span], dst_ref=forward_in.at[slot, span],
             send_sem=forward_send.at[stage, part], recv_sem=forward_recv.at[slot, part],
             device_id=(dp, to * 2 + core), device_id_type=MESH,
         )
@@ -909,12 +962,21 @@
         @pl.when(inner == 1)
         def _():
             for (dest, slot, to, stage), part in ways:
-                span = pl.ds(part * (D // 2), D // 2)
+                span = pl.ds(part * (count // 2), count // 2)
                 forward_copy(dest, dest, to, stage, part).wait_recv()
-                add(forward.at[dest, :, span], forward_in.at[dest, :, span])
+                add(forward.at[dest, span], forward_in.at[dest, span])
                 forward_copy(dest, slot, to, stage, part).start()
 
     pl.semaphore_wait(barrier, 7)
+    weight_copies = [
+        pltpu.make_async_remote_copy(
+            src_ref=weights.at[i], dst_ref=weights_in.at[i], send_sem=weights_send.at[i],
+            recv_sem=weights_recv.at[i], device_id=place, device_id_type=MESH,
+        )
+        for i, place in enumerate((behind, beside))
+    ]
+    for made in weight_copies:
+        made.start()
 
     @pl.when(inner == 0)
     def _():
@@ -971,17 +1033,17 @@
 
     def output_rows():
         for part in range(2):
-            span = pl.ds(part * (D // 2), D // 2)
+            span = pl.ds(part * (count // 2), count // 2)
             forward_copy(z, z, z, 0, part).wait_recv()
-            add(forward.at[z, :, span], forward_in.at[z, :, span])
+            add(forward.at[z, span], forward_in.at[z, span])
 
             @pl.when(inner == 1)
             def _():
                 forward_copy(z, 4, z, 0, part).wait_recv()
-                add(forward.at[z, :, span], forward_in.at[4, :, span])
+                add(forward.at[z, span], forward_in.at[4, span])
 
         sums = lax.fori_loop(0, count // rows_each, last_rows, jnp.zeros((1, 128), full))
-        sums_in[0] = jnp.broadcast_to(sums, (8, 128))
+        return sums
 
     def weight_grad(i, turned, right):
         def some(n, carry):
@@ -1068,7 +1130,7 @@
     weight_grad(4, one_turned, grad_query[...])
     halve_near(3)
     hidden_turned[...] = hidden[...].T
-    grad_one[...] = dot_last(grad_query[...], query_weight[...])
+    returned[:, :D] = dot_last(grad_query[...], query_weight[...])
     halve_near(4)
     got["value_all"].wait()
 
@@ -1100,19 +1162,21 @@
     weight_grad(9, one_turned, grad_key[...])
     halve_near(8)
     got["key_weight"].wait()
-    grad_one[...] += dot_last(grad_key[...], key_weight[...])
+    returned[:, :D] += dot_last(grad_key[...], key_weight[...])
     halve_near(9)
     halve_far(2)
-    grad_one[...] += jnp.dot(logit_one[...].astype(low), routers[...], preferred_element_type=full)
+    returned[:, :D] += jnp.dot(logit_one[...].astype(low), routers[...], preferred_element_type=full)
 
     def first_norm(n, gain_sum):
         rows = pl.ds(pl.multiple_of(n * rows_each, rows_each), rows_each)
-        back, gain_part = norm_back(hidden[rows, :].astype(full), grad_one[rows, :], gains[0:1, :])
+        back, gain_part = norm_back(hidden[rows, :].astype(full), returned[rows, :D], gains[0:1, :])
         grad_in[rows, :] = grad_middle[rows, :] + back
         return gain_sum + gain_part
 
     gain_one_sum = lax.fori_loop(0, count // rows_each, first_norm, jnp.zeros((1, D), full))
     halve_far(3)
+    for made in weight_copies:
+        made.wait()
     got["normed_two"].wait()
     small_turned[...] = dot_first(logit_one[...].astype(low), normed_one[...]) + dot_first(
         logit_two[...], normed_two[...]
@@ -1120,27 +1184,13 @@
     small_rows = 2 * spread_count + total_experts
     small_turned[small_rows : small_rows + 1, :] = gain_one_sum
     small_turned[small_rows + 1 : small_rows + 2, :] = gain_two_sum
+    sums = output_rows()
+    for i in range(5):
+        small_turned[small_rows + 2 + i : small_rows + 3 + i, :] = jnp.broadcast_to(sums[:, i : i + 1], (1, D))
     grads_small[...] = small_turned[...].T.astype(low).reshape(grads_small.shape)
     halve_core(10)
     spread(2)
     halve_far(4)
-    output_rows()
-
-    rounds = [[sibling], [beside], [behind], line]
-    offset = [1, 2, 3, 4]
-
-    def sum_start(r):
-        for j, place in enumerate(rounds[r]):
-            begin(("sum", r, j), sums_in.at[0], sums_in.at[offset[r] + j], (len(pieces) + j, r), place)
-
-    def sum_end(r):
-        for j in range(len(rounds[r])):
-            started["sum", r, j].wait()
-        total = sums_in[0]
-        for j in range(len(rounds[r])):
-            total = total + sums_in[offset[r] + j]
-        sums_in[0] = total
-
     def value_side(n):
         value_copy(n).wait()
         grad_in[...] += dot_last(grad_each[:, n * PIECE : (n + 1) * PIECE], value_part[n % 2])
@@ -1148,16 +1198,15 @@
             value_copy(n + 2).start()
 
     for action, i in (
-        (sum_start, 0), (halve_near, 10), (spread, 3),
-        (value_side, 0), (sum_end, 0), (sum_start, 1), (halve_far, 5), (halve_far, 0), (spread, 4), (finish, 2),
-        (value_side, 1), (sum_end, 1), (sum_start, 2), (halve_far, 6), (spread, 0), (finish, 3), (spread, 5),
-        (value_side, 2), (sum_end, 2), (sum_start, 3), (halve_far, 7), (finish, 4), (spread, 6),
-        (value_side, 3), (finish, 0), (halve_far, 1), (halve_far, 8), (finish, 5), (spread, 7), (sum_end, 3),
+        (halve_near, 10), (spread, 3),
+        (value_side, 0), (halve_far, 5), (halve_far, 0), (spread, 4), (finish, 2),
+        (value_side, 1), (halve_far, 6), (spread, 0), (finish, 3), (spread, 5),
+        (value_side, 2), (halve_far, 7), (finish, 4), (spread, 6),
+        (value_side, 3), (finish, 0), (halve_far, 1), (halve_far, 8), (finish, 5), (spread, 7),
         (spread, 1), (halve_far, 9), (finish, 6), (spread, 8), (halve_far, 10), (finish, 7), (finish, 1), (spread, 9),
         (spread, 10), (finish, 8), (finish, 9), (finish, 10),
     ):
         action(i)
-    sums_out[...] = sums_in[0]
     for h in range(HEADS):
         for k in (1, 2, 3):
 
@@ -1185,7 +1234,7 @@
     vmem = pl.BlockSpec(memory_space=pltpu.VMEM)
     anywhere = pl.BlockSpec(memory_space=pl.ANY)
     dma = pltpu.SemaphoreType.DMA
-    whole = [pltpu.VMEM(a.shape, a.dtype) for a in arrays[:14]]
+    whole = [pltpu.VMEM(a.shape, a.dtype) for a in arrays[:15]]
     n = 11
     return pl.pallas_call(
         functools.partial(backward_kernel, total_experts),
@@ -1197,7 +1246,7 @@
             jax.ShapeDtypeStruct((ROWS, wide), full),
             jax.ShapeDtypeStruct((ROWS, wide), full),
             jax.ShapeDtypeStruct((ROWS, 128), full),
-            jax.ShapeDtypeStruct((8, 128), full),
+            jax.ShapeDtypeStruct(arrays[0].shape, low),
         ],
         in_specs=[pl.BlockSpec(memory_space=pltpu.SMEM)] + [vmem] * 4 + [anywhere] * len(arrays),
         out_specs=[vmem] * 8,
@@ -1216,7 +1265,6 @@
             pltpu.VMEM((count, width), low),
             pltpu.VMEM((count, wide), low),
             pltpu.VMEM((count, D), full),
-            pltpu.VMEM((count, D), full),
             pltpu.VMEM((count, 128), full),
             pltpu.VMEM((count, 128), low),
             pltpu.VMEM((128, D), full),
@@ -1226,16 +1274,17 @@
             pltpu.VMEM((n, 4, 4, ROWS, PIECE), low),
             pltpu.VMEM((n, 12, ROWS, PIECE), low),
             pltpu.VMEM((n, 3, ROWS, PIECE), low),
-            pltpu.VMEM((7, 8, 128), full),
             pltpu.VMEM((5, count, D), low),
-            dma((14,)),
+            dma((15,)),
             dma((2, 2)),
             dma((3, HEADS)),
             dma((3, HEADS)),
-            dma((n + 3, 7)),
-            dma((n + 3, 7)),
+            dma((n, 7)),
+            dma((n, 7)),
             dma((4, 2)),
             dma((5, 2)),
+            dma((2,)),
+            dma((2,)),
         ],
         compiler_params=pltpu.CompilerParams(
             collective_id=3, has_side_effects=True, vmem_limit_bytes=62 * 2**20
@@ -1542,11 +1591,11 @@
     )
 
 
-def deliver_kernel(total, sums, small, *refs):
-    count = (len(refs) - 7) // 3
+def deliver_kernel(total, small, weights_kept, weights_in, *refs):
+    count = (len(refs) - 9) // 3
     sources, targets = refs[:count], refs[count : 2 * count]
-    value_out, output_out, expert_out, gains_out, norms_out = refs[2 * count : 2 * count + 5]
-    held = refs[2 * count + 5 : -2]
+    value_out, output_out, expert_out, gains_out, norms_out, up_out, down_out = refs[2 * count : 2 * count + 7]
+    held = refs[2 * count + 7 : -2]
     inward, outward = refs[-2:]
     arrived = [pltpu.make_async_copy(a, b, inward.at[i]) for i, (a, b) in enumerate(zip(sources, held))]
     left = [pltpu.make_async_copy(a, b, outward.at[i]) for i, (a, b) in enumerate(zip(held, targets))]
@@ -1558,8 +1607,17 @@
     output_out[...] = turned[spread : 2 * spread, :ROWS]
     expert_out[...] = small[:, 2 * spread : 2 * spread + total]
     gains_out[...] = turned[2 * spread + total : 2 * spread + total + 2, :ROWS]
-    row = sums[0:1, :]
-    norms_out[...] = jnp.sqrt(row[:, :4] / (row[:, 4:5] * D))
+    row = small[0:1, :]
+    first = 2 * spread + total + 2
+    norms_out[...] = jnp.sqrt(row[:, first : first + 4] / (row[:, first + 4 : first + 5] * D))
+    for e in range(up_out.shape[0]):
+        rows = slice(e * HEAD_DIM, (e + 1) * HEAD_DIM)
+        up_sum, down_sum = [
+            weights_kept[i, rows, :].astype(jnp.float32) + weights_in[i, rows, :].astype(jnp.float32)
+            for i in range(2)
+        ]
+        up_out[e] = up_sum.T
+        down_out[e] = down_sum
     for one, other in zip(arrived, left):
         one.wait()
         other.start()
@@ -1567,7 +1625,8 @@
         made.wait()
 
 
-def deliver(total, sums, small, *arrays):
+def deliver(total, small, weights_kept, weights_in, *arrays):
+    experts = weights_in.shape[1] // HEAD_DIM
     full = jnp.float32
     vmem = pl.BlockSpec(memory_space=pltpu.VMEM)
     anywhere = pl.BlockSpec(memory_space=pl.ANY)
@@ -1581,14 +1640,16 @@
             jax.ShapeDtypeStruct((ROWS, total), full),
             jax.ShapeDtypeStruct((2, ROWS), full),
             jax.ShapeDtypeStruct((1, 4), full),
+            jax.ShapeDtypeStruct((experts, D // 4, HEAD_DIM), full),
+            jax.ShapeDtypeStruct((experts, HEAD_DIM, D // 4), full),
         ],
-        in_specs=[vmem] * 2 + [anywhere] * len(arrays),
-        out_specs=[anywhere] * len(arrays) + [vmem] * 5,
+        in_specs=[vmem] * 3 + [anywhere] * len(arrays),
+        out_specs=[anywhere] * len(arrays) + [vmem] * 7,
         scratch_shapes=[pltpu.VMEM(a.shape, a.dtype) for a in arrays]
         + [pltpu.SemaphoreType.DMA((len(arrays),))] * 2,
         compiler_params=pltpu.CompilerParams(vmem_limit_bytes=63 * 2**20),
         name="deliver",
-    )(sums, small, *arrays)
+    )(small, weights_kept, weights_in, *arrays)
 
 
 def shards_fast(
@@ -1644,14 +1705,15 @@
         query_weight,
         output_weight,
     )
-    returned, up_grad, down_grad, forward = expert_kernel_visit(sent, cot_line, expert_up, expert_down)
-    block_out, grad_input, grad_query, grad_key, grad_value, grad_output, small, sums = backward(
+    returned, weights, weights_kept, forward = expert_kernel_visit(sent, cot_line, expert_up, expert_down)
+    block_out, grad_input, grad_query, grad_key, grad_value, grad_output, small, weights_in = backward(
         total,
         lengths,
         gates,
         slopes,
         routers,
         gains,
+        weights,
         forward,
         returned,
         middle,
@@ -1669,10 +1731,10 @@
         value_weight,
         output_weight,
     )
-    kept = (block_out, grad_input, grad_query, grad_key, grad_value, grad_output, up_grad, down_grad)
-    delivered = deliver(total, sums, small, *kept)
-    block_out, grad_input, grad_query, grad_key, grad_value, grad_output, up_grad, down_grad = delivered[:8]
-    value_small, output_small, expert_small, gain_grads, norms = delivered[8:]
+    kept = (block_out, grad_input, grad_query, grad_key, grad_value, grad_output)
+    delivered = deliver(total, small, weights_kept, weights_in, *kept)
+    block_out, grad_input, grad_query, grad_key, grad_value, grad_output = delivered[:6]
+    value_small, output_small, expert_small, gain_grads, norms, up_grad, down_grad = delivered[6:]
     return (
         block_out[None],
         grad_input[None],

time: 259 us -> 255 us (0.985)
  Pallas kernels: 252 us -> 248 us
    pallas_call x1, Pallas kernels: 47.4 us -> 44.7 us  [attend(): pl.pallas_call(functools.partial(attend_kernel, total), out_shape=[jax.Sh...]
where the time goes in v5:
time: 255 us
  Pallas kernels  248 us (97%)
  local copies, waits for them, and re-layouts  2.7 us (1%)
    pallas_call x1, Pallas kernels, backward(): pl.pallas_call(functools.partial(backward_kernel, total_experts), out_sha...  105 us
    pallas_call x1, Pallas kernels, expert_kernel_visit(): pl.pallas_call(visit_kernel, out_shape=[jax.ShapeDtypeStruct((tokens, D +...  93 us
    pallas_call x1, Pallas kernels, attend(): pl.pallas_call(functools.partial(attend_kernel, total), out_shape=[jax.Sh...  44.7 us
    pallas_call x1, Pallas kernels, deliver(): pl.pallas_call(functools.partial(deliver_kernel, total), out_shape=[jax.S...  5.27 us

profile of v5, /device:TPU:0, one launch (start us, length us, event | category | flops | bytes accessed | tf_op | source)
XLA Modules:
  0.0 254.6 jit_solution(15241182633811787983)
XLA Ops:
  1.3 0.1 pad.5.clone
  1.4 0.7 stack.9
  2.1 0.7 stack.10
  2.8 0.6 maximum_convert_fusion.gains
  3.4 1.7 maximum_maximum_fusion.routers
  5.1 44.7 %attend.1 = (f32[256,1024]{1,0:T(8,128)}, bf16[256,1152]{1,0:T(8,128)(2,1)}, bf16[256,1024]{1,0:T(8,128)(2,1)}, bf16[256,1024]{1,0:T(8,128)(2,1)}, bf16[256,512]...) custom-call(s32[1]{0:T(128)S(6)} %copy.31.lengths, ...), custom_call_target="tpu_custom_call" | custom-call | tf_op jit(solution)/shard_map/attend/pallas_call | solution.py:737
  49.8 93.0 %expert_visit.1 = (f32[256,1152]{1,0:T(8,128)}, bf16[2,768,256]{2,1,0:T(8,128)(2,1)}, bf16[2,768,256]{2,1,0:T(8,128)(2,1)}, bf16[4,256,1024]{2,1,0:T(8,128)(2,1)}) custom-call(bf16[256,1152]{1,0:T(8,128)(2,1)} %get-tuple-element.53.sent, bf16[4,256,1024]{2,1,0:T(8,128)(2,1)} %get-tuple-element.54.cot_at, bf16[6,1024,128]{2,1,0:T(8,128)(2,1)} %up_at.1, ...), custom_call_target="tpu_custom_call" | custom-call | tf_op jit(solution)/shard_map/expert_visit/pallas_call | solution.py:419
  142.8 105.2 %backward.1 = (bf16[256,1024]{1,0:T(8,128)(2,1)}, f32[256,1024]{1,0:T(8,128)}, f32[32,512]{1,0:T(8,128)}, f32[32,512]{1,0:T(8,128)}, f32[32,2560]{1,0:T(8,128)},...) custom-call(s32[1]{0:T(128)S(6)} %copy.31.lengths, f32[256,128]{1,0:T(8,128)} %get-tuple-element.51.gates, ...), custom_call_target="tpu_custom_call" | custom-call | tf_op jit(solution)/shard_map/backward/pallas_call | solution.py:1239
  248.0 5.3 %deliver.1 = (bf16[256,1024]{1,0:T(8,128)(2,1)}, f32[256,1024]{1,0:T(8,128)}, f32[32,512]{1,0:T(8,128)}, f32[32,512]{1,0:T(8,128)}, f32[32,2560]{1,0:T(8,128)}, ...) custom-call(f32[32,128]{1,0:T(8,128)} %get-tuple-element.66.small, ...), custom_call_target="tpu_custom_call" | custom-call | tf_op jit(solution)/shard_map/deliver/pallas_call | solution.py:1634
  253.3 1.3 slice_bitcast_fusion
  (1 shorter events, 0.0 us)

commit v6 on v5

--- a/solution.py
+++ b/solution.py
@@ -456,12 +456,13 @@
 
 
 def attend_kernel(
-    expert_total, lengths, hidden, cot, value_pick, output_pick, expert_pick, routers, gains,
+    expert_total, lengths, hidden, cot, value_pick, output_pick, expert_pick, value_router, output_router, expert_router,
+    gain_one, gain_two,
     key_weight_at, value_weight_at, query_weight_at, output_weight_at,
     middle_at, sent_at, normed_one_at, normed_two_at, queries_at, key_value_at, probs_at, value_all_at, attended_at,
-    gates_at, slopes_at, cot_line_at,
+    gates_at, slopes_at, cot_line_at, routers_at, gains_at,
     middle, sent, normed_one, normed_two, queries, key_value, probs, value_all, attended,
-    gates, slopes, cot_line,
+    gates, slopes, cot_line, routers, gains, routers_full,
     key_weight, value_weight, query_weight, output_weight, mixed, hot_turned, hot,
     fetch, leave, pair_send, pair_recv, cot_send, cot_recv, own_sem,
 ):
@@ -492,6 +493,7 @@
         (middle, middle_at), (sent, sent_at), (normed_one, normed_one_at), (normed_two, normed_two_at),
         (queries, queries_at), (key_value, key_value_at), (probs, probs_at), (value_all, value_all_at),
         (attended, attended_at), (gates, gates_at), (slopes, slopes_at), (cot_line, cot_line_at),
+        (routers, routers_at), (gains, gains_at),
     )
     leaving = [pltpu.make_async_copy(source, target, leave.at[i]) for i, (source, target) in enumerate(results)]
 
@@ -569,6 +571,8 @@
             def _():
                 pair_copy(step, part, dp).start()
 
+    gains[0:1, :] = gain_one[...].astype(jnp.float32).reshape(1, D)
+    gains[1:2, :] = gain_two[...].astype(jnp.float32).reshape(1, D)
     normed_one[...] = norm(hidden[...].astype(jnp.float32), gains[0:1, :])
     leaving[2].start()
     weights[0].wait()
@@ -577,6 +581,13 @@
     ).astype(low)
     send_part(0)
 
+    routers_full[...] = jnp.zeros(routers_full.shape, jnp.float32)
+    routers_full[0:spread, :] = value_router[...].astype(jnp.float32)
+    routers_full[spread : 2 * spread, :] = output_router[...].astype(jnp.float32)
+    routers_full[2 * spread : 2 * spread + total, :] = expert_router[...].astype(jnp.float32)
+    routers[...] = routers_full[...].astype(low)
+    leaving[12].start()
+    leaving[13].start()
     hot_turned[...] = jnp.zeros(hot_turned.shape, jnp.float32)
 
     def mark(picks, base, size):
@@ -650,9 +661,9 @@
     lax.fori_loop(0, HEADS, score, 0)
     leaving[6].start()
     leaving[9].start()
+    pass_on(2)
     wait_part(1)
     leaving[5].start()
-    pass_on(2)
 
     def collect(h, carry):
         span = pl.ds(pl.multiple_of(h * HEAD_DIM, HEAD_DIM), HEAD_DIM)
@@ -733,6 +744,8 @@
         ((count, 128), full),
         ((count, 128), full),
         ((4, count, D), low),
+        ((128, D), low),
+        ((2, D), full),
     ]
     return pl.pallas_call(
         functools.partial(attend_kernel, total),
@@ -740,6 +753,7 @@
         in_specs=[pl.BlockSpec(memory_space=pltpu.SMEM)] + [vmem] * (len(operands) - 4) + [anywhere] * 4,
         out_specs=[anywhere] * len(shapes),
         scratch_shapes=[pltpu.VMEM(*shape) for shape in shapes]
+        + [pltpu.VMEM((128, D), full)]
         + [pltpu.VMEM(a.shape, a.dtype) for a in operands[-4:]]
         + [
             pltpu.VMEM((count, wide), low),
@@ -1672,11 +1686,6 @@
     cotangent,
 ):
     total = expert_router.shape[1]
-    spread = HEADS * VE
-    routers = jnp.concatenate(
-        [value_router.T, output_router.T, expert_router.T, jnp.zeros((128 - 2 * spread - total, D), jnp.bfloat16)]
-    )
-    gains = jnp.stack([attention_gain, feedforward_gain]).astype(jnp.float32)
     (
         middle,
         sent,
@@ -1690,6 +1699,8 @@
         gates,
         slopes,
         cot_line,
+        routers,
+        gains,
     ) = attend(
         total,
         lengths,
@@ -1698,8 +1709,11 @@
         value_pick[0].transpose(1, 2, 0),
         output_pick[0].transpose(1, 2, 0),
         expert_pick[0].T,
-        routers,
-        gains,
+        value_router.T,
+        output_router.T,
+        expert_router.T,
+        attention_gain,
+        feedforward_gain,
         key_weight,
         value_weight,
         query_weight,

time: 255 us -> 248 us (0.973)
  Pallas kernels: 248 us -> 245 us
    pallas_call x1, Pallas kernels: 105 us -> 101 us  [backward(): pl.pallas_call(functools.partial(backward_kernel, total_experts), out_sha...]
where the time goes in v6:
time: 248 us; the launch traced here: 247 us
  Pallas kernels  245 us (99%)
    pallas_call x1, Pallas kernels, backward(): pl.pallas_call(functools.partial(backward_kernel, total_experts), out_sha...  101 us
    pallas_call x1, Pallas kernels, expert_kernel_visit(): pl.pallas_call(visit_kernel, out_shape=[jax.ShapeDtypeStruct((tokens, D +...  93.4 us
    pallas_call x1, Pallas kernels, attend(): pl.pallas_call(functools.partial(attend_kernel, total), out_shape=[jax.Sh...  44.7 us
    pallas_call x1, Pallas kernels, deliver(): pl.pallas_call(functools.partial(deliver_kernel, total), out_shape=[jax.S...  5.27 us

profile of v6, /device:TPU:0, one launch (start us, length us, event | category | flops | bytes accessed | tf_op | source)
XLA Modules:
  0.0 247.3 jit_solution(9488082535576546333)
XLA Ops:
  1.3 44.7 %attend.1 = (f32[256,1024]{1,0:T(8,128)}, bf16[256,1152]{1,0:T(8,128)(2,1)}, bf16[256,1024]{1,0:T(8,128)(2,1)}, bf16[256,1024]{1,0:T(8,128)(2,1)}, bf16[256,512]...) custom-call(s32[1]{0:T(128)S(6)} %copy.31.lengths, ...), custom_call_target="tpu_custom_call" | custom-call | tf_op jit(solution)/shard_map/attend/pallas_call | solution.py:750
  46.0 93.4 %expert_visit.1 = (f32[256,1152]{1,0:T(8,128)}, bf16[2,768,256]{2,1,0:T(8,128)(2,1)}, bf16[2,768,256]{2,1,0:T(8,128)(2,1)}, bf16[4,256,1024]{2,1,0:T(8,128)(2,1)}) custom-call(bf16[256,1152]{1,0:T(8,128)(2,1)} %get-tuple-element.57.sent, bf16[4,256,1024]{2,1,0:T(8,128)(2,1)} %get-tuple-element.58.cot_at, bf16[6,1024,128]{2,1,0:T(8,128)(2,1)} %up_at.1, ...), custom_call_target="tpu_custom_call" | custom-call | tf_op jit(solution)/shard_map/expert_visit/pallas_call | solution.py:419
  139.4 101.3 %backward.1 = (bf16[256,1024]{1,0:T(8,128)(2,1)}, f32[256,1024]{1,0:T(8,128)}, f32[32,512]{1,0:T(8,128)}, f32[32,512]{1,0:T(8,128)}, f32[32,2560]{1,0:T(8,128)},...) custom-call(s32[1]{0:T(128)S(6)} %copy.31.lengths, f32[256,128]{1,0:T(8,128)} %get-tuple-element.53.gates, ...), custom_call_target="tpu_custom_call" | custom-call | tf_op jit(solution)/shard_map/backward/pallas_call | solution.py:1253
  240.7 5.3 %deliver.1 = (bf16[256,1024]{1,0:T(8,128)(2,1)}, f32[256,1024]{1,0:T(8,128)}, f32[32,512]{1,0:T(8,128)}, f32[32,512]{1,0:T(8,128)}, f32[32,2560]{1,0:T(8,128)}, ...) custom-call(f32[32,128]{1,0:T(8,128)} %get-tuple-element.70.small, ...), custom_call_target="tpu_custom_call" | custom-call | tf_op jit(solution)/shard_map/deliver/pallas_call | solution.py:1648
  246.0 1.3 slice_bitcast_fusion

commit v7 on v6

--- a/solution.py
+++ b/solution.py
@@ -59,9 +59,9 @@
 
 
 def visit_kernel(
-    sent, cot_at, up_at, down_at, back_out, weights_out, weights_kept, forward_out,
-    cot, up, down, rows, cot_other, up_wide, chosen, cots, gated, grad_pre, forward, forward_in, gated_turned, pre_turned, partial, paired_in, chain_in, up_low, down_low, up_in, down_in,
-    fetch, row_send, row_recv, half_send, half_recv, cot_send, cot_recv, pair_send, pair_recv, forward_send, forward_recv, chain_send, chain_recv, grad_send, grad_recv,
+    sent, cot_at, up_at, down_at, back_at, weights_out, weights_kept, forward_at,
+    back_out, forward_out, cot, up, down, rows, cot_other, up_wide, chosen, cots, gated, grad_pre, forward, forward_in, gated_turned, pre_turned, partial, paired_in, chain_in, up_low, down_low, up_in, down_in,
+    fetch, back_leave, forward_leave, row_send, row_recv, half_send, half_recv, cot_send, cot_recv, pair_send, pair_recv, forward_send, forward_recv, chain_send, chain_recv, grad_send, grad_recv,
 ):
     experts = up.shape[0]
     wide = down.shape[0]
@@ -334,10 +334,17 @@
             for way, part in ways:
                 relay(*way, part)
 
+    def forward_leaves(at):
+        return pltpu.make_async_copy(forward_out.at[at], forward_at.at[at], forward_leave.at[at])
+
+    def back_leaves(part):
+        return pltpu.make_async_copy(back_out.at[spans[part]], back_at.at[spans[part]], back_leave.at[part])
+
     def forward_add(p):
         at = order(p)
         forward_copy(at).wait()
         add(forward_out.at[at], forward_in.at[at])
+        forward_leaves(at).start()
 
     relays((next_one, 2), (next_one, 3))
     up_quarter(0)
@@ -370,6 +377,8 @@
             chain_copy(z, 4, z, 0, part).wait_recv()
             back_out[span, :] = back_out[span, :] + chain_in[4, span, :].astype(jnp.float32)
 
+        back_leaves(part).start()
+
     ends = (
         (up_copy(0), up_low, 2, up_in, 0, weights_out.at[0]),
         (up_copy(1), up_low, 3, up_in, 1, weights_kept.at[0]),
@@ -407,6 +416,11 @@
 
         chain_copy(z, 0, z, 1, part).wait_send()
         chain_copy(z, 0, z, 3, part).wait_send()
+
+    for at in range(4):
+        forward_leaves(at).wait()
+        back_leaves(at).wait()
+
 
 def expert_kernel_visit(sent, cot_line, up, down):
     tokens = sent.shape[0]
@@ -425,8 +439,10 @@
             jax.ShapeDtypeStruct((4, tokens, D), low),
         ],
         in_specs=[vmem] + [pl.BlockSpec(memory_space=pl.ANY)] * 3,
-        out_specs=[vmem] * 4,
+        out_specs=[pl.BlockSpec(memory_space=pl.ANY), vmem, vmem, pl.BlockSpec(memory_space=pl.ANY)],
         scratch_shapes=[
+            pltpu.VMEM((tokens, D + 128), f32),
+            pltpu.VMEM((4, tokens, D), low),
             pltpu.VMEM((4, tokens, D), low),
             pltpu.VMEM((experts, D, hidden), low),
             pltpu.VMEM((wide, D), low),
@@ -448,7 +464,7 @@
             pltpu.VMEM((4, wide, D // 4), low),
             pltpu.VMEM((3, wide, D // 4), low),
             pltpu.VMEM((3, wide, D // 4), low),
-            dma((3,)), dma((4,)), dma((4,)), dma((2, 4, 2)), dma((4, 2)), dma((4,)), dma((4,)), dma((4,)), dma((4,)), dma((4,)), dma((4,)), dma((4, 4)), dma((5, 4)), dma((2, 3)), dma((2, 3)),
+            dma((3,)), dma((4,)), dma((4,)), dma((4,)), dma((4,)), dma((2, 4, 2)), dma((4, 2)), dma((4,)), dma((4,)), dma((4,)), dma((4,)), dma((4,)), dma((4,)), dma((4, 4)), dma((5, 4)), dma((2, 3)), dma((2, 3)),
         ],
         compiler_params=pltpu.CompilerParams(collective_id=2, has_side_effects=True, vmem_limit_bytes=58 * 2**20),
         name="expert_visit",
@@ -778,13 +794,13 @@
     total_experts, lengths, gates, slopes, routers, gains,
     weights_at, forward_at, returned_at, middle_at, cot_at, hidden_at, normed_one_at, queries_at, key_value_at, probs_at, value_all_at,
     attended_at, normed_two_at, query_weight_at, key_weight_at, value_weight_at, output_weight_at,
-    block_out, grad_in, out_query, out_key, out_value, out_output, out_small, weights_in,
-    weights, forward, returned, middle, cot, hidden, normed_one, queries, key_value, probs, value_all,
+    block_at, grad_at, out_query, out_key, out_value, out_output, out_small, weights_in,
+    block_out, grad_in, weights, forward, returned, middle, cot, hidden, normed_one, queries, key_value, probs, value_all,
     attended, normed_two, query_weight, key_weight, value_part, output_part,
     branch, branch_turned, one_turned, hidden_turned, grad_att, grad_query, leave, arrive, grad_key,
     grad_each, grad_middle, logit_one, logit_two, small_turned, mixed,
     grads, grads_small, core_in, plane_in, last_in, forward_in,
-    fetch, part_fetch, leave_send, leave_recv, send, recv, forward_send, forward_recv, weights_send, weights_recv,
+    fetch, out_leave, part_fetch, leave_send, leave_recv, send, recv, forward_send, forward_recv, weights_send, weights_recv,
 ):
     dp, ex = lax.axis_index("dp"), lax.axis_index("expert")
     y, x, z, core = dp // 2, dp % 2, ex // 2, ex % 2
@@ -1199,6 +1215,9 @@
     small_turned[small_rows : small_rows + 1, :] = gain_one_sum
     small_turned[small_rows + 1 : small_rows + 2, :] = gain_two_sum
     sums = output_rows()
+    block_leaves = pltpu.make_async_copy(block_out, block_at, out_leave.at[0])
+    block_leaves.start()
+    grad_leaves = pltpu.make_async_copy(grad_in, grad_at, out_leave.at[1])
     for i in range(5):
         small_turned[small_rows + 2 + i : small_rows + 3 + i, :] = jnp.broadcast_to(sums[:, i : i + 1], (1, D))
     grads_small[...] = small_turned[...].T.astype(low).reshape(grads_small.shape)
@@ -1210,6 +1229,8 @@
         grad_in[...] += dot_last(grad_each[:, n * PIECE : (n + 1) * PIECE], value_part[n % 2])
         if n + 2 < HEADS:
             value_copy(n + 2).start()
+        if n == HEADS - 1:
+            grad_leaves.start()
 
     for action, i in (
         (halve_near, 10), (spread, 3),
@@ -1239,6 +1260,9 @@
         @pl.when(inner == 1)
         def _():
             forward_copy(z, 0, z, 2, part).wait_send()
+
+    block_leaves.wait()
+    grad_leaves.wait()
 
 
 def backward(total_experts, lengths, gates, slopes, routers, gains, *arrays):
@@ -1263,8 +1287,9 @@
             jax.ShapeDtypeStruct(arrays[0].shape, low),
         ],
         in_specs=[pl.BlockSpec(memory_space=pltpu.SMEM)] + [vmem] * 4 + [anywhere] * len(arrays),
-        out_specs=[vmem] * 8,
-        scratch_shapes=whole
+        out_specs=[anywhere] * 2 + [vmem] * 6,
+        scratch_shapes=[pltpu.VMEM((count, D), low), pltpu.VMEM((count, D), full)]
+        + whole
         + [
             pltpu.VMEM((2, D, PIECE), low),
             pltpu.VMEM((2, PIECE, D), low),
@@ -1290,6 +1315,7 @@
             pltpu.VMEM((n, 3, ROWS, PIECE), low),
             pltpu.VMEM((5, count, D), low),
             dma((15,)),
+            dma((2,)),
             dma((2, 2)),
             dma((3, HEADS)),
             dma((3, HEADS)),
@@ -1605,15 +1631,25 @@
     )
 
 
-def deliver_kernel(total, small, weights_kept, weights_in, *refs):
+def deliver_kernel(total, small, weights_kept_at, weights_in_at, *refs):
+    weights_kept, weights_in, up_out, down_out, weights_sem = refs[-5:]
+    refs = refs[:-5]
     count = (len(refs) - 9) // 3
     sources, targets = refs[:count], refs[count : 2 * count]
-    value_out, output_out, expert_out, gains_out, norms_out, up_out, down_out = refs[2 * count : 2 * count + 7]
+    value_out, output_out, expert_out, gains_out, norms_out, up_at, down_at = refs[2 * count : 2 * count + 7]
     held = refs[2 * count + 7 : -2]
     inward, outward = refs[-2:]
     arrived = [pltpu.make_async_copy(a, b, inward.at[i]) for i, (a, b) in enumerate(zip(sources, held))]
     left = [pltpu.make_async_copy(a, b, outward.at[i]) for i, (a, b) in enumerate(zip(held, targets))]
-    for made in arrived:
+    weights = [
+        pltpu.make_async_copy(weights_kept_at, weights_kept, weights_sem.at[0]),
+        pltpu.make_async_copy(weights_in_at, weights_in, weights_sem.at[1]),
+    ]
+    summed = [
+        pltpu.make_async_copy(up_out, up_at, weights_sem.at[2]),
+        pltpu.make_async_copy(down_out, down_at, weights_sem.at[3]),
+    ]
+    for made in arrived + weights:
         made.start()
     spread = HEADS * VE
     turned = jnp.concatenate([small[...], jnp.zeros((128 - ROWS, 128), jnp.float32)]).T
@@ -1624,6 +1660,11 @@
     row = small[0:1, :]
     first = 2 * spread + total + 2
     norms_out[...] = jnp.sqrt(row[:, first : first + 4] / (row[:, first + 4 : first + 5] * D))
+    for one, other in zip(arrived, left):
+        one.wait()
+        other.start()
+    for made in weights:
+        made.wait()
     for e in range(up_out.shape[0]):
         rows = slice(e * HEAD_DIM, (e + 1) * HEAD_DIM)
         up_sum, down_sum = [
@@ -1632,10 +1673,9 @@
         ]
         up_out[e] = up_sum.T
         down_out[e] = down_sum
-    for one, other in zip(arrived, left):
-        one.wait()
-        other.start()
-    for made in left:
+    for made in summed:
+        made.start()
+    for made in left + summed:
         made.wait()
 
 
@@ -1657,10 +1697,17 @@
             jax.ShapeDtypeStruct((experts, D // 4, HEAD_DIM), full),
             jax.ShapeDtypeStruct((experts, HEAD_DIM, D // 4), full),
         ],
-        in_specs=[vmem] * 3 + [anywhere] * len(arrays),
-        out_specs=[anywhere] * len(arrays) + [vmem] * 7,
+        in_specs=[vmem] + [anywhere] * (2 + len(arrays)),
+        out_specs=[anywhere] * len(arrays) + [vmem] * 5 + [anywhere] * 2,
         scratch_shapes=[pltpu.VMEM(a.shape, a.dtype) for a in arrays]
-        + [pltpu.SemaphoreType.DMA((len(arrays),))] * 2,
+        + [pltpu.SemaphoreType.DMA((len(arrays),))] * 2
+        + [
+            pltpu.VMEM(weights_kept.shape, weights_kept.dtype),
+            pltpu.VMEM(weights_in.shape, weights_in.dtype),
+            pltpu.VMEM((experts, D // 4, HEAD_DIM), full),
+            pltpu.VMEM((experts, HEAD_DIM, D // 4), full),
+            pltpu.SemaphoreType.DMA((4,)),
+        ],
         compiler_params=pltpu.CompilerParams(vmem_limit_bytes=63 * 2**20),
         name="deliver",
     )(small, weights_kept, weights_in, *arrays)

time: 248 us -> 246 us (level)
  no operation moved by 1% of the time
where the time goes in v7:
time: 246 us
  Pallas kernels  243 us (99%)
    pallas_call x1, Pallas kernels, backward(): pl.pallas_call(functools.partial(backward_kernel, total_experts), out_sha...  101 us
    pallas_call x1, Pallas kernels, expert_kernel_visit(): pl.pallas_call(visit_kernel, out_shape=[jax.ShapeDtypeStruct((tokens, D +...  92.4 us
    pallas_call x1, Pallas kernels, attend(): pl.pallas_call(functools.partial(attend_kernel, total), out_shape=[jax.Sh...  44.7 us
    pallas_call x1, Pallas kernels, deliver(): pl.pallas_call(functools.partial(deliver_kernel, total), out_shape=[jax.S...  5.19 us

profile of v7, /device:TPU:0, one launch (start us, length us, event | category | flops | bytes accessed | tf_op | source)
XLA Modules:
  0.0 245.8 jit_solution(5126931955316218589)
XLA Ops:
  1.3 44.7 %attend.1 = (f32[256,1024]{1,0:T(8,128)}, bf16[256,1152]{1,0:T(8,128)(2,1)}, bf16[256,1024]{1,0:T(8,128)(2,1)}, bf16[256,1024]{1,0:T(8,128)(2,1)}, bf16[256,512]...) custom-call(s32[1]{0:T(128)S(6)} %copy.31.lengths, ...), custom_call_target="tpu_custom_call" | custom-call | tf_op jit(solution)/shard_map/attend/pallas_call | solution.py:766
  46.0 92.4 %expert_visit.1 = (f32[256,1152]{1,0:T(8,128)}, bf16[2,768,256]{2,1,0:T(8,128)(2,1)}, bf16[2,768,256]{2,1,0:T(8,128)(2,1)}, bf16[4,256,1024]{2,1,0:T(8,128)(2,1)}) custom-call(bf16[256,1152]{1,0:T(8,128)(2,1)} %get-tuple-element.57.sent, bf16[4,256,1024]{2,1,0:T(8,128)(2,1)} %get-tuple-element.58.cot_at, bf16[6,1024,128]{2,1,0:T(8,128)(2,1)} %up_at.1, ...), custom_call_target="tpu_custom_call" | custom-call | tf_op jit(solution)/shard_map/expert_visit/pallas_call | solution.py:433
  138.5 100.8 %backward.1 = (bf16[256,1024]{1,0:T(8,128)(2,1)}, f32[256,1024]{1,0:T(8,128)}, f32[32,512]{1,0:T(8,128)}, f32[32,512]{1,0:T(8,128)}, f32[32,2560]{1,0:T(8,128)},...) custom-call(s32[1]{0:T(128)S(6)} %copy.31.lengths, f32[256,128]{1,0:T(8,128)} %get-tuple-element.53.gates, ...), custom_call_target="tpu_custom_call" | custom-call | tf_op jit(solution)/shard_map/backward/pallas_call | solution.py:1277
  239.3 5.2 %deliver.1 = (bf16[256,1024]{1,0:T(8,128)(2,1)}, f32[256,1024]{1,0:T(8,128)}, f32[32,512]{1,0:T(8,128)}, f32[32,512]{1,0:T(8,128)}, f32[32,2560]{1,0:T(8,128)}, ...) custom-call(f32[32,128]{1,0:T(8,128)} %get-tuple-element.70.small, ...), custom_call_target="tpu_custom_call" | custom-call | tf_op jit(solution)/shard_map/deliver/pallas_call | solution.py:1688
  244.5 1.3 slice_bitcast_fusion

commit v8 on v7

--- a/solution.py
+++ b/solution.py
@@ -530,38 +530,41 @@
 
     pl.semaphore_wait(barrier, 4 + inner)
 
-    def cot_copy(way, at, source=None):
-        block = cot_line.at[at]
+    def cot_copy(way, at, part, source=None):
+        span = pl.ds(part * (count // 2), count // 2)
+        block = cot_line.at[at, span]
         return pltpu.make_async_remote_copy(
-            src_ref=block if source is None else source, dst_ref=block,
-            send_sem=cot_send.at[way, at], recv_sem=cot_recv.at[at],
+            src_ref=block if source is None else source.at[span], dst_ref=block,
+            send_sem=cot_send.at[way, at, part], recv_sem=cot_recv.at[at, part],
             device_id=at_z(z + 1 - 2 * way), device_id_type=MESH,
         )
 
-    def pass_on(distance):
+    def pass_on(distance, part):
         @pl.when(z >= distance)
         def _():
-            cot_copy(0, z - distance).wait_recv()
+            cot_copy(0, z - distance, part).wait_recv()
 
         @pl.when((z >= distance) & (z < 3))
         def _():
-            cot_copy(0, z - distance).start()
+            cot_copy(0, z - distance, part).start()
 
         @pl.when(z + distance <= 3)
         def _():
-            cot_copy(1, z + distance).wait_recv()
+            cot_copy(1, z + distance, part).wait_recv()
 
         @pl.when((z + distance <= 3) & (z > 0))
         def _():
-            cot_copy(1, z + distance).start()
-
-    @pl.when(z < 3)
-    def _():
-        cot_copy(0, z, cot).start()
-
-    @pl.when(z > 0)
-    def _():
-        cot_copy(1, z, cot).start()
+            cot_copy(1, z + distance, part).start()
+
+    for part in range(2):
+
+        @pl.when(z < 3)
+        def _():
+            cot_copy(0, z, part, cot).start()
+
+        @pl.when(z > 0)
+        def _():
+            cot_copy(1, z, part, cot).start()
 
     keep = pltpu.make_async_copy(cot, cot_line.at[z], own_sem)
     keep.start()
@@ -641,6 +644,7 @@
             row += gates[:, e : e + 1] * value_all[:, e * HEAD_DIM : (e + 1) * HEAD_DIM].astype(jnp.float32)
         key_value[dp, :, width + h * HEAD_DIM : width + (h + 1) * HEAD_DIM] = row.astype(low)
     send_part(1)
+    pass_on(1, 0)
 
     weights[2].wait()
     queries[...] = jnp.dot(normed_one[...], query_weight[...], preferred_element_type=jnp.float32).astype(low)
@@ -651,7 +655,7 @@
         def _():
             key_value[block] = jnp.zeros((count, 2 * width), low)
 
-    pass_on(1)
+    pass_on(1, 1)
 
     def wait_part(part):
         for block in range(3):
@@ -677,7 +681,8 @@
     lax.fori_loop(0, HEADS, score, 0)
     leaving[6].start()
     leaving[9].start()
-    pass_on(2)
+    pass_on(2, 0)
+    pass_on(2, 1)
     wait_part(1)
     leaving[5].start()
 
@@ -716,7 +721,8 @@
 
     for i in (1, 3, 10):
         leaving[i].start()
-    pass_on(3)
+    pass_on(3, 0)
+    pass_on(3, 1)
     keep.wait()
     leaving[11].start()
     for part in range(2):
@@ -727,14 +733,15 @@
                 pair_copy(step, part, dp).wait_send()
 
     for at in range(4):
-
-        @pl.when((at <= z) & (z < 3))
-        def _():
-            cot_copy(0, at).wait_send()
-
-        @pl.when((at >= z) & (z > 0))
-        def _():
-            cot_copy(1, at).wait_send()
+        for part in range(2):
+
+            @pl.when((at <= z) & (z < 3))
+            def _():
+                cot_copy(0, at, part).wait_send()
+
+            @pl.when((at >= z) & (z > 0))
+            def _():
+                cot_copy(1, at, part).wait_send()
 
     for made in leaving:
         made.wait()
@@ -779,8 +786,8 @@
             dma((len(shapes),)),
             dma((4, 2)),
             dma((4, 2)),
-            dma((2, 4)),
-            dma((4,)),
+            dma((2, 4, 2)),
+            dma((4, 2)),
             dma,
         ],
         compiler_params=pltpu.CompilerParams(

time: 246 us -> 247 us (level)
  no operation moved by 1% of the time
where the time goes in v8:
time: 247 us; the launch traced here: 246 us
  Pallas kernels  244 us (99%)
    pallas_call x1, Pallas kernels, backward(): pl.pallas_call(functools.partial(backward_kernel, total_experts), out_sha...  102 us
    pallas_call x1, Pallas kernels, expert_kernel_visit(): pl.pallas_call(visit_kernel, out_shape=[jax.ShapeDtypeStruct((tokens, D +...  94.3 us
    pallas_call x1, Pallas kernels, attend(): pl.pallas_call(functools.partial(attend_kernel, total), out_shape=[jax.Sh...  42.7 us
    pallas_call x1, Pallas kernels, deliver(): pl.pallas_call(functools.partial(deliver_kernel, total), out_shape=[jax.S...  5.19 us

profile of v8, /device:TPU:0, one launch (start us, length us, event | category | flops | bytes accessed | tf_op | source)
XLA Modules:
  0.0 246.4 jit_solution(15682946495710551887)
XLA Ops:
  1.3 42.7 %attend.1 = (f32[256,1024]{1,0:T(8,128)}, bf16[256,1152]{1,0:T(8,128)(2,1)}, bf16[256,1024]{1,0:T(8,128)(2,1)}, bf16[256,1024]{1,0:T(8,128)(2,1)}, bf16[256,512]...) custom-call(s32[1]{0:T(128)S(6)} %copy.31.lengths, ...), custom_call_target="tpu_custom_call" | custom-call | tf_op jit(solution)/shard_map/attend/pallas_call | solution.py:773
  44.0 94.3 %expert_visit.1 = (f32[256,1152]{1,0:T(8,128)}, bf16[2,768,256]{2,1,0:T(8,128)(2,1)}, bf16[2,768,256]{2,1,0:T(8,128)(2,1)}, bf16[4,256,1024]{2,1,0:T(8,128)(2,1)}) custom-call(bf16[256,1152]{1,0:T(8,128)(2,1)} %get-tuple-element.57.sent, bf16[4,256,1024]{2,1,0:T(8,128)(2,1)} %get-tuple-element.58.cot_at, bf16[6,1024,128]{2,1,0:T(8,128)(2,1)} %up_at.1, ...), custom_call_target="tpu_custom_call" | custom-call | tf_op jit(solution)/shard_map/expert_visit/pallas_call | solution.py:433
  138.3 101.7 %backward.1 = (bf16[256,1024]{1,0:T(8,128)(2,1)}, f32[256,1024]{1,0:T(8,128)}, f32[32,512]{1,0:T(8,128)}, f32[32,512]{1,0:T(8,128)}, f32[32,2560]{1,0:T(8,128)},...) custom-call(s32[1]{0:T(128)S(6)} %copy.31.lengths, f32[256,128]{1,0:T(8,128)} %get-tuple-element.53.gates, ...), custom_call_target="tpu_custom_call" | custom-call | tf_op jit(solution)/shard_map/backward/pallas_call | solution.py:1284
  240.0 5.2 %deliver.1 = (bf16[256,1024]{1,0:T(8,128)(2,1)}, f32[256,1024]{1,0:T(8,128)}, f32[32,512]{1,0:T(8,128)}, f32[32,512]{1,0:T(8,128)}, f32[32,2560]{1,0:T(8,128)}, ...) custom-call(f32[32,128]{1,0:T(8,128)} %get-tuple-element.70.small, ...), custom_call_target="tpu_custom_call" | custom-call | tf_op jit(solution)/shard_map/deliver/pallas_call | solution.py:1695
  245.2 1.3 slice_bitcast_fusion
